TPU v7x, 32 devices: a whole 2x2x4 slice. The times are simulated.
32 devices in a mesh: gx: 4 (over y, x), gy: 4 (over z), gz: 2 (over core).
Axes of the slice: x: 2, y: 2, z: 4, core: 2. Of those that a mesh axis runs over, the one named last changes fastest.
Arguments:
- positions: float32 [3, 1024], P(None, ('gx', 'gy', 'gz')), may hold values from 0 to 35.2, as said below
- species: int32 [1024], P(('gx', 'gy', 'gz')), may hold values from 0 to 63
- neighbours: int32 [32, 1024], P(None, ('gx', 'gy', 'gz')), may hold values from 0 to 863, as said below
- embed_center: float32 [64, 1024], replicated, may hold values from -3.5 to 3.5
- embed_neigh: float32 [64, 1024], replicated, may hold values from -3.5 to 3.5
- embed_radial: float32 [8, 1024], replicated, may hold values from -3.5 to 3.5
- value_proj: float32 [1024, 64], replicated, may hold values from -0.1875 to 0.1875
- env_weight: float32 [2, 1024, 64], replicated, may hold values from -0.1875 to 0.1875
- latent_weight: float32 [2, 1216, 1024], replicated, may hold values from -0.15625 to 0.15625
- path_weight: float32 [9, 64], replicated, may hold values from -4 to 4
- out_weight: float32 [1024], replicated, may hold values from -0.1875 to 0.1875
- scale_table: float32 [64], replicated, may hold values from 0.2 to 1
- shift_table: float32 [64], replicated, may hold values from -4 to 4
- cotangent: float32 [1024], P(('gx', 'gy', 'gz')), may hold values from -6 to 6
Outputs:
- atom_energy: float32 [1024], P(('gx', 'gy', 'gz'))
- position_grad: float32 [3, 1024], P(None, ('gx', 'gy', 'gz'))
- grad_embed_center: float32 [64, 1024], replicated
- grad_embed_neigh: float32 [64, 1024], replicated
- grad_embed_radial: float32 [8, 1024], replicated
- grad_value_proj: float32 [1024, 64], replicated
- grad_env_weight: float32 [2, 1024, 64], replicated
- grad_latent_weight: float32 [2, 1216, 1024], replicated
- grad_path_weight: float32 [9, 64], replicated
- grad_out_weight: float32 [1024], replicated
- grad_scale_table: float32 [64], replicated
- grad_shift_table: float32 [64], replicated
Inputs may be any that keep to these rules, and one draw needn't show every extreme that they name: Column i = d * 32 + a lists atom i's neighbours as slots (bx * 9 + by * 3 + bz) * 32 + a' of a table of the atoms of the 27 devices at grid offsets (bx - 1, by - 1, bz - 1) around d; the real neighbours come first, lie on devices that exist, are distinct and are closer than 5 to atom i; the other slots hold 416 + a; at most 32 real neighbours per atom. `positions`: atoms of device d lie in its own box of the grid of devices, at distances 1.5 or more from each other.
All inputs are finite; a program needn't handle non-finite values.
Results may differ from a plain program's by a relative error of at most 0.0003.
Values sent between devices are 32-bit elements; how exact they have to be, the bound alone decides.
No kernel may reach another device: no remote copies, remote signals or barrier semaphores. Data moves between devices by JAX's collectives and lax.ppermute only.
A program may use at most 256 MiB of HBM per device.

v0:
```python
import functools
import math

import jax
import jax.numpy as jnp
import numpy as np
from jax import lax
from jax.experimental import pallas as pl
from jax.experimental.pallas import tpu as pltpu
from jax.sharding import PartitionSpec as P

LATENT = 1024
CHANNELS = 64
NSPEC = 64
NBESSEL = 8
NB = 32
ATOMS = 32
EDGES = NB * ATOMS
WIDE = LATENT + 3 * CHANNELS
HALF = LATENT // 2
QUARTER = LATENT // 4
NTAB = 9 * 128
OWN = 4 * 128 + ATOMS

CUTOFF = 5.0
RH = 0.7071067811865476
HR = 0.7071067811865476
SR = 0.4082482904638631
R3 = math.sqrt(3.0)
Q75 = math.sqrt(7.5)
NORM = NB**-0.5
BESSEL = math.sqrt(2.0 / CUTOFF)

F32 = jnp.float32
BF16 = jnp.bfloat16

G_SMOOTH, G_LIVE, G_R, G_DISP, G_GRAD, G_RAD, G_GS, G_SPEC = 9, 10, 11, 12, 15, 16, 24, 25
G_ROWS = 32


def dot(a, b, ca, cb):
    return lax.dot_general(a, b, (((ca,), (cb,)), ((), ())), preferred_element_type=F32)


def dot3(ah, al, bh, bl, ca, cb):
    return dot(ah, bh, ca, cb) + dot(ah, bl, ca, cb) + dot(al, bh, ca, cb)


def split(x):
    hi = x.astype(BF16)
    return hi, (x - hi.astype(F32)).astype(BF16)


def pieces(x):
    hi = x.astype(BF16).astype(F32)
    rest = x - hi
    mid = rest.astype(BF16).astype(F32)
    return hi, mid, rest - mid


def sigmoid(x):
    return 0.5 * jnp.tanh(0.5 * x) + 0.5


def silu_both(x):
    sig = sigmoid(x)
    return x * sig, sig * (1.0 + x * (1.0 - sig))


def lanes(i, width):
    return pl.ds(pl.multiple_of(i * width, width), width)


def over(count, body):
    def step(i, carry):
        body(i)
        return carry

    lax.fori_loop(0, count, step, 0)


def staggered(count, bufs, first, second):
    first(0, bufs[0])
    for i in range(count):
        if i + 1 < count:
            first(i + 1, bufs[(i + 1) % 2])
        second(i, bufs[i % 2])


def iota(shape, dim):
    return lax.broadcasted_iota(jnp.int32, shape, dim)


def slot_total(x):
    x = x + pltpu.roll(x, 64, 1)
    return x + pltpu.roll(x, 32, 1)


def make_env(geo, w, env):
    for c in range(9):
        acc = None
        for k in range(8):
            cols = pl.ds(k * 128, 128)
            term = w[:, cols] if c == 0 else geo[c : c + 1, cols] * w[:, cols]
            acc = term if acc is None else acc + term
        env[c * 64 : (c + 1) * 64, :] = slot_total(acc) * NORM


def rows_of(ref, c, cols=slice(None)):
    return ref[c * 64 : (c + 1) * 64, cols]


def pack_kernel(pos, spec, out):
    out[...] = jnp.zeros_like(out)
    out[0:3, 0:ATOMS] = pos[...]
    out[3:4, 0:ATOMS] = spec[...].astype(F32)


def join_z_kernel(place, own, even_in, odd_in, out):
    is_odd = place[0] == 1
    left = jnp.where(is_odd, even_in[...], odd_in[...])
    right = jnp.where(is_odd, odd_in[...], even_in[...])
    out[...] = left + pltpu.roll(own[...], ATOMS, 1) + pltpu.roll(right, 2 * ATOMS, 1)


def join_y_kernel(place, own, even_in, odd_in, out):
    is_odd = place[1] == 1
    out[:, 0:128] = jnp.where(is_odd, even_in[...], odd_in[...])
    out[:, 128:256] = own[...]
    out[:, 256:384] = jnp.where(is_odd, odd_in[...], even_in[...])


def prep_kernel(
    w, ec_in, en_in, rad_in, vp_in, env_in, neigh_in, pos_in, spec_in, cot_in, path_in, outw_in,
    scale_in, shift_in,
    w0h, w0l, w1h, w1l, table, veh, vel, evh, evl, path_b, cols, slots, cent, rad_w,
    ec, en, vp, env, neigh, pos, spec, cot, path, outw, scale, shift, square, sem,
):
    pairs = (
        (ec_in, ec), (en_in, en), (rad_in, rad_w), (vp_in, vp), (env_in, env), (neigh_in, neigh),
        (pos_in, pos), (spec_in, spec), (cot_in, cot), (path_in, path), (outw_in, outw),
        (scale_in, scale), (shift_in, shift),
    )
    copies = [
        pltpu.make_async_copy(src, dst, sem.at[n]) for n, (src, dst) in enumerate(pairs)
    ]
    for copy in copies:
        copy.start()

    for layer, (hi, lo) in enumerate(((w0h, w0l), (w1h, w1l))):

        def part(i, layer=layer, hi=hi, lo=lo):
            rows = pl.ds(pl.multiple_of(i * 64, 64), 64)
            hi[rows, :], lo[rows, :] = split(w[layer, rows, :])

        over(WIDE // 64, part)
    for copy in copies:
        copy.wait()

    ech, ecl = split(ec[...])
    enh, enl = split(en[...])
    rh = rad_w[...].astype(BF16).astype(F32)
    rl = rad_w[...] - rh
    table[0:64, :] = ech
    table[64:128, :] = enh
    table[128:192, :] = ecl
    table[192:256, :] = enl
    table[256:288, :] = jnp.concatenate([rh, rl, rh, jnp.zeros_like(rh)], 0).astype(BF16)
    veh[0:64, :], vel[0:64, :] = split(vp[...])
    veh[64:128, :], vel[64:128, :] = split(env[0])
    evh[...], evl[...] = split(env[1])

    square[...] = jnp.zeros_like(square)
    square[0:8, :] = outw[...]
    square[8:9, 0:64] = scale[...]
    square[9:10, 0:64] = shift[...]
    square[16:25, 0:64] = path[...]
    turned = square[...].T
    cols[...] = turned
    for n in range(9):
        path_b[n * 64 : (n + 1) * 64, :] = jnp.broadcast_to(
            turned[0:64, 16 + n : 17 + n], (64, 128)
        )

    square[0:32, :] = jnp.zeros((32, 128), F32)
    square[0:32, 0:ATOMS] = neigh[...].astype(F32)
    row = square[pl.ds(0, 8, 4), :]
    for i in range(1, 4):
        row = row + pltpu.roll(square[pl.ds(i, 8, 4), :], i * ATOMS, 1)
    padded = row
    for m in range(1, 9):
        padded = padded + jnp.where(row >= 96.0 * m, 32.0, 0.0)
    padded = padded.astype(jnp.int32)
    square[0:8, :] = jnp.zeros((8, 128), F32)
    square[0:3, 0:ATOMS] = pos[...]
    square[3:4, 0:ATOMS] = spec[...].astype(F32)
    square[4:5, 0:ATOMS] = cot[...]
    own = square[0:8, :]
    own = own + pltpu.roll(own, 32, 1)
    own = own + pltpu.roll(own, 64, 1)
    for k in range(8):
        slots[:, k * 128 : (k + 1) * 128] = padded[k : k + 1]
        cent[:, k * 128 : (k + 1) * 128] = own


def embed_inputs(cent, geo, cols):
    kinds = iota((NSPEC, 256), 0).astype(F32)
    hot_c = jnp.where(kinds == cent[3:4, cols], 1.0, 0.0)
    hot_n = jnp.where(kinds == geo[25:26, cols], 1.0, 0.0)
    hots = jnp.concatenate([hot_c, hot_n], 0).astype(BF16)
    rad = geo[16:24, cols]
    rad_h = rad.astype(BF16).astype(F32)
    rads = jnp.concatenate([rad_h, rad_h, rad - rad_h, jnp.zeros_like(rad)], 0).astype(BF16)
    return jnp.concatenate([hots, hots, rads], 0)


def fwd_kernel(
    place, tab, even_in, odd_in, slots, cent, w0h, w0l, table, veh, vel, evh, evl, path, columns,
    x0h, x0l, x1h, x1l, z0, vw, w1, geo, g0, g1, f1,
    gat, za, zb,
):
    is_odd = place[2] == 1
    whole = jnp.concatenate(
        [
            jnp.where(is_odd, even_in[...], odd_in[...]),
            tab[...],
            jnp.where(is_odd, odd_in[...], even_in[...]),
        ],
        1,
    )
    hi, mid, lo = pieces(whole)
    tab24 = jnp.concatenate([hi, mid, lo], 0).astype(BF16)

    def gather(i):
        cols = lanes(i, 256)
        hot = jnp.where(iota((NTAB, 256), 0) == slots[:, cols], 1.0, 0.0).astype(BF16)
        got = dot(tab24, hot, 1, 0)
        gat[:, cols] = got[0:8] + got[8:16] + got[16:24]

    over(4, gather)

    live = jnp.where(slots[...] != OWN + iota((1, EDGES), 1) % ATOMS, 1.0, 0.0)
    dead = 1.0 - live
    dx = (gat[0:1, :] - cent[0:1, :]) * live + dead * 2.5
    dy = (gat[1:2, :] - cent[1:2, :]) * live
    dz = (gat[2:3, :] - cent[2:3, :]) * live
    r = jnp.sqrt(dx * dx + dy * dy + dz * dz)
    inv = 1.0 / r
    t = r / CUTOFF
    t2 = t * t
    t6 = t2 * t2 * t2
    smooth = live * (1.0 - 28.0 * t6 + 48.0 * t6 * t - 21.0 * t6 * t * t)
    ux, uy, uz = dx * inv, dy * inv, dz * inv
    geo[0:1, :] = jnp.ones_like(r)
    geo[1:2, :] = R3 * ux
    geo[2:3, :] = R3 * uy
    geo[3:4, :] = R3 * uz
    geo[4:5, :] = Q75 * HR * (ux * ux - uy * uy)
    geo[5:6, :] = Q75 * SR * (ux * ux + uy * uy - 2.0 * uz * uz)
    geo[6:7, :] = Q75 * 2.0 * HR * (ux * uy)
    geo[7:8, :] = Q75 * 2.0 * HR * (ux * uz)
    geo[8:9, :] = Q75 * 2.0 * HR * (uy * uz)
    geo[9:10, :] = smooth
    geo[10:11, :] = live
    geo[11:12, :] = r
    geo[12:13, :] = dx
    geo[13:14, :] = dy
    geo[14:15, :] = dz
    order = (iota((8, EDGES), 0) + 1).astype(F32) * (math.pi / CUTOFF)
    geo[16:24, :] = smooth * BESSEL * jnp.sin(order * r) * inv
    hot_c = jnp.where(iota((NSPEC, EDGES), 0).astype(F32) == cent[3:4, :], 1.0, 0.0)
    grad = cent[4:5, :] * jnp.sum(hot_c * columns[0:64, 8:9], 0, keepdims=True)
    geo[15:16, :] = grad
    geo[24:25, :] = grad * smooth
    geo[25:26, :] = gat[3:4, :]
    geo[26:32, :] = jnp.zeros((6, EDGES), F32)

    def embed_product(i, out):
        cols = pl.ds(i * 256, 256)
        out[...] = dot(table[...], embed_inputs(cent, geo, cols), 0, 0)

    def embed(i, before):
        cols = pl.ds(i * 256, 256)
        sm = geo[9:10, cols]
        for b in range(8):
            rows = pl.ds(b * 128, 128)
            p = before[rows, :]
            x0h[rows, cols], x0l[rows, cols] = split(p * sigmoid(p) * sm)
        vw[:, cols] = dot3(
            veh[...], vel[...], x0h[0:LATENT, cols], x0l[0:LATENT, cols], 1, 0
        )

    staggered(4, (za, zb), embed_product, embed)
    make_env(geo, vw.at[64:128, :], g0)

    def tensor(k):
        cols = lanes(k, 128)
        v = vw[0:64, cols]
        y = [geo[c : c + 1, cols] for c in range(9)]
        e0 = rows_of(g0, 0)
        e1, e2, e3 = rows_of(g0, 1), rows_of(g0, 2), rows_of(g0, 3)
        a, b, c = y[1] * e1, y[2] * e2, y[3] * e3
        vec = a + b + c
        quad = y[4] * rows_of(g0, 4)
        for m in range(5, 9):
            quad = quad + y[m] * rows_of(g0, m)
        x0h[1024:1088, cols], x0l[1024:1088, cols] = split(v * e0)
        x0h[1088:1152, cols], x0l[1088:1152, cols] = split(v * vec)
        x0h[1152:1216, cols], x0l[1152:1216, cols] = split(v * quad)
        p = [rows_of(path, n) for n in range(9)]
        e12, e13 = y[1] * e2, y[1] * e3
        e21, e23 = y[2] * e1, y[2] * e3
        e31, e32 = y[3] * e1, y[3] * e2
        q00 = HR * y[4] + SR * y[5]
        q11 = SR * y[5] - HR * y[4]
        q22 = -2.0 * SR * y[5]
        q01, q02, q12 = HR * y[6], HR * y[7], HR * y[8]
        f1[0:64, cols] = v * (p[0] * e0 + p[1] * vec)
        p3g = p[3] * e0
        f1[64:128, cols] = v * (
            p[2] * e1 + p3g * y[1] + p[4] * (e23 - e32) + p[5] * (q00 * e1 + q01 * e2 + q02 * e3)
        )
        f1[128:192, cols] = v * (
            p[2] * e2 + p3g * y[2] + p[4] * (e31 - e13) + p[5] * (q01 * e1 + q11 * e2 + q12 * e3)
        )
        f1[192:256, cols] = v * (
            p[2] * e3 + p3g * y[3] + p[4] * (e12 - e21) + p[5] * (q02 * e1 + q12 * e2 + q22 * e3)
        )
        p8g = p[8] * e0
        pair = (
            HR * (a - b),
            SR * (a + b - 2.0 * c),
            HR * (e12 + e21),
            HR * (e13 + e31),
            HR * (e23 + e32),
        )
        for m in range(5):
            f1[(4 + m) * 64 : (5 + m) * 64, cols] = v * (
                p[6] * pair[m] + p[7] * rows_of(g0, 4 + m) + p8g * y[4 + m]
            )

    over(8, tensor)

    def layer_product(i, out):
        cols = pl.ds(i * 256, 256)
        out[...] = dot3(w0h[...], w0l[...], x0h[:, cols], x0l[:, cols], 0, 0)

    def layer(i, zs):
        cols = pl.ds(i * 256, 256)
        sm = geo[9:10, cols]
        for b in range(8):
            rows = pl.ds(b * 128, 128)
            z = zs[rows, :]
            z0[rows, cols] = z
            old = x0h[rows, cols].astype(F32) + x0l[rows, cols].astype(F32)
            x1h[rows, cols], x1l[rows, cols] = split((old + sm * (z * sigmoid(z))) * RH)
        w1[:, cols] = dot3(
            evh[...], evl[...], x1h[0:LATENT, cols], x1l[0:LATENT, cols], 1, 0
        )

    staggered(4, (za, zb), layer_product, layer)
    make_env(geo, w1, g1)

    def scalars(k):
        cols = lanes(k, 128)
        s0 = rows_of(f1, 0, cols) * rows_of(g1, 0)
        s1 = rows_of(f1, 1, cols) * rows_of(g1, 1)
        for c in range(2, 4):
            s1 = s1 + rows_of(f1, c, cols) * rows_of(g1, c)
        s2 = rows_of(f1, 4, cols) * rows_of(g1, 4)
        for c in range(5, 9):
            s2 = s2 + rows_of(f1, c, cols) * rows_of(g1, c)
        x1h[1024:1088, cols], x1l[1024:1088, cols] = split(s0)
        x1h[1088:1152, cols], x1l[1088:1152, cols] = split(s1)
        x1h[1152:1216, cols], x1l[1152:1216, cols] = split(s2)

    over(8, scalars)


def grad_kernel(mine, place, xh, xl, qh, ql, out):
    block = place[3] if mine else 1 - place[3]
    for n in range(0, HALF, QUARTER):
        rows = pl.ds(pl.multiple_of(block * HALF, HALF) + n, QUARTER)
        out[:, n : n + QUARTER] = dot3(xh[...], xl[...], qh[rows, :], ql[rows, :], 1, 1)


def late_kernel(x1h, x1l, wh, wl, columns, geo, qh, ql, side, dout, acc, za, zb):
    acc[...] = jnp.zeros_like(acc)
    side[...] = jnp.zeros_like(side)

    def product(i, out):
        cols = pl.ds(i * 256, 256)
        out[...] = dot3(wh[...], wl[...], x1h[:, cols], x1l[:, cols], 0, 0)

    def step(i, zs):
        cols = pl.ds(i * 256, 256)
        sm = geo[9:10, cols]
        gs = geo[24:25, cols]
        scale = gs * sm * RH
        reach = jnp.zeros((8, 256), F32)
        total = jnp.zeros((8, 256), F32)
        for b in range(8):
            rows = pl.ds(b * 128, 128)
            si, dsi = silu_both(zs[rows, :])
            ow = columns[:, b : b + 1]
            qh[rows, cols], ql[rows, cols] = split((ow * scale) * dsi)
            lat = (x1h[rows, cols].astype(F32) + x1l[rows, cols].astype(F32) + sm * si) * RH
            part = gs * lat
            acc[rows, :] += part[:, 0:128] + part[:, 128:256]
            reach = reach + jnp.sum((ow * si).reshape(16, 8, 256), 0)
            total = total + jnp.sum((ow * lat).reshape(16, 8, 256), 0)
        side[0:1, cols] = jnp.sum(reach, 0, keepdims=True)
        side[1:2, cols] = jnp.sum(total, 0, keepdims=True)

    staggered(4, (za, zb), product, step)
    dout[...] = jnp.broadcast_to(jnp.sum(acc[...].T, 0, keepdims=True), dout.shape)


def mid_kernel(qh, ql, wh, wl, f1, g1, w1, geo, ds1, dwh, dwl, dy, denv):
    def scal(i):
        cols = lanes(i, 256)
        ds1[:, cols] = dot3(wh[1024:1216, :], wl[1024:1216, :], qh[:, cols], ql[:, cols], 1, 0)

    over(4, scal)
    for c in range(9):
        kind = 0 if c == 0 else (1 if c < 4 else 2)
        acc = None
        for k in range(8):
            cols = pl.ds(k * 128, 128)
            term = rows_of(ds1, kind, cols) * rows_of(f1, c, cols)
            acc = term if acc is None else acc + term
        denv[c * 64 : (c + 1) * 64, :] = slot_total(acc) * NORM
    env_back(geo, w1, denv, dwh, dwl, dy, None)


def env_back(geo, w, denv, dwh, dwl, dy, more):
    def step(k):
        cols = lanes(k, 128)
        acc = rows_of(denv, 0)
        wk = w[:, cols]
        rows = [jnp.zeros((1, 128), F32)]
        for c in range(1, 9):
            d = rows_of(denv, c)
            acc = acc + geo[c : c + 1, cols] * d
            rows.append(jnp.sum(wk * d, 0, keepdims=True))
        dwh[:, cols], dwl[:, cols] = split(acc)
        for c in range(1, 9):
            if more is None:
                dy[c : c + 1, cols] = rows[c]
            else:
                dy[c : c + 1, cols] = rows[c] + more[c : c + 1, cols]

    over(8, step)


def early_kernel(
    q1h, q1l, wh, wl, evh, evl, dwh, dwl, columns, geo, z0, dlat, qh, ql, side, da, db
):
    side[...] = jnp.zeros_like(side)

    def product(i, out):
        cols = pl.ds(i * 256, 256)
        out[...] = dot3(
            wh[0:LATENT, :], wl[0:LATENT, :], q1h[:, cols], q1l[:, cols], 1, 0
        ) + dot3(evh[...], evl[...], dwh[:, cols], dwl[:, cols], 0, 0)

    def step(i, ds):
        cols = pl.ds(i * 256, 256)
        sm = geo[9:10, cols] * RH
        gs = geo[24:25, cols] * RH
        total = jnp.zeros((8, 256), F32)
        for b in range(8):
            rows = pl.ds(b * 128, 128)
            dl = ds[rows, :] + columns[:, b : b + 1] * gs
            dlat[rows, cols] = dl * RH
            si, dsi = silu_both(z0[rows, cols])
            qh[rows, cols], ql[rows, cols] = split(dl * dsi * sm)
            total = total + jnp.sum((dl * si).reshape(16, 8, 256), 0)
        side[0:1, cols] = jnp.sum(total, 0, keepdims=True) * RH

    staggered(4, (da, db), product, step)


def couple_kernel(
    qh, ql, wh, wl, vw, geo, g0, g1, ds1, path, dy1,
    dvwh, dvwl, dy, dpath,
    ds0, denv, dyv,
):
    def scal(i):
        cols = lanes(i, 256)
        ds0[:, cols] = dot3(wh[1024:1216, :], wl[1024:1216, :], qh[:, cols], ql[:, cols], 1, 0)

    over(4, scal)
    denv[...] = jnp.zeros_like(denv)
    dpath[...] = jnp.zeros_like(dpath)

    def step(k):
        cols = lanes(k, 128)
        v = vw[0:64, cols]
        y = [geo[c : c + 1, cols] for c in range(9)]
        e = [rows_of(g0, c) for c in range(9)]
        p = [rows_of(path, n) for n in range(9)]
        s = [rows_of(ds0, n, cols) for n in range(3)]
        u = [rows_of(ds1, n, cols) for n in range(3)]
        f0 = u[0] * rows_of(g1, 0)
        fv = [u[1] * rows_of(g1, c) for c in range(1, 4)]
        fq = [u[2] * rows_of(g1, c) for c in range(4, 9)]
        yv, yq, ev_, eq = y[1:4], y[4:9], e[1:4], e[4:9]

        def dot_of(a, b):
            out = a[0] * b[0]
            for i in range(1, len(a)):
                out = out + a[i] * b[i]
            return out

        m00 = HR * yq[0] + SR * yq[1]
        m11 = SR * yq[1] - HR * yq[0]
        m22 = -2.0 * SR * yq[1]
        m01, m02, m12 = HR * yq[2], HR * yq[3], HR * yq[4]
        t00 = HR * fq[0] + SR * fq[1]
        t11 = SR * fq[1] - HR * fq[0]
        t22 = (-2.0 * SR) * fq[1]
        t01, t02, t12 = HR * fq[2], HR * fq[3], HR * fq[4]

        te = [
            t00 * ev_[0] + t01 * ev_[1] + t02 * ev_[2],
            t01 * ev_[0] + t11 * ev_[1] + t12 * ev_[2],
            t02 * ev_[0] + t12 * ev_[1] + t22 * ev_[2],
        ]
        ty = [
            t00 * yv[0] + t01 * yv[1] + t02 * yv[2],
            t01 * yv[0] + t11 * yv[1] + t12 * yv[2],
            t02 * yv[0] + t12 * yv[1] + t22 * yv[2],
        ]
        mf = [
            m00 * fv[0] + m01 * fv[1] + m02 * fv[2],
            m01 * fv[0] + m11 * fv[1] + m12 * fv[2],
            m02 * fv[0] + m12 * fv[1] + m22 * fv[2],
        ]
        ef = [
            ev_[1] * fv[2] - ev_[2] * fv[1],
            ev_[2] * fv[0] - ev_[0] * fv[2],
            ev_[0] * fv[1] - ev_[1] * fv[0],
        ]
        fy = [
            fv[1] * yv[2] - fv[2] * yv[1],
            fv[2] * yv[0] - fv[0] * yv[2],
            fv[0] * yv[1] - fv[1] * yv[0],
        ]
        e_fv = dot_of(ev_, fv)
        y_fv = dot_of(yv, fv)
        e_fq = dot_of(eq, fq)
        y_fq = dot_of(yq, fq)
        vec = dot_of(yv, ev_)
        y_te = dot_of(yv, te)
        e_mf = dot_of(ev_, mf)
        y_ef = dot_of(yv, ef)

        grads = (
            e[0] * f0,
            vec * f0,
            e_fv,
            e[0] * y_fv,
            y_ef,
            e_mf,
            y_te,
            e_fq,
            e[0] * y_fq,
        )
        for n in range(9):
            dpath[n * 64 : (n + 1) * 64, :] += v * grads[n]

        p1f = p[1] * f0
        d0 = s[0] * e[0] + p[0] * e[0] * f0 + p[2] * e_fv + p[7] * e_fq
        p3e = p[3] * e[0]
        p8e = p[8] * e[0]
        s1f = s[1] + p1f
        dv = d0
        for i in range(3):
            di = s1f * ev_[i] + p3e * fv[i] + p[4] * ef[i] + p[6] * te[i]
            dv = dv + yv[i] * di
            dyv[1 + i : 2 + i, cols] = jnp.sum(v * di, 0, keepdims=True)
        a, b, c = fv[0] * ev_[0], fv[1] * ev_[1], fv[2] * ev_[2]
        bil = (
            HR * (a - b),
            SR * (a + b - 2.0 * c),
            HR * (fv[0] * ev_[1] + fv[1] * ev_[0]),
            HR * (fv[0] * ev_[2] + fv[2] * ev_[0]),
            HR * (fv[1] * ev_[2] + fv[2] * ev_[1]),
        )
        for m in range(5):
            dm = s[2] * eq[m] + p[5] * bil[m] + p8e * fq[m]
            dv = dv + yq[m] * dm
            dyv[4 + m : 5 + m, cols] = jnp.sum(v * dm, 0, keepdims=True)
        dvwh[0:64, cols], dvwl[0:64, cols] = split(dv)

        denv[0:64, :] += v * (s[0] + p[0] * f0 + p[3] * y_fv + p[8] * y_fq)
        for i in range(3):
            denv[(1 + i) * 64 : (2 + i) * 64, :] += v * (
                s1f * yv[i] + p[2] * fv[i] + p[4] * fy[i] + p[5] * mf[i] + p[6] * ty[i]
            )
        for m in range(5):
            denv[(4 + m) * 64 : (5 + m) * 64, :] += v * (s[2] * yq[m] + p[7] * fq[m])

    over(8, step)
    for c in range(9):
        denv[c * 64 : (c + 1) * 64, :] = slot_total(rows_of(denv, c)) * NORM
    dyv[0:1, :] = jnp.zeros((1, EDGES), F32)
    dyv[...] += dy1[...]
    env_back(geo, vw.at[64:128, :], denv, dvwh.at[64:128, :], dvwl.at[64:128, :], dy, dyv)


def pre_kernel(
    half, qh, ql, wh, wl, veh, vel, dvwh, dvwl, dl, table, cent, geo, rad_w,
    qph, qpl, side, drad, da, db, pre,
):
    base = half * HALF
    wr = slice(base, base + HALF)
    rwh, rwl = split(jnp.concatenate([rad_w[:, wr], jnp.zeros((8, HALF), F32)], 0))
    side[...] = jnp.zeros_like(side)

    def product(i, out):
        cols = pl.ds(i * 256, 256)
        out[...] = dot3(wh[wr, :], wl[wr, :], qh[:, cols], ql[:, cols], 1, 0) + dot3(
            veh[:, wr], vel[:, wr], dvwh[:, cols], dvwl[:, cols], 0, 0
        )

    def step(i, ds):
        cols = pl.ds(i * 256, 256)
        sm = geo[9:10, cols]
        total = jnp.zeros((8, 256), F32)
        pre[...] = dot(table[:, wr], embed_inputs(cent, geo, cols), 0, 0)
        for b in range(4):
            rows = pl.ds(b * 128, 128)
            dd = ds[rows, :] + dl[pl.ds(base + b * 128, 128), cols]
            si, dsi = silu_both(pre[rows, :])
            qph[rows, cols], qpl[rows, cols] = split(dd * dsi * sm)
            total = total + jnp.sum((dd * si).reshape(16, 8, 256), 0)
        side[0:1, cols] = jnp.sum(total, 0, keepdims=True)
        drad[:, cols] = dot3(rwh, rwl, qph[:, cols], qpl[:, cols], 1, 0)[0:8]

    staggered(4, (da, db), product, step)


def last_kernel(
    rows_y, rows_z, place, qps, sides, drads, geo, slots, cent, sl, se, dy,
    dpath, columns, dout, more,
    small_keep, small_send, energy,
    ghost, small, spread,
):
    kinds = iota((NSPEC, EDGES), 0).astype(F32)
    hot_c = jnp.where(kinds == cent[3:4, :], 1.0, 0.0)
    hot_n = jnp.where(kinds == geo[25:26, :], 1.0, 0.0)
    hots = jnp.concatenate([hot_c, hot_n], 0).astype(BF16)
    rad = geo[16:24, :]
    rad_h = rad.astype(BF16).astype(F32)
    rads = jnp.concatenate([rad_h, rad - rad_h], 0).astype(BF16)
    left = jnp.concatenate([hots, rads], 0)
    for n, (qh, ql) in enumerate(zip(qps[0::2], qps[1::2])):
        full = dot(left, qh[...], 1, 1)
        rest = dot(left, ql[...], 1, 1)
        part = slice(n * HALF, (n + 1) * HALF)
        small[0:128, part] = full[0:128] + rest[0:128]
        small[128:136, part] = full[128:136] + full[136:144] + rest[128:136]

    live, r, smooth = geo[10:11, :], geo[11:12, :], geo[9:10, :]
    inv = 1.0 / r
    grad = geo[15:16, :]
    reach = sl[0:1, :]
    lat_out = sl[1:2, :]
    order = (iota((8, EDGES), 0) + 1).astype(F32) * (math.pi / CUTOFF)
    angle = order * r
    sine = jnp.sin(angle) * inv
    cosine = jnp.cos(angle) * inv
    dr8 = drads[0][...] + drads[1][...]
    d_s = (
        grad * lat_out
        + grad * smooth * RH * reach
        + se[0:1, :]
        + sides[0][0:1, :]
        + sides[1][0:1, :]
        + BESSEL * jnp.sum(dr8 * sine, 0, keepdims=True)
    )
    t = r / CUTOFF
    t2 = t * t
    gap = 1.0 - t
    d_r = d_s * (live * (-168.0 / CUTOFF) * (t2 * t2 * t) * (gap * gap)) + (
        smooth * BESSEL
    ) * jnp.sum(dr8 * (order * cosine - sine * inv), 0, keepdims=True)
    ux, uy, uz = geo[12:13, :] * inv, geo[13:14, :] * inv, geo[14:15, :] * inv
    yy = [dy[c : c + 1, :] for c in range(9)]
    h2, s2 = 2.0 * HR * Q75, 2.0 * SR * Q75
    gx = R3 * yy[1] + ux * (h2 * yy[4] + s2 * yy[5]) + h2 * (uy * yy[6] + uz * yy[7])
    gy = R3 * yy[2] + uy * (s2 * yy[5] - h2 * yy[4]) + h2 * (ux * yy[6] + uz * yy[8])
    gz = R3 * yy[3] - 2.0 * s2 * uz * yy[5] + h2 * (ux * yy[7] + uy * yy[8])
    along = ux * gx + uy * gy + uz * gz
    zero = jnp.zeros((5, EDGES), F32)
    disp = jnp.concatenate(
        [
            live * ((gx - ux * along) * inv + ux * d_r),
            live * ((gy - uy * along) * inv + uy * d_r),
            live * ((gz - uz * along) * inv + uz * d_r),
            zero,
        ],
        0,
    )
    hi, mid, lo = pieces(disp)
    disp24 = jnp.concatenate([hi, mid, lo], 0).astype(BF16)
    acc = None
    mine = None
    for k in range(8):
        term = disp[:, k * 128 : (k + 1) * 128]
        mine = term if mine is None else mine + term
    mine = slot_total(mine)
    for i in range(4):
        cols = pl.ds(i * 256, 256)
        hot = jnp.where(iota((NTAB, 256), 0) == slots[:, cols], 1.0, 0.0).astype(BF16)
        term = dot(disp24[:, i * 256 : (i + 1) * 256], hot, 1, 1)
        acc = term if acc is None else acc + term
    ghost[...] = acc[0:8] + acc[8:16] + acc[16:24]
    lane = iota((8, 128), 1)
    middle = ghost[:, 512:640] - jnp.where(
        (lane >= ATOMS) & (lane < 2 * ATOMS), pltpu.roll(mine, ATOMS, 1), 0.0
    )
    ghost[:, 512:640] = middle
    atoms = spread.shape[1]
    spread[...] = jnp.zeros_like(spread)
    total = jnp.zeros_like(spread)
    for bx in range(3):
        for by in range(3):
            block = 3 * bx + by
            spread[:, 0:128] = ghost[:, block * 128 : (block + 1) * 128]
            start = place[4] + ((bx - 1) * rows_y + by - 1) * rows_z * ATOMS - ATOMS
            total = total + pltpu.roll(spread[...], lax.rem(start + 2 * atoms, atoms), 1)
    for n in range(atoms // LATENT):
        small[144 + 8 * n : 152 + 8 * n, :] = total[:, n * LATENT : (n + 1) * LATENT]

    edge_energy = smooth * lat_out
    total = None
    for k in range(8):
        term = edge_energy[:, k * 128 : (k + 1) * 128]
        total = term if total is None else total + term
    total = slot_total(jnp.broadcast_to(total, (8, 128)))[0:1]
    hot = jnp.where(iota((NSPEC, 128), 0).astype(F32) == cent[3:4, 0:128], 1.0, 0.0)
    energy[...] = jnp.broadcast_to(
        jnp.sum(hot * columns[0:64, 8:9], 0, keepdims=True) * total
        + jnp.sum(hot * columns[0:64, 9:10], 0, keepdims=True),
        energy.shape,
    )
    cot = cent[4:5, 0:128] * jnp.where(iota((1, 128), 1) < ATOMS, 1.0, 0.0)
    stack = jnp.concatenate(
        [dpath[...], hot * (cot * total), hot * cot, jnp.zeros((64, 128), F32)], 0
    )
    row = jnp.sum(stack.T, 0, keepdims=True)
    small[136:144, :] = jnp.zeros((8, LATENT), F32)
    small[136:137, 0:768] = row
    small[137:138, :] = dout[0:1, :]
    mine = pl.ds(pl.multiple_of(place[3] * HALF, HALF), HALF)
    other = pl.ds(pl.multiple_of((1 - place[3]) * HALF, HALF), HALF)
    for out, cols in ((small_keep, mine), (small_send, other)):
        out[0:192, :] = more[:, cols]
        out[192:, :] = small[:, cols]


def weights_kernel(dvwh, dvwl, x0h, x0l, dw1h, dw1l, x1h, x1l, out):
    out[0:128, :] = dot3(dvwh[...], dvwl[...], x0h[0:LATENT, :], x0l[0:LATENT, :], 1, 1)
    out[128:192, :] = dot3(dw1h[...], dw1l[...], x1h[0:LATENT, :], x1l[0:LATENT, :], 1, 1)


def halves(shape, dim):
    rows, cols = shape
    return (rows // 2, cols) if dim == 0 else (rows, cols // 2) if dim == 1 else shape


def half_of(shape, dim, bit):
    rows, cols = shape
    if dim == 0:
        rows //= 2
        return pl.ds(pl.multiple_of(bit * rows, 8), rows), slice(None)
    cols //= 2
    return slice(None), pl.ds(pl.multiple_of(bit * cols, 128), cols)


def down_kernel(dim, flag, place, keep, got, *outs):
    if dim is None:
        outs[0][...] = keep[...] + got[...]
        return
    for out, bit in zip(outs, (1 - place[flag], place[flag])):
        index = half_of(keep.shape, dim, bit)
        out[...] = keep[index] + got[index]


def up_kernel(dim, flag, place, mine, got, out):
    out[half_of(out.shape, dim, place[flag])] = mine[...]
    out[half_of(out.shape, dim, 1 - place[flag])] = got[...]


def end_kernel(parts, place, *refs):
    srcs, out, sem = refs[: len(parts)], refs[-2], refs[-1]
    copies = []
    for n, ((layer, start, mine), src) in enumerate(zip(parts, srcs)):
        block = place[3] if mine else 1 - place[3]
        cols = pl.ds(pl.multiple_of(block * HALF, HALF), HALF)
        rows = pl.ds(start, src.shape[0])
        copies.append(pltpu.make_async_copy(src, out.at[layer, rows, cols], sem.at[n]))
    for copy in copies:
        copy.start()
    for copy in copies:
        copy.wait()


def small_end_kernel(
    core_at, place, mine, got, energy,
    center, neigh, radial, value, env, path, out, scale, shift, grad, energies,
):
    for src, b in ((mine, place[core_at]), (got, 1 - place[core_at])):
        cols = pl.ds(pl.multiple_of(b * HALF, HALF), HALF)
        value[:, cols] = src[0:64, :]
        env[0, :, cols] = src[64:128, :]
        env[1, :, cols] = src[128:192, :]
        center[:, cols] = src[192:256, :]
        neigh[:, cols] = src[256:320, :]
        radial[:, cols] = src[320:328, :]
    is_first = place[core_at] == 0

    def whole(rows):
        first = jnp.where(is_first, mine[rows, :], got[rows, :])
        second = jnp.where(is_first, got[rows, :], mine[rows, :])
        return jnp.concatenate([first, second], 1)

    base = 336 + 8 * (place[4] // LATENT)
    spread = whole(pl.ds(pl.multiple_of(base, 8), 8))
    shift_by = LATENT - lax.rem(place[4], LATENT)
    grad[...] = pltpu.roll(spread, lax.rem(shift_by, LATENT), 1)[0:3, 0:ATOMS]
    energies[...] = energy[0:1, 0:ATOMS]
    row = whole(slice(328, 336))
    for n in range(9):
        path[n : n + 1, :] = row[0:1, n * 64 : (n + 1) * 64]
    scale[...] = row[0:1, 576:640]
    shift[...] = row[0:1, 640:704]
    for n in range(8):
        out[n : n + 1, :] = row[1:2, n * 128 : (n + 1) * 128]


VSPEC = pl.BlockSpec(memory_space=pltpu.VMEM)
SSPEC = pl.BlockSpec(memory_space=pltpu.SMEM)
ASPEC = pl.BlockSpec(memory_space=pl.ANY)
HSPEC = pl.BlockSpec(memory_space=pltpu.HBM)


class Order:
    def __init__(self):
        self.token = None
        self.free = False

    def __call__(
        self, body, outs, args, scratch=(), scalar=False, hbm=(), plain=False, alias=None, us=1,
        limit=6, name=None,
    ):
        specs = [HSPEC if n in hbm else VSPEC for n in range(len(args))]
        if scalar:
            specs[0] = SSPEC
        count, given = len(args), len(outs)
        tokens = () if self.token is None or self.free else (self.token,)

        def kernel(*refs):
            after = refs[count + len(tokens) :]
            if self.free:
                return body(*refs[:count], *after)
            after[given][...] = jnp.zeros((8, 128), F32)
            body(*refs[:count], *after[:given], *after[given + 1 :])

        if plain:
            shapes = [jax.ShapeDtypeStruct(shape, dtype) for shape, dtype in outs]
        else:
            shapes = [pltpu.VMEM(shape, dtype) for shape, dtype in outs]
        out_spec = HSPEC if plain == "hbm" else VSPEC
        got = pl.pallas_call(
            kernel,
            name=name or getattr(body, "func", body).__name__,
            out_shape=shapes + ([] if self.free else [pltpu.VMEM((8, 128), F32)]),
            in_specs=specs + [ASPEC] * len(tokens),
            out_specs=[out_spec] * given + ([] if self.free else [VSPEC]),
            scratch_shapes=list(scratch),
            input_output_aliases=alias or {},
            compiler_params=pltpu.CompilerParams(vmem_limit_bytes=limit << 20),
            cost_estimate=pl.CostEstimate(
                flops=int(us * 3e9), bytes_accessed=1 << 20, transcendentals=0
            ),
        )(*args, *tokens)
        if self.free:
            return got
        self.token = got[-1]
        return got[:-1]


def is_up(axis, bit):
    return (lax.axis_index(axis) // bit) & 1


def even_pairs(axis):
    return [(i, i ^ 1) for i in range(lax.axis_size(axis))]


def odd_pairs(axis):
    count = lax.axis_size(axis)
    return [p for i in range(1, count - 1, 2) for p in ((i, i + 1), (i + 1, i))]


def neighbours_of(axis, even, odd):
    pairs = odd_pairs(axis)
    return (
        lax.ppermute(even, axis, even_pairs(axis)),
        lax.ppermute(odd, axis, pairs) if pairs else jnp.zeros_like(odd),
    )


class Route:
    def __init__(self, mesh_sizes, base, tall_first=False):
        sizes = dict(mesh_sizes)
        names = list(sizes)

        def bits(axis, least=1):
            return [(axis, 1 << n) for n in range(20) if least <= 1 << n < sizes[axis]]

        flat, tall = bits("gx"), bits("gy") + bits("gz", 2)
        first = [("gz", 1)]
        one, two = (flat, tall), (flat[::-1], tall[::-1])
        if tall_first:
            one, two = one[::-1], two[::-1]
        self.steps = list(zip(first + one[0] + one[1], first + two[0] + two[1]))
        self.count = len(self.steps)
        self.base = base
        self.names = tuple(names)
        coords = [()]
        for name in names:
            coords = [c + (i,) for c in coords for i in range(sizes[name])]
        index = {c: n for n, c in enumerate(coords)}
        self.pairs = []
        for step in self.steps:
            pairs = []
            for c in coords:
                axis, bit = step[c[names.index("gz")] & 1]
                at = names.index(axis)
                pairs.append((index[c], index[c[:at] + (c[at] ^ bit,) + c[at + 1 :]]))
            self.pairs.append(pairs)

    def flags(self):
        core = is_up("gz", 1)
        return [jnp.where(core == 1, is_up(*two), is_up(*one)) for one, two in self.steps]

    def swap(self, x, at):
        return lax.ppermute(x, self.names, self.pairs[at])


class Sum:
    def __init__(self, name, order, place, route, send, dims):
        self.name = name
        self.order, self.place, self.route = order, place, route
        self.dims = (1,) + dims + (None,) * (route.count - 1 - len(dims))
        self.keep, self.send = None, send
        self.at, self.rising = 0, False
        self.shapes = []
        self.launch()

    def launch(self):
        with jax.named_scope(f"sum_{self.name}_{'up' if self.rising else 'down'}_{self.at}"):
            self.got = self.route.swap(self.send, self.at)

    @property
    def over(self):
        return self.rising and self.at == 0

    def land(self):
        (self.climb if self.rising else self.descend)()
        self.launch()

    def call(self, body, dim, flag, shapes, args):
        return self.order(
            functools.partial(body, dim, flag),
            [(shape, F32) for shape in shapes],
            (self.place, *args),
            scalar=True,
            us=2,
            name=f"land_{self.name}_{'up' if self.rising else 'down'}_{self.at}",
        )

    def descend(self):
        self.shapes.append(self.keep.shape)
        self.at += 1
        last = self.at == self.route.count
        dim = None if last else self.dims[self.at]
        shapes = [halves(self.keep.shape, dim)] * (1 if dim is None else 2)
        outs = self.call(
            down_kernel, dim, self.route.base + self.at, shapes, (self.keep, self.got)
        )
        self.send, self.keep = outs[0], outs[-1]
        if last:
            self.rising = True
            self.rise()

    def rise(self):
        self.at -= 1
        while self.at > 0 and self.dims[self.at] is None:
            self.at -= 1

    def climb(self):
        (self.send,) = self.call(
            up_kernel,
            self.dims[self.at],
            self.route.base + self.at,
            [self.shapes[self.at - 1]],
            (self.send, self.got),
        )
        self.rise()


def per_device(
    positions,
    species,
    neighbours,
    embed_center,
    embed_neigh,
    embed_radial,
    value_proj,
    env_weight,
    latent_weight,
    path_weight,
    out_weight,
    scale_table,
    shift_table,
    cotangent,
):
    vm, sem = pltpu.VMEM, pltpu.SemaphoreType
    order = Order()
    sizes = [(axis, lax.axis_size(axis)) for axis in ("gx", "gy", "gz")]
    route = Route(sizes, 5)
    steep = Route(sizes, 5 + route.count, tall_first=True)
    first_atom = lax.axis_index(("gx", "gy", "gz")) * ATOMS
    place = [is_up("gz", 1), is_up("gy", 1), is_up("gx", 1), is_up("gz", 1), first_atom]
    place = jnp.stack(place + route.flags() + steep.flags()).astype(jnp.int32)
    spec_row = species.reshape(1, ATOMS)

    (table,) = order(pack_kernel, [((8, 128), F32)], (positions, spec_row), us=0.3)
    even, odd = neighbours_of("gz", table, table)
    (table,) = order(
        join_z_kernel, [((8, 128), F32)], (place, table, even, odd), scalar=True, us=0.3
    )
    even, odd = neighbours_of("gy", table, table)
    (table,) = order(
        join_y_kernel,
        [((8, 384), F32)],
        (place, table, even, odd),
        scalar=True,
        us=0.3,
    )
    even, odd = neighbours_of("gx", table, table)

    wide = ((WIDE, EDGES), BF16)
    half = ((HALF, EDGES), BF16)
    row64 = ((64, LATENT), BF16)
    row128 = ((128, LATENT), BF16)
    w0h, w0l, w1h, w1l, hots, veh, vel, evh, evl, path, columns, slots, cent, rad_w = order(
        prep_kernel,
        [
            wide, wide, wide, wide, ((288, LATENT), BF16), row128, row128, row64, row64,
            ((576, 128), F32), ((128, 128), F32), ((1, EDGES), jnp.int32), ((8, EDGES), F32),
            ((8, LATENT), F32),
        ],
        (latent_weight, embed_center, embed_neigh, embed_radial, value_proj.T,
         jnp.swapaxes(env_weight, 1, 2), neighbours, positions, spec_row,
         cotangent.reshape(1, ATOMS), path_weight, out_weight.reshape(8, 128),
         scale_table.reshape(1, NSPEC), shift_table.reshape(1, NSPEC)),
        [
            vm((NSPEC, LATENT), F32), vm((NSPEC, LATENT), F32), vm((CHANNELS, LATENT), F32),
            vm((2, CHANNELS, LATENT), F32), vm((NB, ATOMS), jnp.int32), vm((3, ATOMS), F32),
            vm((1, ATOMS), jnp.int32), vm((1, ATOMS), F32), vm((9, CHANNELS), F32),
            vm((8, 128), F32), vm((1, NSPEC), F32), vm((1, NSPEC), F32), vm((128, 128), F32),
            sem.DMA((13,)),
        ],
        hbm=range(1, 14),
        us=4,
    )

    x0h, x0l, x1h, x1l, z0, vw, w1, geo, g0, g1, f1 = order(
        fwd_kernel,
        [
            wide, wide, wide, wide,
            ((LATENT, EDGES), F32), ((128, EDGES), F32), ((64, EDGES), F32), ((G_ROWS, EDGES), F32), ((576, 128), F32), ((576, 128), F32),
            ((576, EDGES), F32),
        ],
        (place, table, even, odd, slots, cent, w0h, w0l, hots, veh, vel, evh, evl, path, columns),
        [vm((8, EDGES), F32), vm((LATENT, 256), F32), vm((LATENT, 256), F32)],
        scalar=True,
        us=22,
        limit=18,
    )

    chains = {}

    def grad(mine, xh, xl, qh, ql):
        return order(
            functools.partial(grad_kernel, mine),
            [((WIDE, HALF), F32)],
            (place, xh, xl, qh, ql),
            scalar=True,
            us=4.6,
        )[0]

    def send(name, *args):
        chains[name] = Sum(name, order, place, route, grad(False, *args), (0, 0, 0, 1))

    def keep(name, *args):
        chains[name].keep = grad(True, *args)

    def late():
        return order(
            late_kernel,
            [
                ((LATENT, EDGES), BF16), ((LATENT, EDGES), BF16), ((8, EDGES), F32),
                ((8, LATENT), F32),
            ],
            (x1h, x1l, w1h, w1l, columns, geo),
            [vm((LATENT, 128), F32), vm((LATENT, 256), F32), vm((LATENT, 256), F32)],
            us=13,
            limit=17,
        )

    def mid():
        return order(
            mid_kernel,
            [((192, EDGES), F32), ((64, EDGES), BF16), ((64, EDGES), BF16), ((16, EDGES), F32)],
            (q1h, q1l, w1h, w1l, f1, g1, w1, geo),
            [vm((576, 128), F32)],
            us=3,
        )

    def early():
        return order(
            early_kernel,
            [
                ((LATENT, EDGES), F32), ((LATENT, EDGES), BF16), ((LATENT, EDGES), BF16),
                ((8, EDGES), F32),
            ],
            (q1h, q1l, w1h, w1l, evh, evl, dw1h, dw1l, columns, geo, z0),
            [vm((LATENT, 256), F32), vm((LATENT, 256), F32)],
            us=10,
            limit=12,
        )

    def couple():
        return order(
            couple_kernel,
            [
                ((128, EDGES), BF16), ((128, EDGES), BF16), ((16, EDGES), F32),
                ((576, 128), F32),
            ],
            (q0h, q0l, w0h, w0l, vw, geo, g0, g1, ds1, path, dy1),
            [vm((192, EDGES), F32), vm((576, 128), F32), vm((16, EDGES), F32)],
            us=6.3,
        )

    def before(h):
        return order(
            functools.partial(pre_kernel, h),
            [half, half, ((8, EDGES), F32), ((8, EDGES), F32)],
            (q0h, q0l, w0h, w0l, veh, vel, dvwh, dvwl, dlat, hots, cent, geo, rad_w),
            [vm((HALF, 256), F32), vm((HALF, 256), F32), vm((HALF, 256), F32)],
            us=7,
        )

    def land(names):
        for name in names.split():
            if not chains[name].over:
                chains[name].land()

    q1h, q1l, sl, dout = late()
    send("a", x1h, x1l, q1h, q1l)
    keep("a", x1h, x1l, q1h, q1l)
    ds1, dw1h, dw1l, dy1 = mid()
    land("a")
    dlat, q0h, q0l, se = early()
    send("c", x0h, x0l, q0h, q0l)
    land("a")
    keep("c", x0h, x0l, q0h, q0l)
    land("c a")
    dvwh, dvwl, dy, dpath = couple()
    land("a")
    (more,) = order(
        weights_kernel, [((192, LATENT), F32)], (dvwh, dvwl, x0h, x0l, dw1h, dw1l, x1h, x1l), us=4
    )
    pres = [before(0)]
    land("c a")
    pres.append(before(1))
    land("c")
    atoms = ATOMS * math.prod(size for _, size in sizes)
    height = 144 + 8 * (atoms // LATENT)
    qps = [x for got in pres for x in got[0:2]]
    small_keep, small_send, energy = order(
        lambda place, *refs: last_kernel(
            sizes[1][1], sizes[2][1], place, refs[0:4], refs[4:6], refs[6:8], *refs[8:]
        ),
        [((192 + height, HALF), F32), ((192 + height, HALF), F32), ((8, 128), F32)],
        (place, *qps, *[got[2] for got in pres], *[got[3] for got in pres], geo, slots, cent, sl,
         se, dy, dpath, columns, dout, more),
        [vm((8, NTAB), F32), vm((height, LATENT), F32), vm((8, atoms), F32)],
        scalar=True,
        us=5,
        name="last_kernel",
    )
    chains["s"] = s = Sum("s", order, place, route, small_send, (1, 1))
    s.keep = small_keep
    land("c s a")
    order.free = True
    land("s c a c s a s c s c s a s a")
    a, c = chains["a"], chains["c"]
    while not (a.over and s.over):
        for chain in (a, s):
            if not chain.over:
                chain.land()

    def finish(parts, arrays, done=()):
        last = 1 + len(arrays)
        return order(
            functools.partial(end_kernel, parts),
            [((2, WIDE, LATENT), F32)],
            (place, *arrays, *done),
            [sem.DMA((len(parts),))],
            scalar=True,
            hbm=(last,) if done else (),
            plain="hbm",
            alias={last: 0} if done else None,
            us=3,
        )

    d_latent = finish(((1, 0, True), (1, 0, False)), (a.send, a.got))
    center, neigh, radial, value, env, path_grad, out, scale, shift, position_grad, energies = order(
        functools.partial(small_end_kernel, 3),
        [
            ((NSPEC, LATENT), F32), ((NSPEC, LATENT), F32), ((NBESSEL, LATENT), F32),
            ((CHANNELS, LATENT), F32), ((2, CHANNELS, LATENT), F32), ((9, CHANNELS), F32),
            ((8, 128), F32), ((1, NSPEC), F32), ((1, NSPEC), F32), ((3, ATOMS), F32),
            ((1, ATOMS), F32),
        ],
        (place, s.send, s.got, energy),
        scalar=True,
        plain=True,
        us=2,
    )
    while not c.over:
        c.land()
    d_latent = finish(((0, 0, True),), (c.send,), tuple(d_latent))
    (d_latent,) = finish(((0, 0, False),), (c.got,), tuple(d_latent))
    return (
        energies.reshape(ATOMS),
        position_grad,
        center,
        neigh,
        radial,
        value.T,
        jnp.swapaxes(env, 1, 2),
        d_latent,
        path_grad,
        out.reshape(LATENT),
        scale.reshape(NSPEC),
        shift.reshape(NSPEC),
    )


def solution(mesh):
    everything = ("gx", "gy", "gz")
    return jax.shard_map(
        per_device,
        mesh=mesh,
        in_specs=(
            P(None, everything),
            P(everything),
            P(None, everything),
            P(),
            P(),
            P(),
            P(),
            P(),
            P(),
            P(),
            P(),
            P(),
            P(),
            P(everything),
        ),
        out_specs=(
            P(everything),
            P(None, everything),
            P(),
            P(),
            P(),
            P(),
            P(),
            P(),
            P(),
            P(),
            P(),
            P(),
        ),
        check_vma=False,
    )
```

profile of v0, /device:TPU:0, one launch (start us, length us, event | category | flops | bytes accessed | tf_op | source)
XLA Modules:
  0.0 233.3 jit_solution(14995955232838803881)
XLA Ops:
  0.7 0.7 copy-done.9
  1.3 0.7 copy-done.11
  2.5 0.7 collective-permute-done.refs_2_
  4.0 0.8 collective-permute-start.2
  4.8 5.8 %collective-permute-start.1 = (f32[8,128]{1,0:T(8,128)S(1)}, f32[8,128]{1,0:T(8,128)S(1)}, u32[]{:S(2)}, u32[]{:S(2)}) collective-permute-start(f32[8,128]{1,0:T(8,128)S(1)} %get-tuple-element.134.refs_1_), channel_id=1, source_target_pairs={{0,2},{2,0},{4,6},{6,4},{1,3},{3,1},{5,7},{7,5},{8,10},{10,8},{12,... | collective-permute-start | bytes 12296 | tf_op jit(solution)/shard_map/ppermute | solution.py:913
  10.6 1.6 collective-permute-done.1.refs_2_
  12.7 0.7 collective-permute-start.4
  13.4 4.3 %collective-permute-start.3 = (f32[8,384]{1,0:T(8,128)S(1)}, f32[8,384]{1,0:T(8,128)S(1)}, u32[]{:S(2)}, u32[]{:S(2)}) collective-permute-start(f32[8,384]{1,0:T(8,128)S(1)} %get-tuple-element.136.refs_1_), channel_id=1, source_target_pairs={{0,8},{8,0},{16,24},{24,16},{1,9},{9,1},{17,25},{25,17},{2,10},{10... | collective-permute-start | bytes 36872 | tf_op jit(solution)/shard_map/ppermute | solution.py:913
  17.8 3.8 %copy-done = f32[2,1216,1024]{2,1,0:T(8,128)S(1)} copy-done((f32[2,1216,1024]{2,1,0:T(8,128)S(1)}, f32[2,1216,1024]{2,1,0:T(8,128)}, u32[]{:S(2)}) %copy-start) | copy-done | bytes 9961496
  21.6 2.6 %prep_kernel.1 = (bf16[1216,1024]{1,0:T(8,128)(2,1)S(1)}, bf16[1216,1024]{1,0:T(8,128)(2,1)S(1)}, bf16[1216,1024]{1,0:T(8,128)(2,1)S(1)}, bf16[1216,1024]{1,0:T(...) custom-call(f32[2,1216,1024]{2,1,0:T(8,128)S(1)} %copy-done, ...), custom_call_target="tpu_custom_call" | custom-call | flops 12000000000 | bytes 1048576 | tf_op jit(solution)/shard_map/prep_kernel/pallas_call | solution.py:878
  24.3 18.9 %fwd_kernel.1 = (bf16[1216,1024]{1,0:T(8,128)(2,1)S(1)}, bf16[1216,1024]{1,0:T(8,128)(2,1)S(1)}, bf16[1216,1024]{1,0:T(8,128)(2,1)S(1)}, bf16[1216,1024]{1,0:T(8...) custom-call(s32[15]{0:T(128)S(1)} %stack.42.refs_0_, ...), custom_call_target="tpu_custom_call" | custom-call | flops 65999998976 | bytes 1048576 | tf_op jit(solution)/shard_map/fwd_kernel/pallas_call | solution.py:878
  43.3 11.0 %late_kernel.1 = (bf16[1024,1024]{1,0:T(8,128)(2,1)S(1)}, bf16[1024,1024]{1,0:T(8,128)(2,1)S(1)}, f32[8,1024]{1,0:T(8,128)S(1)}, f32[8,1024]{1,0:T(8,128)S(1)}, f32[8,128]{1,0:T(8,128)S(1)}) custom-call(bf16[1216,1024]{1,0:T(8,128)(2,1)S(1)} %get-tuple-element.150.refs_0_.refs_1_.refs_6_, bf16[1216,1024]{1,0:T(8,128)(2,1)S(1)} %get-tuple-element.151.refs_1_.refs_2_.refs_7_, ...), custom_call_target="tpu_custom_call" | custom-call | flops 38999998464 | bytes 1048576 | tf_op jit(solution)/shard_map/late_kernel/pallas_call | solution.py:878
  54.3 4.8 %grad_kernel.4 = (f32[1216,512]{1,0:T(8,128)S(1)}, f32[8,128]{1,0:T(8,128)S(1)}) custom-call(s32[15]{0:T(128)S(1)} %stack.42.refs_0_, bf16[1216,1024]{1,0:T(8,128)(2,1)S(1)} %get-tuple-element.150.refs_0_.refs_1_.refs_6_, bf16[1216,1024]{1,0:T(8,128)(2,1)S(1)} %get-tuple-element.151.refs_1_.refs_2_.refs_7_, ...), custom_call_target="tpu_custom_call" | custom-call | flops 13799999488 | bytes 1048576 | tf_op jit(solution)/shard_map/grad_kernel/pallas_call | solution.py:878
  59.3 4.6 %grad_kernel.5 = (f32[1216,512]{1,0:T(8,128)S(1)}, f32[8,128]{1,0:T(8,128)S(1)}) custom-call(s32[15]{0:T(128)S(1)} %stack.42.refs_0_, bf16[1216,1024]{1,0:T(8,128)(2,1)S(1)} %get-tuple-element.150.refs_0_.refs_1_.refs_6_, bf16[1216,1024]{1,0:T(8,128)(2,1)S(1)} %get-tuple-element.151.refs_1_.refs_2_.refs_7_, ...), custom_call_target="tpu_custom_call" | custom-call | flops 13799999488 | bytes 1048576 | tf_op jit(solution)/shard_map/grad_kernel/pallas_call | solution.py:878
  63.9 2.8 %mid_kernel.1 = (f32[192,1024]{1,0:T(8,128)S(1)}, bf16[64,1024]{1,0:T(8,128)(2,1)S(1)}, bf16[64,1024]{1,0:T(8,128)(2,1)S(1)}, f32[16,1024]{1,0:T(8,128)S(1)}, f32[8,128]{1,0:T(8,128)S(1)}) custom-call(bf16[1024,1024]{1,0:T(8,128)(2,1)S(1)} %get-tuple-element.156.refs_3_.refs_0_, bf16[1024,1024]{1,0:T(8,128)(2,1)S(1)} %get-tuple-element.157.refs_4_.refs_1_, ...), custom_call_target="tpu_custom_call" | custom-call | flops 8999999488 | bytes 1048576 | tf_op jit(solution)/shard_map/mid_kernel/pallas_call | solution.py:878
  66.8 0.8 land_a_down_1.1
  67.7 10.4 %early_kernel.1 = (f32[1024,1024]{1,0:T(8,128)S(1)}, bf16[1024,1024]{1,0:T(8,128)(2,1)S(1)}, bf16[1024,1024]{1,0:T(8,128)(2,1)S(1)}, f32[8,1024]{1,0:T(8,128)S(1)}, f32[8,128]{1,0:T(8,128)S(1)}) custom-call(bf16[1024,1024]{1,0:T(8,128)(2,1)S(1)} %get-tuple-element.156.refs_3_.refs_0_, bf16[1024,1024]{1,0:T(8,128)(2,1)S(1)} %get-tuple-element.157.refs_4_.refs_1_, ...), custom_call_target="tpu_custom_call" | custom-call | flops 30000001024 | bytes 1048576 | tf_op jit(solution)/shard_map/early_kernel/pallas_call | solution.py:878
  78.1 2.0 copy-done.20
  80.1 4.6 %grad_kernel.6 = (f32[1216,512]{1,0:T(8,128)S(1)}, f32[8,128]{1,0:T(8,128)S(1)}) custom-call(s32[15]{0:T(128)S(1)} %stack.42.refs_0_, bf16[1216,1024]{1,0:T(8,128)(2,1)S(1)} %get-tuple-element.179.refs_1_.refs_2_, bf16[1216,1024]{1,0:T(8,128)(2,1)S(1)} %get-tuple-element.180.refs_2_.refs_3_, bf16[1024,1024]{1,0:T(8,128)(2,1)S(1)} %get-tuple-element.171.refs_3_.refs_0_, ...), custom_call_target="tpu_custom_call" | custom-call | flops 13799999488 | bytes 1048576 | tf_op jit(solution)/shard_map/grad_kernel/pallas_call | solution.py:878
  85.3 0.7 land_a_down_2.1
  85.9 1.8 collective-permute-start.7
  87.7 5.0 %grad_kernel.7 = (f32[1216,512]{1,0:T(8,128)S(1)}, f32[8,128]{1,0:T(8,128)S(1)}) custom-call(s32[15]{0:T(128)S(1)} %stack.42.refs_0_, bf16[1216,1024]{1,0:T(8,128)(2,1)S(1)} %get-tuple-element.179.refs_1_.refs_2_, bf16[1216,1024]{1,0:T(8,128)(2,1)S(1)} %get-tuple-element.180.refs_2_.refs_3_, bf16[1024,1024]{1,0:T(8,128)(2,1)S(1)} %get-tuple-element.171.refs_3_.refs_0_, ...), custom_call_target="tpu_custom_call" | custom-call | flops 13799999488 | bytes 1048576 | tf_op jit(solution)/shard_map/grad_kernel/pallas_call | solution.py:878
  92.8 0.9 land_c_down_1.1
  93.7 2.5 %collective-permute-done.7.refs_2_ = f32[304,512]{1,0:T(8,128)S(1)} collective-permute-done((f32[304,512]{1,0:T(8,128)S(1)}, f32[304,512]{1,0:T(8,128)S(1)}, u32[]{:S(2)}, u32[]{:S(2)}) %collective-permute-start.7) | collective-permute-done | bytes 622624 | tf_op jit(solution)/shard_map/sum_a_down_2/ppermute | solution.py:953
  96.9 2.1 collective-permute-start.9
  99.0 1.7 collective-permute-start.11
  100.7 6.2 %couple_kernel.1 = (bf16[128,1024]{1,0:T(8,128)(2,1)S(1)}, bf16[128,1024]{1,0:T(8,128)(2,1)S(1)}, f32[16,1024]{1,0:T(8,128)S(1)}, f32[576,128]{1,0:T(8,128)S(1)}, f32[8,128]{1,0:T(8,128)S(1)}) custom-call(bf16[1024,1024]{1,0:T(8,128)(2,1)S(1)} %get-tuple-element.171.refs_3_.refs_0_, bf16[1024,1024]{1,0:T(8,128)(2,1)S(1)} %get-tuple-element.172.refs_4_.refs_1_, ...), custom_call_target="tpu_custom_call" | custom-call | flops 18900000768 | bytes 1048576 | tf_op jit(solution)/shard_map/couple_kernel/pallas_call | solution.py:878
  107.5 1.7 collective-permute-start.10
  109.2 4.0 %weights_kernel.1 = (f32[192,1024]{1,0:T(8,128)S(1)}, f32[8,128]{1,0:T(8,128)S(1)}) custom-call(bf16[128,1024]{1,0:T(8,128)(2,1)S(1)} %get-tuple-element.191.refs_0_.refs_6_, bf16[128,1024]{1,0:T(8,128)(2,1)S(1)} %get-tuple-element.192.refs_1_.refs_7_, bf16[1216,1024]{1,0:T(8,128)(2,1)S(1)} %get-tuple-element.179.refs_1_.refs_2_, ...), custom_call_target="tpu_custom_call" | custom-call | flops 12000000000 | bytes 1048576 | tf_op jit(solution)/shard_map/weights_kernel/pallas_call | solution.py:878
  113.3 6.7 %pre_kernel.2 = (bf16[512,1024]{1,0:T(8,128)(2,1)S(1)}, bf16[512,1024]{1,0:T(8,128)(2,1)S(1)}, f32[8,1024]{1,0:T(8,128)S(1)}, f32[8,1024]{1,0:T(8,128)S(1)}, f32[8,128]{1,0:T(8,128)S(1)}) custom-call(bf16[1024,1024]{1,0:T(8,128)(2,1)S(1)} %get-tuple-element.171.refs_3_.refs_0_, bf16[1024,1024]{1,0:T(8,128)(2,1)S(1)} %get-tuple-element.172.refs_4_.refs_1_, ...), custom_call_target="tpu_custom_call" | custom-call | flops 20999999488 | bytes 1048576 | tf_op jit(solution)/shard_map/pre_kernel/pallas_call | solution.py:878
  120.0 0.7 land_c_down_2.1
  120.7 1.8 collective-permute-start.12
  123.1 6.9 %pre_kernel.3 = (bf16[512,1024]{1,0:T(8,128)(2,1)S(1)}, bf16[512,1024]{1,0:T(8,128)(2,1)S(1)}, f32[8,1024]{1,0:T(8,128)S(1)}, f32[8,1024]{1,0:T(8,128)S(1)}, f32[8,128]{1,0:T(8,128)S(1)}) custom-call(bf16[1024,1024]{1,0:T(8,128)(2,1)S(1)} %get-tuple-element.171.refs_3_.refs_0_, bf16[1024,1024]{1,0:T(8,128)(2,1)S(1)} %get-tuple-element.172.refs_4_.refs_1_, ...), custom_call_target="tpu_custom_call" | custom-call | flops 20999999488 | bytes 1048576 | tf_op jit(solution)/shard_map/pre_kernel/pallas_call | solution.py:878
  129.9 1.1 collective-permute-done.12.refs_2_
  131.9 2.9 %last_kernel.1 = (f32[344,512]{1,0:T(8,128)S(1)}, f32[344,512]{1,0:T(8,128)S(1)}, f32[8,128]{1,0:T(8,128)S(1)}, f32[8,128]{1,0:T(8,128)S(1)}) custom-call(s32[15]{0:T(128)S(1)} %stack.42.refs_0_, bf16[512,1024]{1,0:T(8,128)(2,1)S(1)} %get-tuple-element.200.refs_1_, bf16[512,1024]{1,0:T(8,128)(2,1)S(1)} %get-tuple-element.201.refs_2_, ...), custom_call_target="tpu_custom_call" | custom-call | flops 15000000512 | bytes 1048576 | tf_op jit(solution)/shard_map/last_kernel/pallas_call | solution.py:878
  134.9 7.0 %collective-permute-done.14.refs_2_ = f32[152,512]{1,0:T(8,128)S(1)} collective-permute-done((f32[152,512]{1,0:T(8,128)S(1)}, f32[152,512]{1,0:T(8,128)S(1)}, u32[]{:S(2)}, u32[]{:S(2)}) %collective-permute-start.14) | collective-permute-done | bytes 311328 | tf_op jit(solution)/shard_map/sum_c_down_3/ppermute | solution.py:953
  142.6 2.8 %collective-permute-start.28 = (f32[152,256]{1,0:T(8,128)S(1)}, f32[152,256]{1,0:T(8,128)S(1)}, u32[]{:S(2)}, u32[]{:S(2)}) collective-permute-start(f32[152,256]{1,0:T(8,128)S(1)} %get-tuple-element.245.refs_1_), channel_id=1, source_target_pairs={{0,4},{1,3},{2,6},{3,1},{4,0},{5,7},{6,2},{7,5},{8,12},{9,11},{10,... | collective-permute-start | bytes 466952 | tf_op jit(solution)/shard_map/sum_a_up_4/ppermute | solution.py:953
  145.4 5.6 %collective-permute-done.22.refs_2_ = f32[152,256]{1,0:T(8,128)S(1)} collective-permute-done((f32[152,256]{1,0:T(8,128)S(1)}, f32[152,256]{1,0:T(8,128)S(1)}, u32[]{:S(2)}, u32[]{:S(2)}) %collective-permute-start.22) | collective-permute-done | bytes 155680 | tf_op jit(solution)/shard_map/sum_c_down_4/ppermute | solution.py:953
  151.7 0.6 land_s_down_1.1
  152.7 1.1 land_a_up_4.1
  153.9 10.7 %collective-permute-done.23.refs_2_ = f32[152,256]{1,0:T(8,128)S(1)} collective-permute-done((f32[152,256]{1,0:T(8,128)S(1)}, f32[152,256]{1,0:T(8,128)S(1)}, u32[]{:S(2)}, u32[]{:S(2)}) %collective-permute-start.23) | collective-permute-done | bytes 155680 | tf_op jit(solution)/shard_map/sum_c_up_4/ppermute | solution.py:953
  165.2 1.8 collective-permute-start.15
  167.9 8.2 %collective-permute-done.15.refs_2_ = f32[344,256]{1,0:T(8,128)S(1)} collective-permute-done((f32[344,256]{1,0:T(8,128)S(1)}, f32[344,256]{1,0:T(8,128)S(1)}, u32[]{:S(2)}, u32[]{:S(2)}) %collective-permute-start.15) | collective-permute-done | bytes 352288 | tf_op jit(solution)/shard_map/sum_s_down_1/ppermute | solution.py:953
  176.7 1.8 collective-permute-start.16
  179.4 2.8 %collective-permute-done.16.refs_2_ = f32[344,128]{1,0:T(8,128)S(1)} collective-permute-done((f32[344,128]{1,0:T(8,128)S(1)}, f32[344,128]{1,0:T(8,128)S(1)}, u32[]{:S(2)}, u32[]{:S(2)}) %collective-permute-start.16) | collective-permute-done | bytes 176160 | tf_op jit(solution)/shard_map/sum_s_down_2/ppermute | solution.py:953
  182.8 2.4 %collective-permute-start.17 = (f32[344,128]{1,0:T(8,128)S(1)}, f32[344,128]{1,0:T(8,128)S(1)}, u32[]{:S(2)}, u32[]{:S(2)}) collective-permute-start(f32[344,128]{1,0:T(8,128)S(1)} %land_s_down_3.1.refs_1_), channel_id=1, source_target_pairs={{0,2},{1,5},{2,0},{3,7},{4,6},{5,1},{6,4},{7,3},{8,10},{9,13},{10,... | collective-permute-start | bytes 528392 | tf_op jit(solution)/shard_map/sum_s_down_3/ppermute | solution.py:953
  185.1 0.6 land_a_up_2.1.refs_1_
  185.8 1.8 collective-permute-start.31
  187.6 1.7 collective-permute-done.17.refs_2_
  190.0 3.5 %collective-permute-done.25.refs_2_ = f32[304,512]{1,0:T(8,128)S(1)} collective-permute-done((f32[304,512]{1,0:T(8,128)S(1)}, f32[304,512]{1,0:T(8,128)S(1)}, u32[]{:S(2)}, u32[]{:S(2)}) %collective-permute-start.25) | collective-permute-done | bytes 622624 | tf_op jit(solution)/shard_map/sum_c_up_2/ppermute | solution.py:953
  194.1 0.8 collective-permute-start.26
  194.9 3.3 %collective-permute-done.18.refs_2_ = f32[344,128]{1,0:T(8,128)S(1)} collective-permute-done((f32[344,128]{1,0:T(8,128)S(1)}, f32[344,128]{1,0:T(8,128)S(1)}, u32[]{:S(2)}, u32[]{:S(2)}) %collective-permute-start.18) | collective-permute-done | bytes 176160 | tf_op jit(solution)/shard_map/sum_s_down_4/ppermute | solution.py:953
  198.8 1.8 collective-permute-start.19
  200.5 4.1 %collective-permute-done.31.refs_2_ = f32[608,512]{1,0:T(8,128)S(1)} collective-permute-done((f32[608,512]{1,0:T(8,128)S(1)}, f32[608,512]{1,0:T(8,128)S(1)}, u32[]{:S(2)}, u32[]{:S(2)}) %collective-permute-start.31) | collective-permute-done | bytes 1245216 | tf_op jit(solution)/shard_map/sum_a_up_1/ppermute | solution.py:953
  204.6 0.7 land_a_up_1.1.refs_1_
  205.4 0.8 collective-permute-done.19.refs_2_
  206.8 1.8 collective-permute-start.20
  208.6 13.1 %collective-permute-done.20.refs_2_ = f32[344,256]{1,0:T(8,128)S(1)} collective-permute-done((f32[344,256]{1,0:T(8,128)S(1)}, f32[344,256]{1,0:T(8,128)S(1)}, u32[]{:S(2)}, u32[]{:S(2)}) %collective-permute-start.20) | collective-permute-done | bytes 352288 | tf_op jit(solution)/shard_map/sum_s_up_1/ppermute | solution.py:953
  222.5 0.7 land_c_up_1.1.refs_1_
  223.7 0.9 collective-permute-done.21.refs_2_
  224.6 1.6 small_end_kernel.1
  226.2 2.8 %end_kernel.3.refs_2_ = f32[2,1216,1024]{2,1,0:T(8,128)} custom-call(s32[15]{0:T(128)S(1)} %stack.42.refs_0_, f32[1216,512]{1,0:T(8,128)S(1)} %land_a_up_1.1.refs_1_, f32[1216,512]{1,0:T(8,128)S(1)} %collective-permute-done.32.refs_2_), custom_call_target="tpu_custom_call" | custom-call | flops 8999999488 | bytes 1048576 | tf_op jit(solution)/shard_map/end_kernel/pallas_call | solution.py:878
  229.1 2.0 end_kernel.4.refs_2_
  231.1 2.0 end_kernel.5
  (118 shorter events, 14.4 us)
Async XLA Ops:
  2.0 1.3 collective-permute-start
  3.9 13.8 %copy-start.1 = (f32[2,1024,64]{1,2,0:T(8,128)S(1)}, f32[2,1024,64]{1,2,0:T(8,128)}, u32[]{:S(2)}) copy-start(f32[2,1024,64]{1,2,0:T(8,128)} %param.21) | copy-start | bytes 1572868
  3.9 13.8 %copy-start.2 = (f32[64,1024]{1,0:T(8,128)S(1)}, f32[64,1024]{1,0:T(8,128)}, u32[]{:S(2)}) copy-start(f32[64,1024]{1,0:T(8,128)} %refs_1_.1) | copy-start | bytes 786436
  3.9 13.8 %copy-start.3 = (f32[64,1024]{1,0:T(8,128)S(1)}, f32[64,1024]{1,0:T(8,128)}, u32[]{:S(2)}) copy-start(f32[64,1024]{1,0:T(8,128)} %refs_2_.1) | copy-start | bytes 786436
  3.9 13.8 %copy-start.4 = (f32[1024,64]{0,1:T(8,128)S(1)}, f32[1024,64]{0,1:T(8,128)}, u32[]{:S(2)}) copy-start(f32[1024,64]{0,1:T(8,128)} %param.20) | copy-start | bytes 786436
  3.9 13.8 %copy-start.5 = (f32[8,1024]{1,0:T(8,128)S(1)}, f32[8,1024]{1,0:T(8,128)}, u32[]{:S(2)}) copy-start(f32[8,1024]{1,0:T(8,128)} %refs_3_.1) | copy-start | bytes 98308
  3.9 13.8 %copy-start.6 = (s32[32,32]{1,0:T(8,128)S(1)}, s32[32,32]{1,0:T(8,128)}, u32[]{:S(2)}) copy-start(s32[32,32]{1,0:T(8,128)} %refs_6_.1) | copy-start | bytes 12292
  3.9 13.8 %copy-start.7 = (f32[9,64]{1,0:T(8,128)S(1)}, f32[9,64]{1,0:T(8,128)}, u32[]{:S(2)}) copy-start(f32[9,64]{1,0:T(8,128)} %refs_10_.1) | copy-start | bytes 6916
  3.9 13.8 %copy-start.8 = (f32[1024]{0:T(1024)S(1)}, f32[1024]{0:T(1024)}, u32[]{:S(2)}) copy-start(f32[1024]{0:T(1024)} %param.24) | copy-start | bytes 12292
  3.9 13.8 %copy-start.10 = (f32[3,32]{1,0:T(4,128)S(1)}, f32[3,32]{1,0:T(4,128)}, u32[]{:S(2)}) copy-start(f32[3,32]{1,0:T(4,128)} %refs_7_.1) | copy-start | bytes 1156
  4.0 13.8 %copy-start.12 = (s32[32]{0:T(128)S(1)}, s32[32]{0:T(128)}, u32[]{:S(2)}) copy-start(s32[32]{0:T(128)} %param.15) | copy-start | bytes 388
  4.0 13.8 %copy-start.13 = (f32[32]{0:T(128)S(1)}, f32[32]{0:T(128)}, u32[]{:S(2)}) copy-start(f32[32]{0:T(128)} %param.27) | copy-start | bytes 388
  4.0 13.8 %copy-start.14 = (f32[64]{0:T(128)S(1)}, f32[64]{0:T(128)}, u32[]{:S(2)}) copy-start(f32[64]{0:T(128)} %param.25) | copy-start | bytes 772
  4.0 13.8 %copy-start.15 = (f32[64]{0:T(128)S(1)}, f32[64]{0:T(128)}, u32[]{:S(2)}) copy-start(f32[64]{0:T(128)} %param.26) | copy-start | bytes 772
  4.0 6.6 %collective-permute-start.2 = (f32[8,128]{1,0:T(8,128)S(1)}, f32[8,128]{1,0:T(8,128)S(1)}, u32[]{:S(2)}, u32[]{:S(2)}) collective-permute-start(f32[8,128]{1,0:T(8,128)S(1)} %get-tuple-element.134.refs_1_), channel_id=1, source_target_pairs={{2,4},{4,2},{3,5},{5,3},{10,12},{12,10},{11,13},{13,11},{18,20},{2... | collective-permute-start | bytes 12296 | tf_op jit(solution)/shard_map/ppermute | solution.py:914
  4.8 7.4 %collective-permute-start.1 = (f32[8,128]{1,0:T(8,128)S(1)}, f32[8,128]{1,0:T(8,128)S(1)}, u32[]{:S(2)}, u32[]{:S(2)}) collective-permute-start(f32[8,128]{1,0:T(8,128)S(1)} %get-tuple-element.134.refs_1_), channel_id=1, source_target_pairs={{0,2},{2,0},{4,6},{6,4},{1,3},{3,1},{5,7},{7,5},{8,10},{10,8},{12,... | collective-permute-start | bytes 12296 | tf_op jit(solution)/shard_map/ppermute | solution.py:913
  12.7 11.6 %collective-permute-start.4 = (f32[8,384]{1,0:T(8,128)S(1)}, f32[8,384]{1,0:T(8,128)S(1)}, u32[]{:S(2)}, u32[]{:S(2)}) collective-permute-start(f32[8,384]{1,0:T(8,128)S(1)} %get-tuple-element.136.refs_1_), channel_id=1, source_target_pairs={{8,16},{16,8},{9,17},{17,9},{10,18},{18,10},{11,19},{19,11},{12,20... | collective-permute-start | bytes 36872 | tf_op jit(solution)/shard_map/ppermute | solution.py:914
  13.4 10.9 %collective-permute-start.3 = (f32[8,384]{1,0:T(8,128)S(1)}, f32[8,384]{1,0:T(8,128)S(1)}, u32[]{:S(2)}, u32[]{:S(2)}) collective-permute-start(f32[8,384]{1,0:T(8,128)S(1)} %get-tuple-element.136.refs_1_), channel_id=1, source_target_pairs={{0,8},{8,0},{16,24},{24,16},{1,9},{9,1},{17,25},{25,17},{2,10},{10... | collective-permute-start | bytes 36872 | tf_op jit(solution)/shard_map/ppermute | solution.py:913
  17.8 3.8 %copy-start = (f32[2,1216,1024]{2,1,0:T(8,128)S(1)}, f32[2,1216,1024]{2,1,0:T(8,128)}, u32[]{:S(2)}) copy-start(f32[2,1216,1024]{2,1,0:T(8,128)} %refs_0_.3) | copy-start | bytes 29884420
  24.2 19.0 %copy-start.16 = (bf16[1216,1024]{1,0:T(8,128)(2,1)}, bf16[1216,1024]{1,0:T(8,128)(2,1)S(1)}, u32[]{:S(2)}) copy-start(bf16[1216,1024]{1,0:T(8,128)(2,1)S(1)} %get-tuple-element.140.refs_6_.refs_2_) | copy-start | bytes 7471108
  24.2 19.0 %copy-start.18 = (bf16[1216,1024]{1,0:T(8,128)(2,1)}, bf16[1216,1024]{1,0:T(8,128)(2,1)S(1)}, u32[]{:S(2)}) copy-start(bf16[1216,1024]{1,0:T(8,128)(2,1)S(1)} %get-tuple-element.141.refs_7_.refs_3_) | copy-start | bytes 7471108
  24.2 19.0 %copy-start.22 = (bf16[288,1024]{1,0:T(8,128)(2,1)}, bf16[288,1024]{1,0:T(8,128)(2,1)S(1)}, u32[]{:S(2)}) copy-start(bf16[288,1024]{1,0:T(8,128)(2,1)S(1)} %get-tuple-element.142.refs_8_.refs_9_) | copy-start | bytes 1769476
  24.3 19.0 %copy-start.24 = (f32[576,128]{1,0:T(8,128)}, f32[576,128]{1,0:T(8,128)S(1)}, u32[]{:S(2)}) copy-start(f32[576,128]{1,0:T(8,128)S(1)} %get-tuple-element.147.refs_13_.refs_9_) | copy-start | bytes 884740
  24.3 19.0 %copy-start.26 = (bf16[128,1024]{1,0:T(8,128)(2,1)}, bf16[128,1024]{1,0:T(8,128)(2,1)S(1)}, u32[]{:S(2)}) copy-start(bf16[128,1024]{1,0:T(8,128)(2,1)S(1)} %get-tuple-element.143.refs_9_.refs_4_) | copy-start | bytes 786436
  24.3 19.0 %copy-start.28 = (bf16[128,1024]{1,0:T(8,128)(2,1)}, bf16[128,1024]{1,0:T(8,128)(2,1)S(1)}, u32[]{:S(2)}) copy-start(bf16[128,1024]{1,0:T(8,128)(2,1)S(1)} %get-tuple-element.144.refs_10_.refs_5_) | copy-start | bytes 786436
  24.3 19.0 %copy-start.30 = (f32[8,1024]{1,0:T(8,128)}, f32[8,1024]{1,0:T(8,128)S(1)}, u32[]{:S(2)}) copy-start(f32[8,1024]{1,0:T(8,128)S(1)} %get-tuple-element.139.refs_5_.refs_10_.refs_11_) | copy-start | bytes 98308
  24.3 19.0 %copy-start.32 = (s32[1,1024]{1,0:T(1,128)}, s32[1,1024]{1,0:T(1,128)S(1)}, u32[]{:S(2)}) copy-start(s32[1,1024]{1,0:T(1,128)S(1)} %get-tuple-element.138.refs_4_.refs_10_) | copy-start | bytes 12292
  59.2 7.6 %collective-permute-start.5 = (f32[1216,512]{1,0:T(8,128)S(1)}, f32[1216,512]{1,0:T(8,128)S(1)}, u32[]{:S(2)}, u32[]{:S(2)}) collective-permute-start(f32[1216,512]{1,0:T(8,128)S(1)} %get-tuple-element.168), channel_id=1, source_target_pairs={{0,1},{1,0},{2,3},{3,2},{4,5},{5,4},{6,7},{7,6},{8,9},{9,8},{10,11... | collective-permute-start | bytes 7471112 | tf_op jit(solution)/shard_map/sum_a_down_0/ppermute | solution.py:953
  67.6 17.7 %collective-permute-start.6 = (f32[608,512]{1,0:T(8,128)S(1)}, f32[608,512]{1,0:T(8,128)S(1)}, u32[]{:S(2)}, u32[]{:S(2)}) collective-permute-start(f32[608,512]{1,0:T(8,128)S(1)} %get-tuple-element.178), channel_id=1, source_target_pairs={{0,8},{1,17},{2,10},{3,19},{4,12},{5,21},{6,14},{7,23},{8,0},{9,25... | collective-permute-start | bytes 3735560 | tf_op jit(solution)/shard_map/sum_a_down_1/ppermute | solution.py:953
  78.1 2.0 copy-start.20
  84.7 8.1 %collective-permute-start.8 = (f32[1216,512]{1,0:T(8,128)S(1)}, f32[1216,512]{1,0:T(8,128)S(1)}, u32[]{:S(2)}, u32[]{:S(2)}) collective-permute-start(f32[1216,512]{1,0:T(8,128)S(1)} %get-tuple-element.187), channel_id=1, source_target_pairs={{0,1},{1,0},{2,3},{3,2},{4,5},{5,4},{6,7},{7,6},{8,9},{9,8},{10,11... | collective-permute-start | bytes 7471112 | tf_op jit(solution)/shard_map/sum_c_down_0/ppermute | solution.py:953
  85.9 10.3 %collective-permute-start.7 = (f32[304,512]{1,0:T(8,128)S(1)}, f32[304,512]{1,0:T(8,128)S(1)}, u32[]{:S(2)}, u32[]{:S(2)}) collective-permute-start(f32[304,512]{1,0:T(8,128)S(1)} %get-tuple-element.184), channel_id=1, source_target_pairs={{0,16},{1,9},{2,18},{3,11},{4,20},{5,13},{6,22},{7,15},{8,24},{9,1... | collective-permute-start | bytes 1867784 | tf_op jit(solution)/shard_map/sum_a_down_2/ppermute | solution.py:953
  96.2 4.4 %copy-start.17 = (bf16[1216,1024]{1,0:T(8,128)(2,1)S(1)}, bf16[1216,1024]{1,0:T(8,128)(2,1)}, u32[]{:S(2)}) copy-start(bf16[1216,1024]{1,0:T(8,128)(2,1)} %copy-done.16) | copy-start | bytes 7471108
  96.2 4.4 %copy-start.19 = (bf16[1216,1024]{1,0:T(8,128)(2,1)S(1)}, bf16[1216,1024]{1,0:T(8,128)(2,1)}, u32[]{:S(2)}) copy-start(bf16[1216,1024]{1,0:T(8,128)(2,1)} %copy-done.18) | copy-start | bytes 7471108
  96.3 4.4 %copy-start.25 = (f32[576,128]{1,0:T(8,128)S(1)}, f32[576,128]{1,0:T(8,128)}, u32[]{:S(2)}) copy-start(f32[576,128]{1,0:T(8,128)} %copy-done.24) | copy-start | bytes 884740
  96.9 10.0 %collective-permute-start.9 = (f32[152,512]{1,0:T(8,128)S(1)}, f32[152,512]{1,0:T(8,128)S(1)}, u32[]{:S(2)}, u32[]{:S(2)}) collective-permute-start(f32[152,512]{1,0:T(8,128)S(1)} %get-tuple-element.196), channel_id=1, source_target_pairs={{0,2},{1,5},{2,0},{3,7},{4,6},{5,1},{6,4},{7,3},{8,10},{9,13},{10,... | collective-permute-start | bytes 933896 | tf_op jit(solution)/shard_map/sum_a_down_3/ppermute | solution.py:953
  99.0 21.1 %collective-permute-start.11 = (f32[608,512]{1,0:T(8,128)S(1)}, f32[608,512]{1,0:T(8,128)S(1)}, u32[]{:S(2)}, u32[]{:S(2)}) collective-permute-start(f32[608,512]{1,0:T(8,128)S(1)} %get-tuple-element.205), channel_id=1, source_target_pairs={{0,8},{1,17},{2,10},{3,19},{4,12},{5,21},{6,14},{7,23},{8,0},{9,25... | collective-permute-start | bytes 3735560 | tf_op jit(solution)/shard_map/sum_c_down_1/ppermute | solution.py:953
  107.5 15.0 %collective-permute-start.10 = (f32[152,256]{1,0:T(8,128)S(1)}, f32[152,256]{1,0:T(8,128)S(1)}, u32[]{:S(2)}, u32[]{:S(2)}) collective-permute-start(f32[152,256]{1,0:T(8,128)S(1)} %get-tuple-element.203), channel_id=1, source_target_pairs={{0,4},{1,3},{2,6},{3,1},{4,0},{5,7},{6,2},{7,5},{8,12},{9,11},{10,... | collective-permute-start | bytes 466952 | tf_op jit(solution)/shard_map/sum_a_down_4/ppermute | solution.py:953
  109.2 4.1 %copy-start.21 = (f32[1024,1024]{1,0:T(8,128)S(1)}, f32[1024,1024]{1,0:T(8,128)}, u32[]{:S(2)}) copy-start(f32[1024,1024]{1,0:T(8,128)} %copy-done.20) | copy-start | bytes 12582916
  109.2 4.1 %copy-start.23 = (bf16[288,1024]{1,0:T(8,128)(2,1)S(1)}, bf16[288,1024]{1,0:T(8,128)(2,1)}, u32[]{:S(2)}) copy-start(bf16[288,1024]{1,0:T(8,128)(2,1)} %copy-done.22) | copy-start | bytes 1769476
  109.2 4.1 %copy-start.27 = (bf16[128,1024]{1,0:T(8,128)(2,1)S(1)}, bf16[128,1024]{1,0:T(8,128)(2,1)}, u32[]{:S(2)}) copy-start(bf16[128,1024]{1,0:T(8,128)(2,1)} %copy-done.26) | copy-start | bytes 786436
  109.2 4.1 %copy-start.29 = (bf16[128,1024]{1,0:T(8,128)(2,1)S(1)}, bf16[128,1024]{1,0:T(8,128)(2,1)}, u32[]{:S(2)}) copy-start(bf16[128,1024]{1,0:T(8,128)(2,1)} %copy-done.28) | copy-start | bytes 786436
  109.2 4.1 %copy-start.31 = (f32[8,1024]{1,0:T(8,128)S(1)}, f32[8,1024]{1,0:T(8,128)}, u32[]{:S(2)}) copy-start(f32[8,1024]{1,0:T(8,128)} %copy-done.30) | copy-start | bytes 98308
  120.7 10.3 %collective-permute-start.12 = (f32[304,512]{1,0:T(8,128)S(1)}, f32[304,512]{1,0:T(8,128)S(1)}, u32[]{:S(2)}, u32[]{:S(2)}) collective-permute-start(f32[304,512]{1,0:T(8,128)S(1)} %get-tuple-element.222), channel_id=1, source_target_pairs={{0,16},{1,9},{2,18},{3,11},{4,20},{5,13},{6,22},{7,15},{8,24},{9,1... | collective-permute-start | bytes 1867784 | tf_op jit(solution)/shard_map/sum_c_down_2/ppermute | solution.py:953
  131.6 10.2 %collective-permute-start.14 = (f32[152,512]{1,0:T(8,128)S(1)}, f32[152,512]{1,0:T(8,128)S(1)}, u32[]{:S(2)}, u32[]{:S(2)}) collective-permute-start(f32[152,512]{1,0:T(8,128)S(1)} %get-tuple-element.228), channel_id=1, source_target_pairs={{0,2},{1,5},{2,0},{3,7},{4,6},{5,1},{6,4},{7,3},{8,10},{9,13},{10,... | collective-permute-start | bytes 933896 | tf_op jit(solution)/shard_map/sum_c_down_3/ppermute | solution.py:953
  142.4 8.6 %collective-permute-start.22 = (f32[152,256]{1,0:T(8,128)S(1)}, f32[152,256]{1,0:T(8,128)S(1)}, u32[]{:S(2)}, u32[]{:S(2)}) collective-permute-start(f32[152,256]{1,0:T(8,128)S(1)} %get-tuple-element.244), channel_id=1, source_target_pairs={{0,4},{1,3},{2,6},{3,1},{4,0},{5,7},{6,2},{7,5},{8,12},{9,11},{10,... | collective-permute-start | bytes 466952 | tf_op jit(solution)/shard_map/sum_c_down_4/ppermute | solution.py:953
  142.5 9.2 %collective-permute-start.13 = (f32[344,512]{1,0:T(8,128)S(1)}, f32[344,512]{1,0:T(8,128)S(1)}, u32[]{:S(2)}, u32[]{:S(2)}) collective-permute-start(f32[344,512]{1,0:T(8,128)S(1)} %get-tuple-element.226), channel_id=1, source_target_pairs={{0,1},{1,0},{2,3},{3,2},{4,5},{5,4},{6,7},{7,6},{8,9},{9,8},{10,11... | collective-permute-start | bytes 2113544 | tf_op jit(solution)/shard_map/sum_s_down_0/ppermute | solution.py:953
  142.6 10.1 %collective-permute-start.28 = (f32[152,256]{1,0:T(8,128)S(1)}, f32[152,256]{1,0:T(8,128)S(1)}, u32[]{:S(2)}, u32[]{:S(2)}) collective-permute-start(f32[152,256]{1,0:T(8,128)S(1)} %get-tuple-element.245.refs_1_), channel_id=1, source_target_pairs={{0,4},{1,3},{2,6},{3,1},{4,0},{5,7},{6,2},{7,5},{8,12},{9,11},{10,... | collective-permute-start | bytes 466952 | tf_op jit(solution)/shard_map/sum_a_up_4/ppermute | solution.py:953
  151.6 12.9 %collective-permute-start.23 = (f32[152,256]{1,0:T(8,128)S(1)}, f32[152,256]{1,0:T(8,128)S(1)}, u32[]{:S(2)}, u32[]{:S(2)}) collective-permute-start(f32[152,256]{1,0:T(8,128)S(1)} %land_c_down_5.1.refs_1_), channel_id=1, source_target_pairs={{0,4},{1,3},{2,6},{3,1},{4,0},{5,7},{6,2},{7,5},{8,12},{9,11},{10,... | collective-permute-start | bytes 466952 | tf_op jit(solution)/shard_map/sum_c_up_4/ppermute | solution.py:953
  153.9 13.1 %collective-permute-start.29 = (f32[152,512]{1,0:T(8,128)S(1)}, f32[152,512]{1,0:T(8,128)S(1)}, u32[]{:S(2)}, u32[]{:S(2)}) collective-permute-start(f32[152,512]{1,0:T(8,128)S(1)} %get-tuple-element.247.refs_1_), channel_id=1, source_target_pairs={{0,2},{1,5},{2,0},{3,7},{4,6},{5,1},{6,4},{7,3},{8,10},{9,13},{10,... | collective-permute-start | bytes 933896 | tf_op jit(solution)/shard_map/sum_a_up_3/ppermute | solution.py:953
  165.1 13.4 %collective-permute-start.24 = (f32[152,512]{1,0:T(8,128)S(1)}, f32[152,512]{1,0:T(8,128)S(1)}, u32[]{:S(2)}, u32[]{:S(2)}) collective-permute-start(f32[152,512]{1,0:T(8,128)S(1)} %land_c_up_4.1.refs_1_), channel_id=1, source_target_pairs={{0,2},{1,5},{2,0},{3,7},{4,6},{5,1},{6,4},{7,3},{8,10},{9,13},{10,... | collective-permute-start | bytes 933896 | tf_op jit(solution)/shard_map/sum_c_up_3/ppermute | solution.py:953
  165.2 10.9 %collective-permute-start.15 = (f32[344,256]{1,0:T(8,128)S(1)}, f32[344,256]{1,0:T(8,128)S(1)}, u32[]{:S(2)}, u32[]{:S(2)}) collective-permute-start(f32[344,256]{1,0:T(8,128)S(1)} %get-tuple-element.232), channel_id=1, source_target_pairs={{0,8},{1,17},{2,10},{3,19},{4,12},{5,21},{6,14},{7,23},{8,0},{9,25... | collective-permute-start | bytes 1056776 | tf_op jit(solution)/shard_map/sum_s_down_1/ppermute | solution.py:953
  167.6 17.5 %collective-permute-start.30 = (f32[304,512]{1,0:T(8,128)S(1)}, f32[304,512]{1,0:T(8,128)S(1)}, u32[]{:S(2)}, u32[]{:S(2)}) collective-permute-start(f32[304,512]{1,0:T(8,128)S(1)} %land_a_up_3.1.refs_1_), channel_id=1, source_target_pairs={{0,16},{1,9},{2,18},{3,11},{4,20},{5,13},{6,22},{7,15},{8,24},{9,1... | collective-permute-start | bytes 1867784 | tf_op jit(solution)/shard_map/sum_a_up_2/ppermute | solution.py:953
  176.7 5.5 %collective-permute-start.16 = (f32[344,128]{1,0:T(8,128)S(1)}, f32[344,128]{1,0:T(8,128)S(1)}, u32[]{:S(2)}, u32[]{:S(2)}) collective-permute-start(f32[344,128]{1,0:T(8,128)S(1)} %get-tuple-element.234), channel_id=1, source_target_pairs={{0,16},{1,9},{2,18},{3,11},{4,20},{5,13},{6,22},{7,15},{8,24},{9,1... | collective-permute-start | bytes 528392 | tf_op jit(solution)/shard_map/sum_s_down_2/ppermute | solution.py:953
  179.1 14.4 %collective-permute-start.25 = (f32[304,512]{1,0:T(8,128)S(1)}, f32[304,512]{1,0:T(8,128)S(1)}, u32[]{:S(2)}, u32[]{:S(2)}) collective-permute-start(f32[304,512]{1,0:T(8,128)S(1)} %land_c_up_3.1.refs_1_), channel_id=1, source_target_pairs={{0,16},{1,9},{2,18},{3,11},{4,20},{5,13},{6,22},{7,15},{8,24},{9,1... | collective-permute-start | bytes 1867784 | tf_op jit(solution)/shard_map/sum_c_up_2/ppermute | solution.py:953
  182.8 6.5 %collective-permute-start.17 = (f32[344,128]{1,0:T(8,128)S(1)}, f32[344,128]{1,0:T(8,128)S(1)}, u32[]{:S(2)}, u32[]{:S(2)}) collective-permute-start(f32[344,128]{1,0:T(8,128)S(1)} %land_s_down_3.1.refs_1_), channel_id=1, source_target_pairs={{0,2},{1,5},{2,0},{3,7},{4,6},{5,1},{6,4},{7,3},{8,10},{9,13},{10,... | collective-permute-start | bytes 528392 | tf_op jit(solution)/shard_map/sum_s_down_3/ppermute | solution.py:953
  185.8 18.9 %collective-permute-start.31 = (f32[608,512]{1,0:T(8,128)S(1)}, f32[608,512]{1,0:T(8,128)S(1)}, u32[]{:S(2)}, u32[]{:S(2)}) collective-permute-start(f32[608,512]{1,0:T(8,128)S(1)} %land_a_up_2.1.refs_1_), channel_id=1, source_target_pairs={{0,8},{1,17},{2,10},{3,19},{4,12},{5,21},{6,14},{7,23},{8,0},{9,25... | collective-permute-start | bytes 3735560 | tf_op jit(solution)/shard_map/sum_a_up_1/ppermute | solution.py:953
  189.9 8.3 %collective-permute-start.18 = (f32[344,128]{1,0:T(8,128)S(1)}, f32[344,128]{1,0:T(8,128)S(1)}, u32[]{:S(2)}, u32[]{:S(2)}) collective-permute-start(f32[344,128]{1,0:T(8,128)S(1)} %land_s_down_4.1.refs_1_), channel_id=1, source_target_pairs={{0,4},{1,3},{2,6},{3,1},{4,0},{5,7},{6,2},{7,5},{8,12},{9,11},{10,... | collective-permute-start | bytes 528392 | tf_op jit(solution)/shard_map/sum_s_down_4/ppermute | solution.py:953
  194.1 28.4 %collective-permute-start.26 = (f32[608,512]{1,0:T(8,128)S(1)}, f32[608,512]{1,0:T(8,128)S(1)}, u32[]{:S(2)}, u32[]{:S(2)}) collective-permute-start(f32[608,512]{1,0:T(8,128)S(1)} %land_c_up_2.1.refs_1_), channel_id=1, source_target_pairs={{0,8},{1,17},{2,10},{3,19},{4,12},{5,21},{6,14},{7,23},{8,0},{9,25... | collective-permute-start | bytes 3735560 | tf_op jit(solution)/shard_map/sum_c_up_1/ppermute | solution.py:953
  198.8 7.5 %collective-permute-start.19 = (f32[344,128]{1,0:T(8,128)S(1)}, f32[344,128]{1,0:T(8,128)S(1)}, u32[]{:S(2)}, u32[]{:S(2)}) collective-permute-start(f32[344,128]{1,0:T(8,128)S(1)} %land_s_down_5.1.refs_1_), channel_id=1, source_target_pairs={{0,16},{1,9},{2,18},{3,11},{4,20},{5,13},{6,22},{7,15},{8,24},{9,1... | collective-permute-start | bytes 528392 | tf_op jit(solution)/shard_map/sum_s_up_2/ppermute | solution.py:953
  205.3 20.9 %collective-permute-start.32 = (f32[1216,512]{1,0:T(8,128)S(1)}, f32[1216,512]{1,0:T(8,128)S(1)}, u32[]{:S(2)}, u32[]{:S(2)}) collective-permute-start(f32[1216,512]{1,0:T(8,128)S(1)} %land_a_up_1.1.refs_1_), channel_id=1, source_target_pairs={{0,1},{1,0},{2,3},{3,2},{4,5},{5,4},{6,7},{7,6},{8,9},{9,8},{10,11... | collective-permute-start | bytes 7471112 | tf_op jit(solution)/shard_map/sum_a_up_0/ppermute | solution.py:953
  206.8 14.9 %collective-permute-start.20 = (f32[344,256]{1,0:T(8,128)S(1)}, f32[344,256]{1,0:T(8,128)S(1)}, u32[]{:S(2)}, u32[]{:S(2)}) collective-permute-start(f32[344,256]{1,0:T(8,128)S(1)} %land_s_up_2.1.refs_1_), channel_id=1, source_target_pairs={{0,8},{1,17},{2,10},{3,19},{4,12},{5,21},{6,14},{7,23},{8,0},{9,25... | collective-permute-start | bytes 1056776 | tf_op jit(solution)/shard_map/sum_s_up_1/ppermute | solution.py:953
  222.3 2.2 collective-permute-start.21
  223.2 7.9 %collective-permute-start.27 = (f32[1216,512]{1,0:T(8,128)S(1)}, f32[1216,512]{1,0:T(8,128)S(1)}, u32[]{:S(2)}, u32[]{:S(2)}) collective-permute-start(f32[1216,512]{1,0:T(8,128)S(1)} %land_c_up_1.1.refs_1_), channel_id=1, source_target_pairs={{0,1},{1,0},{2,3},{3,2},{4,5},{5,4},{6,7},{7,6},{8,9},{9,8},{10,11... | collective-permute-start | bytes 7471112 | tf_op jit(solution)/shard_map/sum_c_up_0/ppermute | solution.py:953
  (3 other events, 2.3 us)
where the time goes:
time: 237 us; the launch traced here: 233 us
  Pallas kernels  117 us (49%)
  waiting for transfers between devices  67.9 us (29%)
  starting transfers between devices  38.9 us (16%)
  local copies, waits for them, and re-layouts  7.41 us (3%)
    pallas_call x46, Pallas kernels, __call__(): pl.pallas_call(kernel, name=name or getattr(body, 'func', body).__name__,...  117 us
    ppermute x28, waiting for transfers between devices, swap(): return lax.ppermute(x, self.names, self.pairs[at])  65.6 us
    ppermute x28, starting transfers between devices, swap(): return lax.ppermute(x, self.names, self.pairs[at])  26.9 us
    ppermute x3, starting transfers between devices, neighbours_of(): lax.ppermute(even, axis, even_pairs(axis))  10.5 us
    unnamed x68, local copies, waits for them, and re-layouts  7.32 us
  transfers between devices with their start and end apart: 33, of which 17 were waited for; matrix products, arithmetic and copies ran while one was open for 0% of the time, Pallas kernels for 33%

commit v1 on v0

--- a/solution.py
+++ b/solution.py
@@ -1,5 +1,6 @@
 import functools
 import math
+import types
 
 import jax
 import jax.numpy as jnp
@@ -848,24 +849,43 @@
 HSPEC = pl.BlockSpec(memory_space=pltpu.HBM)
 
 
+PROGRAM = (
+    "late", "send_a", "keep_a", "mid", "a", "early", "send_c", "a", "keep_c", "c",
+    "couple", "a", "pre0", "a", "weights", "c", "a", "pre1", "a", "c",
+    "last", "c", "free", "a", "a", "a", "a", "end_a", "c", "s",
+    "c", "s", "c", "s", "s", "c", "c", "s", "s", "s",
+    "end_s", "c",
+)
+
+
+COST = {
+    "late": 6.5, "send_a": 4.6, "keep_a": 0.57, "mid": 3, "early": 5.0, "send_c": 4.6,
+    "keep_c": 4.6, "couple": 25.2, "weights": 4, "pre0": 3.5, "pre1": 3.5, "last": 5,
+    "land_a": 8, "land_c": 2, "land_s": 3.0,
+}
+
+
 class Order:
     def __init__(self):
         self.token = None
         self.free = False
+        self.extra = ()
 
     def __call__(
         self, body, outs, args, scratch=(), scalar=False, hbm=(), plain=False, alias=None, us=1,
-        limit=6, name=None,
+        limit=6, name=None, mark=False,
     ):
         specs = [HSPEC if n in hbm else VSPEC for n in range(len(args))]
         if scalar:
             specs[0] = SSPEC
         count, given = len(args), len(outs)
+        marked = mark or not self.free
         tokens = () if self.token is None or self.free else (self.token,)
+        tokens, self.extra = tokens + self.extra, ()
 
         def kernel(*refs):
             after = refs[count + len(tokens) :]
-            if self.free:
+            if not marked:
                 return body(*refs[:count], *after)
             after[given][...] = jnp.zeros((8, 128), F32)
             body(*refs[:count], *after[:given], *after[given + 1 :])
@@ -878,9 +898,9 @@
         got = pl.pallas_call(
             kernel,
             name=name or getattr(body, "func", body).__name__,
-            out_shape=shapes + ([] if self.free else [pltpu.VMEM((8, 128), F32)]),
+            out_shape=shapes + ([pltpu.VMEM((8, 128), F32)] if marked else []),
             in_specs=specs + [ASPEC] * len(tokens),
-            out_specs=[out_spec] * given + ([] if self.free else [VSPEC]),
+            out_specs=[out_spec] * given + ([VSPEC] if marked else []),
             scratch_shapes=list(scratch),
             input_output_aliases=alias or {},
             compiler_params=pltpu.CompilerParams(vmem_limit_bytes=limit << 20),
@@ -888,7 +908,7 @@
                 flops=int(us * 3e9), bytes_accessed=1 << 20, transcendentals=0
             ),
         )(*args, *tokens)
-        if self.free:
+        if not marked:
             return got
         self.token = got[-1]
         return got[:-1]
@@ -981,7 +1001,7 @@
             [(shape, F32) for shape in shapes],
             (self.place, *args),
             scalar=True,
-            us=2,
+            us=COST[f"land_{self.name}"],
             name=f"land_{self.name}_{'up' if self.rising else 'down'}_{self.at}",
         )
 
@@ -1041,10 +1061,10 @@
     place = jnp.stack(place + route.flags() + steep.flags()).astype(jnp.int32)
     spec_row = species.reshape(1, ATOMS)
 
-    (table,) = order(pack_kernel, [((8, 128), F32)], (positions, spec_row), us=0.3)
+    (table,) = order(pack_kernel, [((8, 128), F32)], (positions, spec_row), us=1)
     even, odd = neighbours_of("gz", table, table)
     (table,) = order(
-        join_z_kernel, [((8, 128), F32)], (place, table, even, odd), scalar=True, us=0.3
+        join_z_kernel, [((8, 128), F32)], (place, table, even, odd), scalar=True, us=1
     )
     even, odd = neighbours_of("gy", table, table)
     (table,) = order(
@@ -1052,7 +1072,7 @@
         [((8, 384), F32)],
         (place, table, even, odd),
         scalar=True,
-        us=0.3,
+        us=1,
     )
     even, odd = neighbours_of("gx", table, table)
 
@@ -1098,20 +1118,20 @@
 
     chains = {}
 
-    def grad(mine, xh, xl, qh, ql):
+    def grad(mine, cost, xh, xl, qh, ql):
         return order(
             functools.partial(grad_kernel, mine),
             [((WIDE, HALF), F32)],
             (place, xh, xl, qh, ql),
             scalar=True,
-            us=4.6,
+            us=cost,
         )[0]
 
     def send(name, *args):
-        chains[name] = Sum(name, order, place, route, grad(False, *args), (0, 0, 0, 1))
+        chains[name] = Sum(name, order, place, route, grad(False, COST[f"send_{name}"], *args), (0, 0, 0, 1))
 
     def keep(name, *args):
-        chains[name].keep = grad(True, *args)
+        chains[name].keep = grad(True, COST[f"keep_{name}"], *args)
 
     def late():
         return order(
@@ -1122,7 +1142,7 @@
             ],
             (x1h, x1l, w1h, w1l, columns, geo),
             [vm((LATENT, 128), F32), vm((LATENT, 256), F32), vm((LATENT, 256), F32)],
-            us=13,
+            us=COST["late"],
             limit=17,
         )
 
@@ -1130,9 +1150,9 @@
         return order(
             mid_kernel,
             [((192, EDGES), F32), ((64, EDGES), BF16), ((64, EDGES), BF16), ((16, EDGES), F32)],
-            (q1h, q1l, w1h, w1l, f1, g1, w1, geo),
+            (v.q1h, v.q1l, w1h, w1l, f1, g1, w1, geo),
             [vm((576, 128), F32)],
-            us=3,
+            us=COST["mid"],
         )
 
     def early():
@@ -1142,9 +1162,9 @@
                 ((LATENT, EDGES), F32), ((LATENT, EDGES), BF16), ((LATENT, EDGES), BF16),
                 ((8, EDGES), F32),
             ],
-            (q1h, q1l, w1h, w1l, evh, evl, dw1h, dw1l, columns, geo, z0),
+            (v.q1h, v.q1l, w1h, w1l, evh, evl, v.dw1h, v.dw1l, columns, geo, z0),
             [vm((LATENT, 256), F32), vm((LATENT, 256), F32)],
-            us=10,
+            us=COST["early"],
             limit=12,
         )
 
@@ -1155,73 +1175,63 @@
                 ((128, EDGES), BF16), ((128, EDGES), BF16), ((16, EDGES), F32),
                 ((576, 128), F32),
             ],
-            (q0h, q0l, w0h, w0l, vw, geo, g0, g1, ds1, path, dy1),
+            (v.q0h, v.q0l, w0h, w0l, vw, geo, g0, g1, v.ds1, path, v.dy1),
             [vm((192, EDGES), F32), vm((576, 128), F32), vm((16, EDGES), F32)],
-            us=6.3,
+            us=COST["couple"],
         )
 
     def before(h):
         return order(
             functools.partial(pre_kernel, h),
             [half, half, ((8, EDGES), F32), ((8, EDGES), F32)],
-            (q0h, q0l, w0h, w0l, veh, vel, dvwh, dvwl, dlat, hots, cent, geo, rad_w),
+            (v.q0h, v.q0l, w0h, w0l, veh, vel, v.dvwh, v.dvwl, v.dlat, hots, cent, geo, rad_w),
             [vm((HALF, 256), F32), vm((HALF, 256), F32), vm((HALF, 256), F32)],
-            us=7,
-        )
-
-    def land(names):
-        for name in names.split():
-            if not chains[name].over:
-                chains[name].land()
-
-    q1h, q1l, sl, dout = late()
-    send("a", x1h, x1l, q1h, q1l)
-    keep("a", x1h, x1l, q1h, q1l)
-    ds1, dw1h, dw1l, dy1 = mid()
-    land("a")
-    dlat, q0h, q0l, se = early()
-    send("c", x0h, x0l, q0h, q0l)
-    land("a")
-    keep("c", x0h, x0l, q0h, q0l)
-    land("c a")
-    dvwh, dvwl, dy, dpath = couple()
-    land("a")
-    (more,) = order(
-        weights_kernel, [((192, LATENT), F32)], (dvwh, dvwl, x0h, x0l, dw1h, dw1l, x1h, x1l), us=4
-    )
-    pres = [before(0)]
-    land("c a")
-    pres.append(before(1))
-    land("c")
-    atoms = ATOMS * math.prod(size for _, size in sizes)
-    height = 144 + 8 * (atoms // LATENT)
-    qps = [x for got in pres for x in got[0:2]]
-    small_keep, small_send, energy = order(
-        lambda place, *refs: last_kernel(
-            sizes[1][1], sizes[2][1], place, refs[0:4], refs[4:6], refs[6:8], *refs[8:]
-        ),
-        [((192 + height, HALF), F32), ((192 + height, HALF), F32), ((8, 128), F32)],
-        (place, *qps, *[got[2] for got in pres], *[got[3] for got in pres], geo, slots, cent, sl,
-         se, dy, dpath, columns, dout, more),
-        [vm((8, NTAB), F32), vm((height, LATENT), F32), vm((8, atoms), F32)],
-        scalar=True,
-        us=5,
-        name="last_kernel",
-    )
-    chains["s"] = s = Sum("s", order, place, route, small_send, (1, 1))
-    s.keep = small_keep
-    land("c s a")
-    order.free = True
-    land("s c a c s a s c s c s a s a")
-    a, c = chains["a"], chains["c"]
-    while not (a.over and s.over):
-        for chain in (a, s):
-            if not chain.over:
-                chain.land()
-
-    def finish(parts, arrays, done=()):
+            us=COST[f"pre{h}"],
+        )
+
+    def run_late():
+        v.q1h, v.q1l, v.sl, v.dout = late()
+
+    def run_mid():
+        v.ds1, v.dw1h, v.dw1l, v.dy1 = mid()
+
+    def run_early():
+        v.dlat, v.q0h, v.q0l, v.se = early()
+
+    def run_couple():
+        v.dvwh, v.dvwl, v.dy, v.dpath = couple()
+
+    def run_weights():
+        (v.more,) = order(
+            weights_kernel,
+            [((192, LATENT), F32)],
+            (v.dvwh, v.dvwl, x0h, x0l, v.dw1h, v.dw1l, x1h, x1l),
+            us=COST["weights"],
+        )
+
+    def run_last():
+        atoms = ATOMS * math.prod(size for _, size in sizes)
+        height = 144 + 8 * (atoms // LATENT)
+        (ah, al, side_a, drad_a), (bh, bl, side_b, drad_b) = v.pres
+        keep, send, v.energy = order(
+            lambda place, *refs: last_kernel(
+                sizes[1][1], sizes[2][1], place, refs[0:4], refs[4:6], refs[6:8], *refs[8:]
+            ),
+            [((192 + height, HALF), F32), ((192 + height, HALF), F32), ((8, 128), F32)],
+            (place, ah, al, bh, bl, side_a, side_b, drad_a, drad_b, geo, slots, cent, v.sl, v.se,
+             v.dy, v.dpath, columns, v.dout, v.more),
+            [vm((8, NTAB), F32), vm((height, LATENT), F32), vm((8, atoms), F32)],
+            scalar=True,
+            us=COST["last"],
+            name="last_kernel",
+        )
+        chains["s"] = Sum("s", order, place, route, send, (1, 1))
+        chains["s"].keep = keep
+
+    def finish(parts, arrays, mark=False):
         last = 1 + len(arrays)
-        return order(
+        done = () if v.d_latent is None else (v.d_latent,)
+        (v.d_latent,) = order(
             functools.partial(end_kernel, parts),
             [((2, WIDE, LATENT), F32)],
             (place, *arrays, *done),
@@ -1231,26 +1241,82 @@
             plain="hbm",
             alias={last: 0} if done else None,
             us=3,
-        )
-
-    d_latent = finish(((1, 0, True), (1, 0, False)), (a.send, a.got))
-    center, neigh, radial, value, env, path_grad, out, scale, shift, position_grad, energies = order(
-        functools.partial(small_end_kernel, 3),
-        [
-            ((NSPEC, LATENT), F32), ((NSPEC, LATENT), F32), ((NBESSEL, LATENT), F32),
-            ((CHANNELS, LATENT), F32), ((2, CHANNELS, LATENT), F32), ((9, CHANNELS), F32),
-            ((8, 128), F32), ((1, NSPEC), F32), ((1, NSPEC), F32), ((3, ATOMS), F32),
-            ((1, ATOMS), F32),
-        ],
-        (place, s.send, s.got, energy),
-        scalar=True,
-        plain=True,
-        us=2,
-    )
-    while not c.over:
-        c.land()
-    d_latent = finish(((0, 0, True),), (c.send,), tuple(d_latent))
-    (d_latent,) = finish(((0, 0, False),), (c.got,), tuple(d_latent))
+            mark=mark,
+        )
+
+    def finish_small():
+        s = chains["s"]
+        v.small = order(
+            functools.partial(small_end_kernel, 3),
+            [
+                ((NSPEC, LATENT), F32), ((NSPEC, LATENT), F32), ((NBESSEL, LATENT), F32),
+                ((CHANNELS, LATENT), F32), ((2, CHANNELS, LATENT), F32), ((9, CHANNELS), F32),
+                ((8, 128), F32), ((1, NSPEC), F32), ((1, NSPEC), F32), ((3, ATOMS), F32),
+                ((1, ATOMS), F32),
+            ],
+            (place, s.send, s.got, v.energy),
+            scalar=True,
+            plain=True,
+            us=2,
+        )
+
+    def land(name):
+        chain = chains[name]
+        if chain.over:
+            return
+        if name == "c" and chain.rising and chain.at == 1 and v.d_latent is not None:
+            order.extra = (order.token,)
+        chain.land()
+
+    def settle(name):
+        while not chains[name].over:
+            land(name)
+
+    def finish_a():
+        settle("a")
+        finish(((1, 0, True), (1, 0, False)), (chains["a"].send, chains["a"].got), mark=True)
+
+    def finish_s():
+        settle("s")
+        finish_small()
+
+    def set_free():
+        order.free = True
+
+    def set_bound():
+        order.free = False
+
+    v = types.SimpleNamespace(d_latent=None, pres=[])
+    steps = {
+        "late": run_late,
+        "mid": run_mid,
+        "early": run_early,
+        "couple": run_couple,
+        "weights": run_weights,
+        "pre0": lambda: v.pres.append(before(0)),
+        "pre1": lambda: v.pres.append(before(1)),
+        "last": run_last,
+        "send_a": lambda: send("a", x1h, x1l, v.q1h, v.q1l),
+        "keep_a": lambda: keep("a", x1h, x1l, v.q1h, v.q1l),
+        "send_c": lambda: send("c", x0h, x0l, v.q0h, v.q0l),
+        "keep_c": lambda: keep("c", x0h, x0l, v.q0h, v.q0l),
+        "a": lambda: land("a"),
+        "c": lambda: land("c"),
+        "s": lambda: land("s"),
+        "free": set_free,
+        "bind": set_bound,
+        "end_a": finish_a,
+        "end_s": finish_s,
+    }
+    for step in PROGRAM:
+        steps[step]()
+    settle("c")
+    c = chains["c"]
+    finish(((0, 0, True),), (c.send,))
+    finish(((0, 0, False),), (c.got,))
+    (center, neigh, radial, value, env, path_grad, out, scale, shift, position_grad,
+     energies) = v.small
+    d_latent = v.d_latent
     return (
         energies.reshape(ATOMS),
         position_grad,

time: 237 us -> 226 us (0.954)
  waiting for transfers between devices: 67.9 us -> 58.5 us
  local copies, waits for them, and re-layouts: 7.41 us -> 1.55 us
  starting transfers between devices: 38.9 us -> 42.5 us
    ppermute x28, waiting for transfers between devices: 65.6 us -> 56.2 us  [swap(): return lax.ppermute(x, self.names, self.pairs[at])]
    unnamed x68 -> x52, local copies, waits for them, and re-layouts: 7.32 us -> 1.46 us
    ppermute x28, starting transfers between devices: 26.9 us -> 30.2 us  [swap(): return lax.ppermute(x, self.names, self.pairs[at])]
  transfers between devices with their start and end apart: 33 -> 33, of which waited for: 17 -> 17; matrix products, arithmetic and copies ran while one was open for 0% -> 0% of each run, Pallas kernels for 33% -> 35%
where the time goes in v1:
time: 226 us; the launch traced here: 222 us
  Pallas kernels  118 us (52%)
  waiting for transfers between devices  58.5 us (26%)
  starting transfers between devices  42.5 us (19%)
    pallas_call x46, Pallas kernels, __call__(): pl.pallas_call(kernel, name=name or getattr(body, 'func', body).__name__,...  118 us
    ppermute x28, waiting for transfers between devices, swap(): return lax.ppermute(x, self.names, self.pairs[at])  56.2 us
    ppermute x28, starting transfers between devices, swap(): return lax.ppermute(x, self.names, self.pairs[at])  30.2 us
    ppermute x3, starting transfers between devices, neighbours_of(): lax.ppermute(even, axis, even_pairs(axis))  10.7 us
  transfers between devices with their start and end apart: 33, of which 17 were waited for; matrix products, arithmetic and copies ran while one was open for 0% of the time, Pallas kernels for 35%

profile of v1, /device:TPU:0, one launch (start us, length us, event | category | flops | bytes accessed | tf_op | source)
XLA Modules:
  0.0 221.8 jit_solution(2865642932022502459)
XLA Ops:
  0.7 0.7 copy-done.10
  2.5 0.7 collective-permute-done.refs_2_
  3.9 0.8 collective-permute-start.2
  4.7 5.9 %collective-permute-start.1 = (f32[8,128]{1,0:T(8,128)S(1)}, f32[8,128]{1,0:T(8,128)S(1)}, u32[]{:S(2)}, u32[]{:S(2)}) collective-permute-start(f32[8,128]{1,0:T(8,128)S(1)} %get-tuple-element.135.refs_1_), channel_id=1, source_target_pairs={{0,2},{2,0},{4,6},{6,4},{1,3},{3,1},{5,7},{7,5},{8,10},{10,8},{12,... | collective-permute-start | bytes 12296 | tf_op jit(solution)/shard_map/ppermute | solution.py:933
  10.6 1.6 collective-permute-done.1.refs_2_
  12.9 0.8 collective-permute-start.4
  13.7 4.3 %collective-permute-start.3 = (f32[8,384]{1,0:T(8,128)S(1)}, f32[8,384]{1,0:T(8,128)S(1)}, u32[]{:S(2)}, u32[]{:S(2)}) collective-permute-start(f32[8,384]{1,0:T(8,128)S(1)} %get-tuple-element.137.refs_1_), channel_id=1, source_target_pairs={{0,8},{8,0},{16,24},{24,16},{1,9},{9,1},{17,25},{25,17},{2,10},{10... | collective-permute-start | bytes 36872 | tf_op jit(solution)/shard_map/ppermute | solution.py:933
  18.1 2.6 %prep_kernel.1 = (bf16[1216,1024]{1,0:T(8,128)(2,1)S(1)}, bf16[1216,1024]{1,0:T(8,128)(2,1)S(1)}, bf16[1216,1024]{1,0:T(8,128)(2,1)S(1)}, bf16[1216,1024]{1,0:T(...) custom-call(f32[2,1216,1024]{2,1,0:T(8,128)S(1)} %bitcast.22, ...), custom_call_target="tpu_custom_call" | custom-call | flops 12000000000 | bytes 1048576 | tf_op jit(solution)/shard_map/prep_kernel/pallas_call | solution.py:898
  20.8 19.0 %fwd_kernel.1 = (bf16[1216,1024]{1,0:T(8,128)(2,1)S(1)}, bf16[1216,1024]{1,0:T(8,128)(2,1)S(1)}, bf16[1216,1024]{1,0:T(8,128)(2,1)S(1)}, bf16[1216,1024]{1,0:T(8...) custom-call(s32[15]{0:T(128)S(1)} %stack.42.refs_0_, ...), custom_call_target="tpu_custom_call" | custom-call | flops 65999998976 | bytes 1048576 | tf_op jit(solution)/shard_map/fwd_kernel/pallas_call | solution.py:898
  39.9 11.0 %late_kernel.1 = (bf16[1024,1024]{1,0:T(8,128)(2,1)S(1)}, bf16[1024,1024]{1,0:T(8,128)(2,1)S(1)}, f32[8,1024]{1,0:T(8,128)S(1)}, f32[8,1024]{1,0:T(8,128)S(1)}, f32[8,128]{1,0:T(8,128)S(1)}) custom-call(bf16[1216,1024]{1,0:T(8,128)(2,1)S(1)} %get-tuple-element.151.refs_0_.refs_1_.refs_6_, bf16[1216,1024]{1,0:T(8,128)(2,1)S(1)} %get-tuple-element.152.refs_1_.refs_2_.refs_7_, ...), custom_call_target="tpu_custom_call" | custom-call | flops 19499999232 | bytes 1048576 | tf_op jit(solution)/shard_map/late_kernel/pallas_call | solution.py:898
  50.8 4.8 %grad_kernel.4 = (f32[1216,512]{1,0:T(8,128)S(1)}, f32[8,128]{1,0:T(8,128)S(1)}) custom-call(s32[15]{0:T(128)S(1)} %stack.42.refs_0_, bf16[1216,1024]{1,0:T(8,128)(2,1)S(1)} %get-tuple-element.151.refs_0_.refs_1_.refs_6_, bf16[1216,1024]{1,0:T(8,128)(2,1)S(1)} %get-tuple-element.152.refs_1_.refs_2_.refs_7_, ...), custom_call_target="tpu_custom_call" | custom-call | flops 13799999488 | bytes 1048576 | tf_op jit(solution)/shard_map/grad_kernel/pallas_call | solution.py:898
  55.8 4.7 %grad_kernel.5 = (f32[1216,512]{1,0:T(8,128)S(1)}, f32[8,128]{1,0:T(8,128)S(1)}) custom-call(s32[15]{0:T(128)S(1)} %stack.42.refs_0_, bf16[1216,1024]{1,0:T(8,128)(2,1)S(1)} %get-tuple-element.151.refs_0_.refs_1_.refs_6_, bf16[1216,1024]{1,0:T(8,128)(2,1)S(1)} %get-tuple-element.152.refs_1_.refs_2_.refs_7_, ...), custom_call_target="tpu_custom_call" | custom-call | flops 1710000000 | bytes 1048576 | tf_op jit(solution)/shard_map/grad_kernel/pallas_call | solution.py:898
  60.4 2.9 %mid_kernel.1 = (f32[192,1024]{1,0:T(8,128)S(1)}, bf16[64,1024]{1,0:T(8,128)(2,1)S(1)}, bf16[64,1024]{1,0:T(8,128)(2,1)S(1)}, f32[16,1024]{1,0:T(8,128)S(1)}, f32[8,128]{1,0:T(8,128)S(1)}) custom-call(bf16[1024,1024]{1,0:T(8,128)(2,1)S(1)} %get-tuple-element.157.refs_3_.refs_0_, bf16[1024,1024]{1,0:T(8,128)(2,1)S(1)} %get-tuple-element.158.refs_4_.refs_1_, ...), custom_call_target="tpu_custom_call" | custom-call | flops 8999999488 | bytes 1048576 | tf_op jit(solution)/shard_map/mid_kernel/pallas_call | solution.py:898
  63.3 0.9 land_a_down_1.1
  64.2 0.9 collective-permute-start.6
  65.1 10.4 %early_kernel.1 = (f32[1024,1024]{1,0:T(8,128)S(1)}, bf16[1024,1024]{1,0:T(8,128)(2,1)S(1)}, bf16[1024,1024]{1,0:T(8,128)(2,1)S(1)}, f32[8,1024]{1,0:T(8,128)S(1)}, f32[8,128]{1,0:T(8,128)S(1)}) custom-call(bf16[1024,1024]{1,0:T(8,128)(2,1)S(1)} %get-tuple-element.157.refs_3_.refs_0_, bf16[1024,1024]{1,0:T(8,128)(2,1)S(1)} %get-tuple-element.158.refs_4_.refs_1_, ...), custom_call_target="tpu_custom_call" | custom-call | flops 15000000512 | bytes 1048576 | tf_op jit(solution)/shard_map/early_kernel/pallas_call | solution.py:898
  75.5 4.7 %grad_kernel.6 = (f32[1216,512]{1,0:T(8,128)S(1)}, f32[8,128]{1,0:T(8,128)S(1)}) custom-call(s32[15]{0:T(128)S(1)} %stack.42.refs_0_, bf16[1216,1024]{1,0:T(8,128)(2,1)S(1)} %get-tuple-element.178.refs_1_.refs_2_, bf16[1216,1024]{1,0:T(8,128)(2,1)S(1)} %copy-done.18, bf16[1024,1024]{1,0:T(8,128)(2,1)S(1)} %get-tuple-element.172.refs_3_.refs_0_, ...), custom_call_target="tpu_custom_call" | custom-call | flops 13799999488 | bytes 1048576 | tf_op jit(solution)/shard_map/grad_kernel/pallas_call | solution.py:898
  80.4 0.7 collective-permute-done.6.refs_2_
  81.1 0.7 land_a_down_2.1
  81.9 0.9 collective-permute-start.8
  82.8 5.1 %grad_kernel.7 = (f32[1216,512]{1,0:T(8,128)S(1)}, f32[8,128]{1,0:T(8,128)S(1)}) custom-call(s32[15]{0:T(128)S(1)} %stack.42.refs_0_, bf16[1216,1024]{1,0:T(8,128)(2,1)S(1)} %get-tuple-element.178.refs_1_.refs_2_, bf16[1216,1024]{1,0:T(8,128)(2,1)S(1)} %copy-done.18, bf16[1024,1024]{1,0:T(8,128)(2,1)S(1)} %get-tuple-element.172.refs_3_.refs_0_, ...), custom_call_target="tpu_custom_call" | custom-call | flops 13799999488 | bytes 1048576 | tf_op jit(solution)/shard_map/grad_kernel/pallas_call | solution.py:898
  87.8 0.8 land_c_down_1.1
  88.6 6.2 %couple_kernel.1 = (bf16[128,1024]{1,0:T(8,128)(2,1)S(1)}, bf16[128,1024]{1,0:T(8,128)(2,1)S(1)}, f32[16,1024]{1,0:T(8,128)S(1)}, f32[576,128]{1,0:T(8,128)S(1)}, f32[8,128]{1,0:T(8,128)S(1)}) custom-call(bf16[1024,1024]{1,0:T(8,128)(2,1)S(1)} %get-tuple-element.172.refs_3_.refs_0_, bf16[1024,1024]{1,0:T(8,128)(2,1)S(1)} %get-tuple-element.173.refs_4_.refs_1_, ...), custom_call_target="tpu_custom_call" | custom-call | flops 75600003072 | bytes 1048576 | tf_op jit(solution)/shard_map/couple_kernel/pallas_call | solution.py:898
  95.6 2.1 collective-permute-start.9
  97.6 1.2 collective-permute-start.11
  98.8 6.7 %pre_kernel.2 = (bf16[512,1024]{1,0:T(8,128)(2,1)S(1)}, bf16[512,1024]{1,0:T(8,128)(2,1)S(1)}, f32[8,1024]{1,0:T(8,128)S(1)}, f32[8,1024]{1,0:T(8,128)S(1)}, f32[8,128]{1,0:T(8,128)S(1)}) custom-call(bf16[1024,1024]{1,0:T(8,128)(2,1)S(1)} %get-tuple-element.172.refs_3_.refs_0_, bf16[1024,1024]{1,0:T(8,128)(2,1)S(1)} %get-tuple-element.173.refs_4_.refs_1_, ...), custom_call_target="tpu_custom_call" | custom-call | flops 10499999744 | bytes 1048576 | tf_op jit(solution)/shard_map/pre_kernel/pallas_call | solution.py:898
  106.1 2.0 collective-permute-start.10
  108.1 4.0 %weights_kernel.1 = (f32[192,1024]{1,0:T(8,128)S(1)}, f32[8,128]{1,0:T(8,128)S(1)}) custom-call(bf16[128,1024]{1,0:T(8,128)(2,1)S(1)} %get-tuple-element.189.refs_6_.refs_0_, bf16[128,1024]{1,0:T(8,128)(2,1)S(1)} %get-tuple-element.190.refs_7_.refs_1_, bf16[1216,1024]{1,0:T(8,128)(2,1)S(1)} %get-tuple-element.178.refs_1_.refs_2_, ...), custom_call_target="tpu_custom_call" | custom-call | flops 12000000000 | bytes 1048576 | tf_op jit(solution)/shard_map/weights_kernel/pallas_call | solution.py:898
  112.1 2.4 %collective-permute-done.11.refs_2_ = f32[608,512]{1,0:T(8,128)S(1)} collective-permute-done((f32[608,512]{1,0:T(8,128)S(1)}, f32[608,512]{1,0:T(8,128)S(1)}, u32[]{:S(2)}, u32[]{:S(2)}) %collective-permute-start.11) | collective-permute-done | bytes 1245216 | tf_op jit(solution)/shard_map/sum_c_down_1/ppermute | solution.py:973
  114.5 0.7 land_c_down_2.1
  115.9 6.9 %pre_kernel.3 = (bf16[512,1024]{1,0:T(8,128)(2,1)S(1)}, bf16[512,1024]{1,0:T(8,128)(2,1)S(1)}, f32[8,1024]{1,0:T(8,128)S(1)}, f32[8,1024]{1,0:T(8,128)S(1)}, f32[8,128]{1,0:T(8,128)S(1)}) custom-call(bf16[1024,1024]{1,0:T(8,128)(2,1)S(1)} %get-tuple-element.172.refs_3_.refs_0_, bf16[1024,1024]{1,0:T(8,128)(2,1)S(1)} %get-tuple-element.173.refs_4_.refs_1_, ...), custom_call_target="tpu_custom_call" | custom-call | flops 10499999744 | bytes 1048576 | tf_op jit(solution)/shard_map/pre_kernel/pallas_call | solution.py:898
  122.8 1.2 collective-permute-start.12
  124.6 2.0 collective-permute-start.28
  126.5 6.5 %collective-permute-done.12.refs_2_ = f32[304,512]{1,0:T(8,128)S(1)} collective-permute-done((f32[304,512]{1,0:T(8,128)S(1)}, f32[304,512]{1,0:T(8,128)S(1)}, u32[]{:S(2)}, u32[]{:S(2)}) %collective-permute-start.12) | collective-permute-done | bytes 622624 | tf_op jit(solution)/shard_map/sum_c_down_2/ppermute | solution.py:973
  133.7 2.0 collective-permute-start.22
  135.6 2.9 %last_kernel.1 = (f32[344,512]{1,0:T(8,128)S(1)}, f32[344,512]{1,0:T(8,128)S(1)}, f32[8,128]{1,0:T(8,128)S(1)}, f32[8,128]{1,0:T(8,128)S(1)}) custom-call(s32[15]{0:T(128)S(1)} %stack.42.refs_0_, bf16[512,1024]{1,0:T(8,128)(2,1)S(1)} %get-tuple-element.197.refs_1_, bf16[512,1024]{1,0:T(8,128)(2,1)S(1)} %get-tuple-element.198.refs_2_, ...), custom_call_target="tpu_custom_call" | custom-call | flops 15000000512 | bytes 1048576 | tf_op jit(solution)/shard_map/last_kernel/pallas_call | solution.py:898
  139.2 1.3 collective-permute-start.29
  140.5 2.4 %collective-permute-done.22.refs_2_ = f32[152,512]{1,0:T(8,128)S(1)} collective-permute-done((f32[152,512]{1,0:T(8,128)S(1)}, f32[152,512]{1,0:T(8,128)S(1)}, u32[]{:S(2)}, u32[]{:S(2)}) %collective-permute-start.22) | collective-permute-done | bytes 311328 | tf_op jit(solution)/shard_map/sum_c_down_3/ppermute | solution.py:973
  142.9 1.1 land_c_down_4.1
  144.0 0.7 collective-permute-start.23
  145.3 1.2 collective-permute-start.15
  146.5 5.3 %collective-permute-done.23.refs_2_ = f32[152,256]{1,0:T(8,128)S(1)} collective-permute-done((f32[152,256]{1,0:T(8,128)S(1)}, f32[152,256]{1,0:T(8,128)S(1)}, u32[]{:S(2)}, u32[]{:S(2)}) %collective-permute-start.23) | collective-permute-done | bytes 155680 | tf_op jit(solution)/shard_map/sum_c_down_4/ppermute | solution.py:973
  153.4 1.3 collective-permute-start.16
  155.3 0.9 collective-permute-start.30
  156.3 3.3 %collective-permute-done.16.refs_2_ = f32[344,128]{1,0:T(8,128)S(1)} collective-permute-done((f32[344,128]{1,0:T(8,128)S(1)}, f32[344,128]{1,0:T(8,128)S(1)}, u32[]{:S(2)}, u32[]{:S(2)}) %collective-permute-start.16) | collective-permute-done | bytes 176160 | tf_op jit(solution)/shard_map/sum_s_down_2/ppermute | solution.py:973
  160.2 3.3 %collective-permute-start.17 = (f32[344,128]{1,0:T(8,128)S(1)}, f32[344,128]{1,0:T(8,128)S(1)}, u32[]{:S(2)}, u32[]{:S(2)}) collective-permute-start(f32[344,128]{1,0:T(8,128)S(1)} %land_s_down_3.1.refs_1_), channel_id=1, source_target_pairs={{0,2},{1,5},{2,0},{3,7},{4,6},{5,1},{6,4},{7,3},{8,10},{9,13},{10,... | collective-permute-start | bytes 528392 | tf_op jit(solution)/shard_map/sum_s_down_3/ppermute | solution.py:973
  164.1 3.8 %collective-permute-done.17.refs_2_ = f32[344,128]{1,0:T(8,128)S(1)} collective-permute-done((f32[344,128]{1,0:T(8,128)S(1)}, f32[344,128]{1,0:T(8,128)S(1)}, u32[]{:S(2)}, u32[]{:S(2)}) %collective-permute-start.17) | collective-permute-done | bytes 176160 | tf_op jit(solution)/shard_map/sum_s_down_3/ppermute | solution.py:973
  168.5 3.5 %collective-permute-start.18 = (f32[344,128]{1,0:T(8,128)S(1)}, f32[344,128]{1,0:T(8,128)S(1)}, u32[]{:S(2)}, u32[]{:S(2)}) collective-permute-start(f32[344,128]{1,0:T(8,128)S(1)} %land_s_down_4.1.refs_1_), channel_id=1, source_target_pairs={{0,4},{1,3},{2,6},{3,1},{4,0},{5,7},{6,2},{7,5},{8,12},{9,11},{10,... | collective-permute-start | bytes 528392 | tf_op jit(solution)/shard_map/sum_s_down_4/ppermute | solution.py:973
  172.3 0.7 land_a_up_1.1.refs_1_
  173.2 5.3 %collective-permute-done.25.refs_2_ = f32[152,512]{1,0:T(8,128)S(1)} collective-permute-done((f32[152,512]{1,0:T(8,128)S(1)}, f32[152,512]{1,0:T(8,128)S(1)}, u32[]{:S(2)}, u32[]{:S(2)}) %collective-permute-start.25) | collective-permute-done | bytes 311328 | tf_op jit(solution)/shard_map/sum_c_up_3/ppermute | solution.py:973
  179.1 1.2 collective-permute-start.26
  180.8 1.0 collective-permute-start.19
  181.8 9.9 %collective-permute-done.26.refs_2_ = f32[304,512]{1,0:T(8,128)S(1)} collective-permute-done((f32[304,512]{1,0:T(8,128)S(1)}, f32[304,512]{1,0:T(8,128)S(1)}, u32[]{:S(2)}, u32[]{:S(2)}) %collective-permute-start.26) | collective-permute-done | bytes 622624 | tf_op jit(solution)/shard_map/sum_c_up_2/ppermute | solution.py:973
  192.4 1.4 collective-permute-start.27
  193.8 1.7 collective-permute-done.19.refs_2_
  196.1 1.4 collective-permute-start.20
  197.5 2.8 %end_kernel.3 = (f32[2,1216,1024]{2,1,0:T(8,128)}, f32[8,128]{1,0:T(8,128)S(1)}) custom-call(s32[15]{0:T(128)S(1)} %stack.42.refs_0_, f32[1216,512]{1,0:T(8,128)S(1)} %land_a_up_1.1.refs_1_, f32[1216,512]{1,0:T(8,128)S(1)} %collective-permute-done.31.refs_2_), custom_call_target="tpu_custom_call" | custom-call | flops 8999999488 | bytes 1048576 | tf_op jit(solution)/shard_map/end_kernel/pallas_call | solution.py:898
  200.3 9.0 %collective-permute-done.27.refs_2_ = f32[608,512]{1,0:T(8,128)S(1)} collective-permute-done((f32[608,512]{1,0:T(8,128)S(1)}, f32[608,512]{1,0:T(8,128)S(1)}, u32[]{:S(2)}, u32[]{:S(2)}) %collective-permute-start.27) | collective-permute-done | bytes 1245216 | tf_op jit(solution)/shard_map/sum_c_up_1/ppermute | solution.py:973
  209.3 0.7 land_c_up_1.1.refs_1_
  210.1 3.0 %collective-permute-done.20.refs_2_ = f32[344,256]{1,0:T(8,128)S(1)} collective-permute-done((f32[344,256]{1,0:T(8,128)S(1)}, f32[344,256]{1,0:T(8,128)S(1)}, u32[]{:S(2)}, u32[]{:S(2)}) %collective-permute-start.20) | collective-permute-done | bytes 352288 | tf_op jit(solution)/shard_map/sum_s_up_1/ppermute | solution.py:973
  213.8 2.2 collective-permute-done.21.refs_2_
  215.9 1.6 small_end_kernel.1
  217.6 2.0 end_kernel.4.refs_2_
  219.6 2.0 end_kernel.5
  (103 shorter events, 14.8 us)
Async XLA Ops:
  0.6 0.7 copy-start.10
  1.3 0.7 copy-start.12
  2.0 1.3 collective-permute-start
  3.3 14.7 %slice-start = ((s8[9961472]{0:T(1024)(128)(4,1)}), s8[4194304]{0:T(1024)(128)(4,1)S(1)}, s32[]{:S(2)}) async-start(s8[9961472]{0:T(1024)(128)(4,1)} %bitcast.21), calls=%async_computation | async-start | bytes 8388608
  3.3 14.7 %slice-start.1 = ((s8[9961472]{0:T(1024)(128)(4,1)}), s8[4194304]{0:T(1024)(128)(4,1)S(1)}, s32[]{:S(2)}) async-start(s8[9961472]{0:T(1024)(128)(4,1)} %bitcast.21), calls=%async_computation.1 | async-start | bytes 8388608
  3.9 6.7 %collective-permute-start.2 = (f32[8,128]{1,0:T(8,128)S(1)}, f32[8,128]{1,0:T(8,128)S(1)}, u32[]{:S(2)}, u32[]{:S(2)}) collective-permute-start(f32[8,128]{1,0:T(8,128)S(1)} %get-tuple-element.135.refs_1_), channel_id=1, source_target_pairs={{2,4},{4,2},{3,5},{5,3},{10,12},{12,10},{11,13},{13,11},{18,20},{2... | collective-permute-start | bytes 12296 | tf_op jit(solution)/shard_map/ppermute | solution.py:934
  4.7 7.5 %collective-permute-start.1 = (f32[8,128]{1,0:T(8,128)S(1)}, f32[8,128]{1,0:T(8,128)S(1)}, u32[]{:S(2)}, u32[]{:S(2)}) collective-permute-start(f32[8,128]{1,0:T(8,128)S(1)} %get-tuple-element.135.refs_1_), channel_id=1, source_target_pairs={{0,2},{2,0},{4,6},{6,4},{1,3},{3,1},{5,7},{7,5},{8,10},{10,8},{12,... | collective-permute-start | bytes 12296 | tf_op jit(solution)/shard_map/ppermute | solution.py:933
  12.2 5.8 %slice-start.2 = ((s8[9961472]{0:T(1024)(128)(4,1)}), s8[1572864]{0:T(1024)(128)(4,1)S(1)}, s32[]{:S(2)}) async-start(s8[9961472]{0:T(1024)(128)(4,1)} %bitcast.21), calls=%async_computation.2 | async-start | bytes 3145728
  12.2 5.8 %copy-start.2 = (f32[2,1024,64]{1,2,0:T(8,128)S(1)}, f32[2,1024,64]{1,2,0:T(8,128)}, u32[]{:S(2)}) copy-start(f32[2,1024,64]{1,2,0:T(8,128)} %param.21) | copy-start | bytes 1572868
  12.2 5.8 %copy-start.3 = (f32[64,1024]{1,0:T(8,128)S(1)}, f32[64,1024]{1,0:T(8,128)}, u32[]{:S(2)}) copy-start(f32[64,1024]{1,0:T(8,128)} %refs_1_.1) | copy-start | bytes 786436
  12.2 5.8 %copy-start.4 = (f32[64,1024]{1,0:T(8,128)S(1)}, f32[64,1024]{1,0:T(8,128)}, u32[]{:S(2)}) copy-start(f32[64,1024]{1,0:T(8,128)} %refs_2_.1) | copy-start | bytes 786436
  12.2 5.8 %copy-start.5 = (f32[1024,64]{0,1:T(8,128)S(1)}, f32[1024,64]{0,1:T(8,128)}, u32[]{:S(2)}) copy-start(f32[1024,64]{0,1:T(8,128)} %param.20) | copy-start | bytes 786436
  12.2 5.8 %copy-start.6 = (f32[8,1024]{1,0:T(8,128)S(1)}, f32[8,1024]{1,0:T(8,128)}, u32[]{:S(2)}) copy-start(f32[8,1024]{1,0:T(8,128)} %refs_3_.1) | copy-start | bytes 98308
  12.2 5.8 %copy-start.7 = (s32[32,32]{1,0:T(8,128)S(1)}, s32[32,32]{1,0:T(8,128)}, u32[]{:S(2)}) copy-start(s32[32,32]{1,0:T(8,128)} %refs_6_.1) | copy-start | bytes 12292
  12.2 5.8 %copy-start.8 = (f32[9,64]{1,0:T(8,128)S(1)}, f32[9,64]{1,0:T(8,128)}, u32[]{:S(2)}) copy-start(f32[9,64]{1,0:T(8,128)} %refs_10_.1) | copy-start | bytes 6916
  12.3 5.8 %copy-start.9 = (f32[1024]{0:T(1024)S(1)}, f32[1024]{0:T(1024)}, u32[]{:S(2)}) copy-start(f32[1024]{0:T(1024)} %param.24) | copy-start | bytes 12292
  12.3 5.8 %copy-start.11 = (f32[3,32]{1,0:T(4,128)S(1)}, f32[3,32]{1,0:T(4,128)}, u32[]{:S(2)}) copy-start(f32[3,32]{1,0:T(4,128)} %refs_7_.1) | copy-start | bytes 1156
  12.3 5.8 %copy-start.13 = (s32[32]{0:T(128)S(1)}, s32[32]{0:T(128)}, u32[]{:S(2)}) copy-start(s32[32]{0:T(128)} %param.15) | copy-start | bytes 388
  12.3 5.8 %copy-start.14 = (f32[32]{0:T(128)S(1)}, f32[32]{0:T(128)}, u32[]{:S(2)}) copy-start(f32[32]{0:T(128)} %param.27) | copy-start | bytes 388
  12.3 5.8 %copy-start.15 = (f32[64]{0:T(128)S(1)}, f32[64]{0:T(128)}, u32[]{:S(2)}) copy-start(f32[64]{0:T(128)} %param.25) | copy-start | bytes 772
  12.3 5.8 %copy-start.16 = (f32[64]{0:T(128)S(1)}, f32[64]{0:T(128)}, u32[]{:S(2)}) copy-start(f32[64]{0:T(128)} %param.26) | copy-start | bytes 772
  12.9 7.9 %collective-permute-start.4 = (f32[8,384]{1,0:T(8,128)S(1)}, f32[8,384]{1,0:T(8,128)S(1)}, u32[]{:S(2)}, u32[]{:S(2)}) collective-permute-start(f32[8,384]{1,0:T(8,128)S(1)} %get-tuple-element.137.refs_1_), channel_id=1, source_target_pairs={{8,16},{16,8},{9,17},{17,9},{10,18},{18,10},{11,19},{19,11},{12,20... | collective-permute-start | bytes 36872 | tf_op jit(solution)/shard_map/ppermute | solution.py:934
  13.7 7.1 %collective-permute-start.3 = (f32[8,384]{1,0:T(8,128)S(1)}, f32[8,384]{1,0:T(8,128)S(1)}, u32[]{:S(2)}, u32[]{:S(2)}) collective-permute-start(f32[8,384]{1,0:T(8,128)S(1)} %get-tuple-element.137.refs_1_), channel_id=1, source_target_pairs={{0,8},{8,0},{16,24},{24,16},{1,9},{9,1},{17,25},{25,17},{2,10},{10... | collective-permute-start | bytes 36872 | tf_op jit(solution)/shard_map/ppermute | solution.py:933
  20.7 19.1 %copy-start.19 = (bf16[128,1024]{1,0:T(8,128)(2,1)}, bf16[128,1024]{1,0:T(8,128)(2,1)S(1)}, u32[]{:S(2)}) copy-start(bf16[128,1024]{1,0:T(8,128)(2,1)S(1)} %get-tuple-element.144.refs_9_.refs_4_) | copy-start | bytes 786436
  20.8 19.1 %copy-start.21 = (s32[1,1024]{1,0:T(1,128)}, s32[1,1024]{1,0:T(1,128)S(1)}, u32[]{:S(2)}) copy-start(s32[1,1024]{1,0:T(1,128)S(1)} %get-tuple-element.139.refs_4_.refs_10_) | copy-start | bytes 12292
  39.8 11.0 %copy-start.17 = (bf16[1216,1024]{1,0:T(8,128)(2,1)}, bf16[1216,1024]{1,0:T(8,128)(2,1)S(1)}, u32[]{:S(2)}) copy-start(bf16[1216,1024]{1,0:T(8,128)(2,1)S(1)} %get-tuple-element.179.refs_2_.refs_3_) | copy-start | bytes 7471108
  39.8 15.9 %copy-start = (bf16[1216,1024]{1,0:T(8,128)(2,1)}, bf16[1216,1024]{1,0:T(8,128)(2,1)S(1)}, u32[]{:S(2)}) copy-start(bf16[1216,1024]{1,0:T(8,128)(2,1)S(1)} %get-tuple-element.152.refs_1_.refs_2_.refs_7_) | copy-start | bytes 7471108
  55.7 7.6 %collective-permute-start.5 = (f32[1216,512]{1,0:T(8,128)S(1)}, f32[1216,512]{1,0:T(8,128)S(1)}, u32[]{:S(2)}, u32[]{:S(2)}) collective-permute-start(f32[1216,512]{1,0:T(8,128)S(1)} %get-tuple-element.169), channel_id=1, source_target_pairs={{0,1},{1,0},{2,3},{3,2},{4,5},{5,4},{6,7},{7,6},{8,9},{9,8},{10,11... | collective-permute-start | bytes 7471112 | tf_op jit(solution)/shard_map/sum_a_down_0/ppermute | solution.py:973
  64.2 17.0 %collective-permute-start.6 = (f32[608,512]{1,0:T(8,128)S(1)}, f32[608,512]{1,0:T(8,128)S(1)}, u32[]{:S(2)}, u32[]{:S(2)}) collective-permute-start(f32[608,512]{1,0:T(8,128)S(1)} %get-tuple-element.181), channel_id=1, source_target_pairs={{0,8},{1,17},{2,10},{3,19},{4,12},{5,21},{6,14},{7,23},{8,0},{9,25... | collective-permute-start | bytes 3735560 | tf_op jit(solution)/shard_map/sum_a_down_1/ppermute | solution.py:973
  65.1 10.4 %copy-start.18 = (bf16[1216,1024]{1,0:T(8,128)(2,1)S(1)}, bf16[1216,1024]{1,0:T(8,128)(2,1)}, u32[]{:S(2)}) copy-start(bf16[1216,1024]{1,0:T(8,128)(2,1)} %copy-done.17) | copy-start | bytes 7471108
  80.2 7.6 %collective-permute-start.7 = (f32[1216,512]{1,0:T(8,128)S(1)}, f32[1216,512]{1,0:T(8,128)S(1)}, u32[]{:S(2)}, u32[]{:S(2)}) collective-permute-start(f32[1216,512]{1,0:T(8,128)S(1)} %get-tuple-element.186), channel_id=1, source_target_pairs={{0,1},{1,0},{2,3},{3,2},{4,5},{5,4},{6,7},{7,6},{8,9},{9,8},{10,11... | collective-permute-start | bytes 7471112 | tf_op jit(solution)/shard_map/sum_c_down_0/ppermute | solution.py:973
  81.9 13.0 %collective-permute-start.8 = (f32[304,512]{1,0:T(8,128)S(1)}, f32[304,512]{1,0:T(8,128)S(1)}, u32[]{:S(2)}, u32[]{:S(2)}) collective-permute-start(f32[304,512]{1,0:T(8,128)S(1)} %get-tuple-element.194), channel_id=1, source_target_pairs={{0,16},{1,9},{2,18},{3,11},{4,20},{5,13},{6,22},{7,15},{8,24},{9,1... | collective-permute-start | bytes 1867784 | tf_op jit(solution)/shard_map/sum_a_down_2/ppermute | solution.py:973
  94.9 3.9 %copy-start.20 = (bf16[128,1024]{1,0:T(8,128)(2,1)S(1)}, bf16[128,1024]{1,0:T(8,128)(2,1)}, u32[]{:S(2)}) copy-start(bf16[128,1024]{1,0:T(8,128)(2,1)} %copy-done.19) | copy-start | bytes 786436
  95.6 10.0 %collective-permute-start.9 = (f32[152,512]{1,0:T(8,128)S(1)}, f32[152,512]{1,0:T(8,128)S(1)}, u32[]{:S(2)}, u32[]{:S(2)}) collective-permute-start(f32[152,512]{1,0:T(8,128)S(1)} %get-tuple-element.200), channel_id=1, source_target_pairs={{0,2},{1,5},{2,0},{3,7},{4,6},{5,1},{6,4},{7,3},{8,10},{9,13},{10,... | collective-permute-start | bytes 933896 | tf_op jit(solution)/shard_map/sum_a_down_3/ppermute | solution.py:973
  97.6 16.9 %collective-permute-start.11 = (f32[608,512]{1,0:T(8,128)S(1)}, f32[608,512]{1,0:T(8,128)S(1)}, u32[]{:S(2)}, u32[]{:S(2)}) collective-permute-start(f32[608,512]{1,0:T(8,128)S(1)} %get-tuple-element.205), channel_id=1, source_target_pairs={{0,8},{1,17},{2,10},{3,19},{4,12},{5,21},{6,14},{7,23},{8,0},{9,25... | collective-permute-start | bytes 3735560 | tf_op jit(solution)/shard_map/sum_c_down_1/ppermute | solution.py:973
  105.5 2.6 %copy-start.1 = (bf16[1216,1024]{1,0:T(8,128)(2,1)S(1)}, bf16[1216,1024]{1,0:T(8,128)(2,1)}, u32[]{:S(2)}) copy-start(bf16[1216,1024]{1,0:T(8,128)(2,1)} %copy-done) | copy-start | bytes 7471108
  106.1 9.1 %collective-permute-start.10 = (f32[152,256]{1,0:T(8,128)S(1)}, f32[152,256]{1,0:T(8,128)S(1)}, u32[]{:S(2)}, u32[]{:S(2)}) collective-permute-start(f32[152,256]{1,0:T(8,128)S(1)} %get-tuple-element.203), channel_id=1, source_target_pairs={{0,4},{1,3},{2,6},{3,1},{4,0},{5,7},{6,2},{7,5},{8,12},{9,11},{10,... | collective-permute-start | bytes 466952 | tf_op jit(solution)/shard_map/sum_a_down_4/ppermute | solution.py:973
  115.8 8.2 %collective-permute-start.13 = (f32[152,256]{1,0:T(8,128)S(1)}, f32[152,256]{1,0:T(8,128)S(1)}, u32[]{:S(2)}, u32[]{:S(2)}) collective-permute-start(f32[152,256]{1,0:T(8,128)S(1)} %get-tuple-element.224.refs_1_), channel_id=1, source_target_pairs={{0,4},{1,3},{2,6},{3,1},{4,0},{5,7},{6,2},{7,5},{8,12},{9,11},{10,... | collective-permute-start | bytes 466952 | tf_op jit(solution)/shard_map/sum_a_up_4/ppermute | solution.py:973
  122.8 10.2 %collective-permute-start.12 = (f32[304,512]{1,0:T(8,128)S(1)}, f32[304,512]{1,0:T(8,128)S(1)}, u32[]{:S(2)}, u32[]{:S(2)}) collective-permute-start(f32[304,512]{1,0:T(8,128)S(1)} %get-tuple-element.223), channel_id=1, source_target_pairs={{0,16},{1,9},{2,18},{3,11},{4,20},{5,13},{6,22},{7,15},{8,24},{9,1... | collective-permute-start | bytes 1867784 | tf_op jit(solution)/shard_map/sum_c_down_2/ppermute | solution.py:973
  124.6 14.1 %collective-permute-start.28 = (f32[152,512]{1,0:T(8,128)S(1)}, f32[152,512]{1,0:T(8,128)S(1)}, u32[]{:S(2)}, u32[]{:S(2)}) collective-permute-start(f32[152,512]{1,0:T(8,128)S(1)} %get-tuple-element.247.refs_1_), channel_id=1, source_target_pairs={{0,2},{1,5},{2,0},{3,7},{4,6},{5,1},{6,4},{7,3},{8,10},{9,13},{10,... | collective-permute-start | bytes 933896 | tf_op jit(solution)/shard_map/sum_a_up_3/ppermute | solution.py:973
  133.0 2.6 %copy-start.22 = (s32[1,1024]{1,0:T(1,128)S(1)}, s32[1,1024]{1,0:T(1,128)}, u32[]{:S(2)}) copy-start(s32[1,1024]{1,0:T(1,128)} %copy-done.21) | copy-start | bytes 12292
  133.7 9.2 %collective-permute-start.22 = (f32[152,512]{1,0:T(8,128)S(1)}, f32[152,512]{1,0:T(8,128)S(1)}, u32[]{:S(2)}, u32[]{:S(2)}) collective-permute-start(f32[152,512]{1,0:T(8,128)S(1)} %get-tuple-element.243), channel_id=1, source_target_pairs={{0,2},{1,5},{2,0},{3,7},{4,6},{5,1},{6,4},{7,3},{8,10},{9,13},{10,... | collective-permute-start | bytes 933896 | tf_op jit(solution)/shard_map/sum_c_down_3/ppermute | solution.py:973
  138.6 6.1 %collective-permute-start.14 = (f32[344,512]{1,0:T(8,128)S(1)}, f32[344,512]{1,0:T(8,128)S(1)}, u32[]{:S(2)}, u32[]{:S(2)}) collective-permute-start(f32[344,512]{1,0:T(8,128)S(1)} %get-tuple-element.229), channel_id=1, source_target_pairs={{0,1},{1,0},{2,3},{3,2},{4,5},{5,4},{6,7},{7,6},{8,9},{9,8},{10,11... | collective-permute-start | bytes 2113544 | tf_op jit(solution)/shard_map/sum_s_down_0/ppermute | solution.py:973
  139.2 15.5 %collective-permute-start.29 = (f32[304,512]{1,0:T(8,128)S(1)}, f32[304,512]{1,0:T(8,128)S(1)}, u32[]{:S(2)}, u32[]{:S(2)}) collective-permute-start(f32[304,512]{1,0:T(8,128)S(1)} %land_a_up_3.1.refs_1_), channel_id=1, source_target_pairs={{0,16},{1,9},{2,18},{3,11},{4,20},{5,13},{6,22},{7,15},{8,24},{9,1... | collective-permute-start | bytes 1867784 | tf_op jit(solution)/shard_map/sum_a_up_2/ppermute | solution.py:973
  144.0 7.8 %collective-permute-start.23 = (f32[152,256]{1,0:T(8,128)S(1)}, f32[152,256]{1,0:T(8,128)S(1)}, u32[]{:S(2)}, u32[]{:S(2)}) collective-permute-start(f32[152,256]{1,0:T(8,128)S(1)} %get-tuple-element.246), channel_id=1, source_target_pairs={{0,4},{1,3},{2,6},{3,1},{4,0},{5,7},{6,2},{7,5},{8,12},{9,11},{10,... | collective-permute-start | bytes 466952 | tf_op jit(solution)/shard_map/sum_c_down_4/ppermute | solution.py:973
  145.3 7.5 %collective-permute-start.15 = (f32[344,256]{1,0:T(8,128)S(1)}, f32[344,256]{1,0:T(8,128)S(1)}, u32[]{:S(2)}, u32[]{:S(2)}) collective-permute-start(f32[344,256]{1,0:T(8,128)S(1)} %get-tuple-element.231), channel_id=1, source_target_pairs={{0,8},{1,17},{2,10},{3,19},{4,12},{5,21},{6,14},{7,23},{8,0},{9,25... | collective-permute-start | bytes 1056776 | tf_op jit(solution)/shard_map/sum_s_down_1/ppermute | solution.py:973
  152.4 11.1 %collective-permute-start.24 = (f32[152,256]{1,0:T(8,128)S(1)}, f32[152,256]{1,0:T(8,128)S(1)}, u32[]{:S(2)}, u32[]{:S(2)}) collective-permute-start(f32[152,256]{1,0:T(8,128)S(1)} %land_c_down_5.1.refs_1_), channel_id=1, source_target_pairs={{0,4},{1,3},{2,6},{3,1},{4,0},{5,7},{6,2},{7,5},{8,12},{9,11},{10,... | collective-permute-start | bytes 466952 | tf_op jit(solution)/shard_map/sum_c_up_4/ppermute | solution.py:973
  153.4 6.2 %collective-permute-start.16 = (f32[344,128]{1,0:T(8,128)S(1)}, f32[344,128]{1,0:T(8,128)S(1)}, u32[]{:S(2)}, u32[]{:S(2)}) collective-permute-start(f32[344,128]{1,0:T(8,128)S(1)} %get-tuple-element.233), channel_id=1, source_target_pairs={{0,16},{1,9},{2,18},{3,11},{4,20},{5,13},{6,22},{7,15},{8,24},{9,1... | collective-permute-start | bytes 528392 | tf_op jit(solution)/shard_map/sum_s_down_2/ppermute | solution.py:973
  155.3 17.0 %collective-permute-start.30 = (f32[608,512]{1,0:T(8,128)S(1)}, f32[608,512]{1,0:T(8,128)S(1)}, u32[]{:S(2)}, u32[]{:S(2)}) collective-permute-start(f32[608,512]{1,0:T(8,128)S(1)} %land_a_up_2.1.refs_1_), channel_id=1, source_target_pairs={{0,8},{1,17},{2,10},{3,19},{4,12},{5,21},{6,14},{7,23},{8,0},{9,25... | collective-permute-start | bytes 3735560 | tf_op jit(solution)/shard_map/sum_a_up_1/ppermute | solution.py:973
  160.2 7.7 %collective-permute-start.17 = (f32[344,128]{1,0:T(8,128)S(1)}, f32[344,128]{1,0:T(8,128)S(1)}, u32[]{:S(2)}, u32[]{:S(2)}) collective-permute-start(f32[344,128]{1,0:T(8,128)S(1)} %land_s_down_3.1.refs_1_), channel_id=1, source_target_pairs={{0,2},{1,5},{2,0},{3,7},{4,6},{5,1},{6,4},{7,3},{8,10},{9,13},{10,... | collective-permute-start | bytes 528392 | tf_op jit(solution)/shard_map/sum_s_down_3/ppermute | solution.py:973
  164.0 14.4 %collective-permute-start.25 = (f32[152,512]{1,0:T(8,128)S(1)}, f32[152,512]{1,0:T(8,128)S(1)}, u32[]{:S(2)}, u32[]{:S(2)}) collective-permute-start(f32[152,512]{1,0:T(8,128)S(1)} %land_c_up_4.1.refs_1_), channel_id=1, source_target_pairs={{0,2},{1,5},{2,0},{3,7},{4,6},{5,1},{6,4},{7,3},{8,10},{9,13},{10,... | collective-permute-start | bytes 933896 | tf_op jit(solution)/shard_map/sum_c_up_3/ppermute | solution.py:973
  168.5 11.8 %collective-permute-start.18 = (f32[344,128]{1,0:T(8,128)S(1)}, f32[344,128]{1,0:T(8,128)S(1)}, u32[]{:S(2)}, u32[]{:S(2)}) collective-permute-start(f32[344,128]{1,0:T(8,128)S(1)} %land_s_down_4.1.refs_1_), channel_id=1, source_target_pairs={{0,4},{1,3},{2,6},{3,1},{4,0},{5,7},{6,2},{7,5},{8,12},{9,11},{10,... | collective-permute-start | bytes 528392 | tf_op jit(solution)/shard_map/sum_s_down_4/ppermute | solution.py:973
  173.0 24.5 %collective-permute-start.31 = (f32[1216,512]{1,0:T(8,128)S(1)}, f32[1216,512]{1,0:T(8,128)S(1)}, u32[]{:S(2)}, u32[]{:S(2)}) collective-permute-start(f32[1216,512]{1,0:T(8,128)S(1)} %land_a_up_1.1.refs_1_), channel_id=1, source_target_pairs={{0,1},{1,0},{2,3},{3,2},{4,5},{5,4},{6,7},{7,6},{8,9},{9,8},{10,11... | collective-permute-start | bytes 7471112 | tf_op jit(solution)/shard_map/sum_a_up_0/ppermute | solution.py:973
  179.1 12.7 %collective-permute-start.26 = (f32[304,512]{1,0:T(8,128)S(1)}, f32[304,512]{1,0:T(8,128)S(1)}, u32[]{:S(2)}, u32[]{:S(2)}) collective-permute-start(f32[304,512]{1,0:T(8,128)S(1)} %land_c_up_3.1.refs_1_), channel_id=1, source_target_pairs={{0,16},{1,9},{2,18},{3,11},{4,20},{5,13},{6,22},{7,15},{8,24},{9,1... | collective-permute-start | bytes 1867784 | tf_op jit(solution)/shard_map/sum_c_up_2/ppermute | solution.py:973
  180.8 14.7 %collective-permute-start.19 = (f32[344,128]{1,0:T(8,128)S(1)}, f32[344,128]{1,0:T(8,128)S(1)}, u32[]{:S(2)}, u32[]{:S(2)}) collective-permute-start(f32[344,128]{1,0:T(8,128)S(1)} %land_s_down_5.1.refs_1_), channel_id=1, source_target_pairs={{0,16},{1,9},{2,18},{3,11},{4,20},{5,13},{6,22},{7,15},{8,24},{9,1... | collective-permute-start | bytes 528392 | tf_op jit(solution)/shard_map/sum_s_up_2/ppermute | solution.py:973
  192.4 17.0 %collective-permute-start.27 = (f32[608,512]{1,0:T(8,128)S(1)}, f32[608,512]{1,0:T(8,128)S(1)}, u32[]{:S(2)}, u32[]{:S(2)}) collective-permute-start(f32[608,512]{1,0:T(8,128)S(1)} %land_c_up_2.1.refs_1_), channel_id=1, source_target_pairs={{0,8},{1,17},{2,10},{3,19},{4,12},{5,21},{6,14},{7,23},{8,0},{9,25... | collective-permute-start | bytes 3735560 | tf_op jit(solution)/shard_map/sum_c_up_1/ppermute | solution.py:973
  196.1 17.0 %collective-permute-start.20 = (f32[344,256]{1,0:T(8,128)S(1)}, f32[344,256]{1,0:T(8,128)S(1)}, u32[]{:S(2)}, u32[]{:S(2)}) collective-permute-start(f32[344,256]{1,0:T(8,128)S(1)} %land_s_up_2.1.refs_1_), channel_id=1, source_target_pairs={{0,8},{1,17},{2,10},{3,19},{4,12},{5,21},{6,14},{7,23},{8,0},{9,25... | collective-permute-start | bytes 1056776 | tf_op jit(solution)/shard_map/sum_s_up_1/ppermute | solution.py:973
  210.0 9.5 %collective-permute-start.32 = (f32[1216,512]{1,0:T(8,128)S(1)}, f32[1216,512]{1,0:T(8,128)S(1)}, u32[]{:S(2)}, u32[]{:S(2)}) collective-permute-start(f32[1216,512]{1,0:T(8,128)S(1)} %land_c_up_1.1.refs_1_), channel_id=1, source_target_pairs={{0,1},{1,0},{2,3},{3,2},{4,5},{5,4},{6,7},{7,6},{8,9},{9,8},{10,11... | collective-permute-start | bytes 7471112 | tf_op jit(solution)/shard_map/sum_c_up_0/ppermute | solution.py:973
  213.7 2.2 %collective-permute-start.21 = (f32[344,512]{1,0:T(8,128)S(1)}, f32[344,512]{1,0:T(8,128)S(1)}, u32[]{:S(2)}, u32[]{:S(2)}) collective-permute-start(f32[344,512]{1,0:T(8,128)S(1)} %land_s_up_1.1.refs_1_), channel_id=1, source_target_pairs={{0,1},{1,0},{2,3},{3,2},{4,5},{5,4},{6,7},{7,6},{8,9},{9,8},{10,11... | collective-permute-start | bytes 2113544 | tf_op jit(solution)/shard_map/sum_s_up_0/ppermute | solution.py:973

commit v2 on v1

--- a/solution.py
+++ b/solution.py
@@ -851,10 +851,10 @@
 
 PROGRAM = (
     "late", "send_a", "keep_a", "mid", "a", "early", "send_c", "a", "keep_c", "c",
-    "couple", "a", "pre0", "a", "weights", "c", "a", "pre1", "a", "c",
-    "last", "c", "free", "a", "a", "a", "a", "end_a", "c", "s",
-    "c", "s", "c", "s", "s", "c", "c", "s", "s", "s",
-    "end_s", "c",
+    "a", "couple", "a", "pre0", "c", "a", "weights", "a", "pre1", "c",
+    "a", "last", "c", "free", "a", "a", "a", "a", "end_a", "c",
+    "s", "c", "s", "c", "s", "s", "c", "c", "s", "s",
+    "s", "end_s", "c",
 )
 
 
@@ -945,7 +945,7 @@
 
         flat, tall = bits("gx"), bits("gy") + bits("gz", 2)
         first = [("gz", 1)]
-        one, two = (flat, tall), (flat[::-1], tall[::-1])
+        one, two = (flat, tall), (flat[::-1], tall)
         if tall_first:
             one, two = one[::-1], two[::-1]
         self.steps = list(zip(first + one[0] + one[1], first + two[0] + two[1]))

time: 226 us -> 216 us (0.956)
  waiting for transfers between devices: 58.5 us -> 51.8 us
  starting transfers between devices: 42.5 us -> 37.7 us
    ppermute x28, waiting for transfers between devices: 56.2 us -> 49.5 us  [swap(): return lax.ppermute(x, self.names, self.pairs[at])]
    ppermute x28, starting transfers between devices: 30.2 us -> 25.4 us  [swap(): return lax.ppermute(x, self.names, self.pairs[at])]
  transfers between devices with their start and end apart: 33 -> 33, of which waited for: 17 -> 19; matrix products, arithmetic and copies ran while one was open for 0% -> 0% of each run, Pallas kernels for 35% -> 37%
where the time goes in v2:
time: 216 us; the launch traced here: 212 us
  Pallas kernels  118 us (55%)
  waiting for transfers between devices  51.8 us (24%)
  starting transfers between devices  37.7 us (17%)
  local copies, waits for them, and re-layouts  2.96 us (1%)
    pallas_call x46, Pallas kernels, __call__(): pl.pallas_call(kernel, name=name or getattr(body, 'func', body).__name__,...  118 us
    ppermute x28, waiting for transfers between devices, swap(): return lax.ppermute(x, self.names, self.pairs[at])  49.5 us
    ppermute x28, starting transfers between devices, swap(): return lax.ppermute(x, self.names, self.pairs[at])  25.4 us
    ppermute x3, starting transfers between devices, neighbours_of(): lax.ppermute(even, axis, even_pairs(axis))  10.7 us
  transfers between devices with their start and end apart: 33, of which 19 were waited for; matrix products, arithmetic and copies ran while one was open for 0% of the time, Pallas kernels for 37%

profile of v2, /device:TPU:0, one launch (start us, length us, event | category | flops | bytes accessed | tf_op | source)
XLA Modules:
  0.0 211.8 jit_solution(13953834533609959743)
XLA Ops:
  2.5 0.7 collective-permute-done.refs_2_
  3.9 0.8 collective-permute-start.2
  4.7 5.9 %collective-permute-start.1 = (f32[8,128]{1,0:T(8,128)S(1)}, f32[8,128]{1,0:T(8,128)S(1)}, u32[]{:S(2)}, u32[]{:S(2)}) collective-permute-start(f32[8,128]{1,0:T(8,128)S(1)} %get-tuple-element.137.refs_1_), channel_id=1, source_target_pairs={{0,2},{2,0},{4,6},{6,4},{1,3},{3,1},{5,7},{7,5},{8,10},{10,8},{12,... | collective-permute-start | bytes 12296 | tf_op jit(solution)/shard_map/ppermute | solution.py:933
  10.6 1.6 collective-permute-done.1.refs_2_
  12.9 0.8 collective-permute-start.4
  13.7 4.3 %collective-permute-start.3 = (f32[8,384]{1,0:T(8,128)S(1)}, f32[8,384]{1,0:T(8,128)S(1)}, u32[]{:S(2)}, u32[]{:S(2)}) collective-permute-start(f32[8,384]{1,0:T(8,128)S(1)} %get-tuple-element.139.refs_1_), channel_id=1, source_target_pairs={{0,8},{8,0},{16,24},{24,16},{1,9},{9,1},{17,25},{25,17},{2,10},{10... | collective-permute-start | bytes 36872 | tf_op jit(solution)/shard_map/ppermute | solution.py:933
  18.1 2.6 %prep_kernel.1 = (bf16[1216,1024]{1,0:T(8,128)(2,1)S(1)}, bf16[1216,1024]{1,0:T(8,128)(2,1)S(1)}, bf16[1216,1024]{1,0:T(8,128)(2,1)S(1)}, bf16[1216,1024]{1,0:T(...) custom-call(f32[2,1216,1024]{2,1,0:T(8,128)S(1)} %bitcast.21, ...), custom_call_target="tpu_custom_call" | custom-call | flops 12000000000 | bytes 1048576 | tf_op jit(solution)/shard_map/prep_kernel/pallas_call | solution.py:898
  20.8 18.9 %fwd_kernel.1 = (bf16[1216,1024]{1,0:T(8,128)(2,1)S(1)}, bf16[1216,1024]{1,0:T(8,128)(2,1)S(1)}, bf16[1216,1024]{1,0:T(8,128)(2,1)S(1)}, bf16[1216,1024]{1,0:T(8...) custom-call(s32[15]{0:T(128)S(1)} %stack.39.refs_0_, ...), custom_call_target="tpu_custom_call" | custom-call | flops 65999998976 | bytes 1048576 | tf_op jit(solution)/shard_map/fwd_kernel/pallas_call | solution.py:898
  39.8 0.7 copy-done.31
  40.5 10.9 %late_kernel.1 = (bf16[1024,1024]{1,0:T(8,128)(2,1)S(1)}, bf16[1024,1024]{1,0:T(8,128)(2,1)S(1)}, f32[8,1024]{1,0:T(8,128)S(1)}, f32[8,1024]{1,0:T(8,128)S(1)}, f32[8,128]{1,0:T(8,128)S(1)}) custom-call(bf16[1216,1024]{1,0:T(8,128)(2,1)S(1)} %get-tuple-element.153.refs_0_.refs_1_.refs_6_, bf16[1216,1024]{1,0:T(8,128)(2,1)S(1)} %get-tuple-element.154.refs_1_.refs_2_.refs_7_, ...), custom_call_target="tpu_custom_call" | custom-call | flops 19499999232 | bytes 1048576 | tf_op jit(solution)/shard_map/late_kernel/pallas_call | solution.py:898
  51.5 4.8 %grad_kernel.4 = (f32[1216,512]{1,0:T(8,128)S(1)}, f32[8,128]{1,0:T(8,128)S(1)}) custom-call(s32[15]{0:T(128)S(1)} %stack.39.refs_0_, bf16[1216,1024]{1,0:T(8,128)(2,1)S(1)} %get-tuple-element.153.refs_0_.refs_1_.refs_6_, bf16[1216,1024]{1,0:T(8,128)(2,1)S(1)} %get-tuple-element.154.refs_1_.refs_2_.refs_7_, ...), custom_call_target="tpu_custom_call" | custom-call | flops 13799999488 | bytes 1048576 | tf_op jit(solution)/shard_map/grad_kernel/pallas_call | solution.py:898
  56.4 4.7 %grad_kernel.5 = (f32[1216,512]{1,0:T(8,128)S(1)}, f32[8,128]{1,0:T(8,128)S(1)}) custom-call(s32[15]{0:T(128)S(1)} %stack.39.refs_0_, bf16[1216,1024]{1,0:T(8,128)(2,1)S(1)} %get-tuple-element.153.refs_0_.refs_1_.refs_6_, bf16[1216,1024]{1,0:T(8,128)(2,1)S(1)} %get-tuple-element.154.refs_1_.refs_2_.refs_7_, ...), custom_call_target="tpu_custom_call" | custom-call | flops 1710000000 | bytes 1048576 | tf_op jit(solution)/shard_map/grad_kernel/pallas_call | solution.py:898
  61.1 2.9 %mid_kernel.1 = (f32[192,1024]{1,0:T(8,128)S(1)}, bf16[64,1024]{1,0:T(8,128)(2,1)S(1)}, bf16[64,1024]{1,0:T(8,128)(2,1)S(1)}, f32[16,1024]{1,0:T(8,128)S(1)}, f32[8,128]{1,0:T(8,128)S(1)}) custom-call(bf16[1024,1024]{1,0:T(8,128)(2,1)S(1)} %get-tuple-element.159.refs_3_.refs_0_, bf16[1024,1024]{1,0:T(8,128)(2,1)S(1)} %get-tuple-element.160.refs_4_.refs_1_, ...), custom_call_target="tpu_custom_call" | custom-call | flops 8999999488 | bytes 1048576 | tf_op jit(solution)/shard_map/mid_kernel/pallas_call | solution.py:898
  64.0 0.9 land_a_down_1.1
  64.9 0.9 collective-permute-start.6
  65.8 10.4 %early_kernel.1 = (f32[1024,1024]{1,0:T(8,128)S(1)}, bf16[1024,1024]{1,0:T(8,128)(2,1)S(1)}, bf16[1024,1024]{1,0:T(8,128)(2,1)S(1)}, f32[8,1024]{1,0:T(8,128)S(1)}, f32[8,128]{1,0:T(8,128)S(1)}) custom-call(bf16[1024,1024]{1,0:T(8,128)(2,1)S(1)} %get-tuple-element.159.refs_3_.refs_0_, bf16[1024,1024]{1,0:T(8,128)(2,1)S(1)} %get-tuple-element.160.refs_4_.refs_1_, ...), custom_call_target="tpu_custom_call" | custom-call | flops 15000000512 | bytes 1048576 | tf_op jit(solution)/shard_map/early_kernel/pallas_call | solution.py:898
  76.2 4.7 %grad_kernel.6 = (f32[1216,512]{1,0:T(8,128)S(1)}, f32[8,128]{1,0:T(8,128)S(1)}) custom-call(s32[15]{0:T(128)S(1)} %stack.39.refs_0_, bf16[1216,1024]{1,0:T(8,128)(2,1)S(1)} %get-tuple-element.182.refs_1_.refs_2_, bf16[1216,1024]{1,0:T(8,128)(2,1)S(1)} %get-tuple-element.183.refs_2_.refs_3_, bf16[1024,1024]{1,0:T(8,128)(2,1)S(1)} %get-tuple-element.174.refs_3_.refs_0_, ...), custom_call_target="tpu_custom_call" | custom-call | flops 13799999488 | bytes 1048576 | tf_op jit(solution)/shard_map/grad_kernel/pallas_call | solution.py:898
  81.1 0.7 collective-permute-done.6.refs_2_
  81.8 0.7 land_a_down_2.1
  82.5 0.9 collective-permute-start.7
  83.4 5.1 %grad_kernel.7 = (f32[1216,512]{1,0:T(8,128)S(1)}, f32[8,128]{1,0:T(8,128)S(1)}) custom-call(s32[15]{0:T(128)S(1)} %stack.39.refs_0_, bf16[1216,1024]{1,0:T(8,128)(2,1)S(1)} %get-tuple-element.182.refs_1_.refs_2_, bf16[1216,1024]{1,0:T(8,128)(2,1)S(1)} %get-tuple-element.183.refs_2_.refs_3_, bf16[1024,1024]{1,0:T(8,128)(2,1)S(1)} %get-tuple-element.174.refs_3_.refs_0_, ...), custom_call_target="tpu_custom_call" | custom-call | flops 13799999488 | bytes 1048576 | tf_op jit(solution)/shard_map/grad_kernel/pallas_call | solution.py:898
  88.5 0.8 land_c_down_1.1
  89.3 3.5 %collective-permute-done.7.refs_2_ = f32[304,512]{1,0:T(8,128)S(1)} collective-permute-done((f32[304,512]{1,0:T(8,128)S(1)}, f32[304,512]{1,0:T(8,128)S(1)}, u32[]{:S(2)}, u32[]{:S(2)}) %collective-permute-start.7) | collective-permute-done | bytes 622624 | tf_op jit(solution)/shard_map/sum_a_down_2/ppermute | solution.py:973
  93.5 2.1 collective-permute-start.9
  95.6 0.8 collective-permute-start.11
  96.4 6.3 %couple_kernel.1 = (bf16[128,1024]{1,0:T(8,128)(2,1)S(1)}, bf16[128,1024]{1,0:T(8,128)(2,1)S(1)}, f32[16,1024]{1,0:T(8,128)S(1)}, f32[576,128]{1,0:T(8,128)S(1)}, f32[8,128]{1,0:T(8,128)S(1)}) custom-call(bf16[1024,1024]{1,0:T(8,128)(2,1)S(1)} %get-tuple-element.174.refs_3_.refs_0_, bf16[1024,1024]{1,0:T(8,128)(2,1)S(1)} %get-tuple-element.175.refs_4_.refs_1_, ...), custom_call_target="tpu_custom_call" | custom-call | flops 75600003072 | bytes 1048576 | tf_op jit(solution)/shard_map/couple_kernel/pallas_call | solution.py:898
  103.4 0.8 collective-permute-start.10
  104.2 6.7 %pre_kernel.2 = (bf16[512,1024]{1,0:T(8,128)(2,1)S(1)}, bf16[512,1024]{1,0:T(8,128)(2,1)S(1)}, f32[8,1024]{1,0:T(8,128)S(1)}, f32[8,1024]{1,0:T(8,128)S(1)}, f32[8,128]{1,0:T(8,128)S(1)}) custom-call(bf16[1024,1024]{1,0:T(8,128)(2,1)S(1)} %get-tuple-element.174.refs_3_.refs_0_, bf16[1024,1024]{1,0:T(8,128)(2,1)S(1)} %get-tuple-element.175.refs_4_.refs_1_, ...), custom_call_target="tpu_custom_call" | custom-call | flops 10499999744 | bytes 1048576 | tf_op jit(solution)/shard_map/pre_kernel/pallas_call | solution.py:898
  110.9 1.6 collective-permute-done.11.refs_2_
  113.8 0.7 collective-permute-start.12
  114.9 4.0 %weights_kernel.1 = (f32[192,1024]{1,0:T(8,128)S(1)}, f32[8,128]{1,0:T(8,128)S(1)}) custom-call(bf16[128,1024]{1,0:T(8,128)(2,1)S(1)} %get-tuple-element.194.refs_6_.refs_0_, bf16[128,1024]{1,0:T(8,128)(2,1)S(1)} %get-tuple-element.195.refs_7_.refs_1_, bf16[1216,1024]{1,0:T(8,128)(2,1)S(1)} %get-tuple-element.182.refs_1_.refs_2_, ...), custom_call_target="tpu_custom_call" | custom-call | flops 12000000000 | bytes 1048576 | tf_op jit(solution)/shard_map/weights_kernel/pallas_call | solution.py:898
  118.9 0.8 collective-permute-start.14
  119.8 1.7 collective-permute-done.12.refs_2_
  122.1 6.9 %pre_kernel.3 = (bf16[512,1024]{1,0:T(8,128)(2,1)S(1)}, bf16[512,1024]{1,0:T(8,128)(2,1)S(1)}, f32[8,1024]{1,0:T(8,128)S(1)}, f32[8,1024]{1,0:T(8,128)S(1)}, f32[8,128]{1,0:T(8,128)S(1)}) custom-call(bf16[1024,1024]{1,0:T(8,128)(2,1)S(1)} %get-tuple-element.174.refs_3_.refs_0_, bf16[1024,1024]{1,0:T(8,128)(2,1)S(1)} %get-tuple-element.175.refs_4_.refs_1_, ...), custom_call_target="tpu_custom_call" | custom-call | flops 10499999744 | bytes 1048576 | tf_op jit(solution)/shard_map/pre_kernel/pallas_call | solution.py:898
  129.9 1.9 collective-permute-start.23
  132.6 2.9 %last_kernel.1 = (f32[344,512]{1,0:T(8,128)S(1)}, f32[344,512]{1,0:T(8,128)S(1)}, f32[8,128]{1,0:T(8,128)S(1)}, f32[8,128]{1,0:T(8,128)S(1)}) custom-call(s32[15]{0:T(128)S(1)} %stack.39.refs_0_, bf16[512,1024]{1,0:T(8,128)(2,1)S(1)} %get-tuple-element.202.refs_1_, bf16[512,1024]{1,0:T(8,128)(2,1)S(1)} %get-tuple-element.203.refs_2_, ...), custom_call_target="tpu_custom_call" | custom-call | flops 15000000512 | bytes 1048576 | tf_op jit(solution)/shard_map/last_kernel/pallas_call | solution.py:898
  135.6 1.2 collective-permute-start.29
  136.8 0.8 collective-permute-done.23.refs_2_
  137.5 1.1 land_c_down_4.1
  138.7 2.8 %collective-permute-start.24 = (f32[152,256]{1,0:T(8,128)S(1)}, f32[152,256]{1,0:T(8,128)S(1)}, u32[]{:S(2)}, u32[]{:S(2)}) collective-permute-start(f32[152,256]{1,0:T(8,128)S(1)} %get-tuple-element.250), channel_id=1, source_target_pairs={{0,4},{1,5},{2,6},{3,7},{4,0},{5,1},{6,2},{7,3},{8,12},{9,13},{10,... | collective-permute-start | bytes 466952 | tf_op jit(solution)/shard_map/sum_c_down_4/ppermute | solution.py:973
  142.2 5.5 %collective-permute-done.24.refs_2_ = f32[152,256]{1,0:T(8,128)S(1)} collective-permute-done((f32[152,256]{1,0:T(8,128)S(1)}, f32[152,256]{1,0:T(8,128)S(1)}, u32[]{:S(2)}, u32[]{:S(2)}) %collective-permute-start.24) | collective-permute-done | bytes 155680 | tf_op jit(solution)/shard_map/sum_c_down_4/ppermute | solution.py:973
  148.3 1.2 collective-permute-done.16.refs_2_
  150.1 0.8 collective-permute-start.17
  151.5 1.6 collective-permute-start.30
  153.1 4.0 %collective-permute-done.17.refs_2_ = f32[344,128]{1,0:T(8,128)S(1)} collective-permute-done((f32[344,128]{1,0:T(8,128)S(1)}, f32[344,128]{1,0:T(8,128)S(1)}, u32[]{:S(2)}, u32[]{:S(2)}) %collective-permute-start.17) | collective-permute-done | bytes 176160 | tf_op jit(solution)/shard_map/sum_s_down_2/ppermute | solution.py:973
  157.7 1.8 collective-permute-start.18
  160.4 6.5 %collective-permute-done.18.refs_2_ = f32[344,128]{1,0:T(8,128)S(1)} collective-permute-done((f32[344,128]{1,0:T(8,128)S(1)}, f32[344,128]{1,0:T(8,128)S(1)}, u32[]{:S(2)}, u32[]{:S(2)}) %collective-permute-start.18) | collective-permute-done | bytes 176160 | tf_op jit(solution)/shard_map/sum_s_down_3/ppermute | solution.py:973
  167.8 0.7 collective-permute-done.30.refs_2_
  168.5 0.7 land_a_up_1.1.refs_1_
  169.9 0.9 collective-permute-done.26.refs_2_
  171.4 1.7 collective-permute-start.27
  173.1 2.1 %collective-permute-done.19.refs_2_ = f32[344,128]{1,0:T(8,128)S(1)} collective-permute-done((f32[344,128]{1,0:T(8,128)S(1)}, f32[344,128]{1,0:T(8,128)S(1)}, u32[]{:S(2)}, u32[]{:S(2)}) %collective-permute-start.19) | collective-permute-done | bytes 176160 | tf_op jit(solution)/shard_map/sum_s_down_4/ppermute | solution.py:973
  175.8 1.2 collective-permute-start.20
  177.0 4.8 %collective-permute-done.27.refs_2_ = f32[304,512]{1,0:T(8,128)S(1)} collective-permute-done((f32[304,512]{1,0:T(8,128)S(1)}, f32[304,512]{1,0:T(8,128)S(1)}, u32[]{:S(2)}, u32[]{:S(2)}) %collective-permute-start.27) | collective-permute-done | bytes 622624 | tf_op jit(solution)/shard_map/sum_c_up_2/ppermute | solution.py:973
  182.4 1.7 collective-permute-start.28
  184.7 1.8 collective-permute-start.21
  186.5 2.8 %end_kernel.3 = (f32[2,1216,1024]{2,1,0:T(8,128)}, f32[8,128]{1,0:T(8,128)S(1)}) custom-call(s32[15]{0:T(128)S(1)} %stack.39.refs_0_, f32[1216,512]{1,0:T(8,128)S(1)} %land_a_up_1.1.refs_1_, f32[1216,512]{1,0:T(8,128)S(1)} %collective-permute-done.31.refs_2_), custom_call_target="tpu_custom_call" | custom-call | flops 8999999488 | bytes 1048576 | tf_op jit(solution)/shard_map/end_kernel/pallas_call | solution.py:898
  189.3 10.0 %collective-permute-done.28.refs_2_ = f32[608,512]{1,0:T(8,128)S(1)} collective-permute-done((f32[608,512]{1,0:T(8,128)S(1)}, f32[608,512]{1,0:T(8,128)S(1)}, u32[]{:S(2)}, u32[]{:S(2)}) %collective-permute-start.28) | collective-permute-done | bytes 1245216 | tf_op jit(solution)/shard_map/sum_c_up_1/ppermute | solution.py:973
  199.3 0.7 land_c_up_1.1.refs_1_
  200.1 3.0 %collective-permute-done.21.refs_2_ = f32[344,256]{1,0:T(8,128)S(1)} collective-permute-done((f32[344,256]{1,0:T(8,128)S(1)}, f32[344,256]{1,0:T(8,128)S(1)}, u32[]{:S(2)}, u32[]{:S(2)}) %collective-permute-start.21) | collective-permute-done | bytes 352288 | tf_op jit(solution)/shard_map/sum_s_up_1/ppermute | solution.py:973
  203.8 2.2 %collective-permute-done.22.refs_2_ = f32[344,512]{1,0:T(8,128)S(1)} collective-permute-done((f32[344,512]{1,0:T(8,128)S(1)}, f32[344,512]{1,0:T(8,128)S(1)}, u32[]{:S(2)}, u32[]{:S(2)}) %collective-permute-start.22) | collective-permute-done | bytes 704544 | tf_op jit(solution)/shard_map/sum_s_up_0/ppermute | solution.py:973
  205.9 1.6 small_end_kernel.1
  207.6 2.0 end_kernel.4.refs_2_
  209.6 2.0 end_kernel.5
  (127 shorter events, 17.4 us)
Async XLA Ops:
  2.0 1.3 collective-permute-start
  3.3 14.7 %slice-start = ((s8[9961472]{0:T(1024)(128)(4,1)}), s8[4194304]{0:T(1024)(128)(4,1)S(1)}, s32[]{:S(2)}) async-start(s8[9961472]{0:T(1024)(128)(4,1)} %bitcast.20), calls=%async_computation | async-start | bytes 8388608
  3.3 14.7 %slice-start.1 = ((s8[9961472]{0:T(1024)(128)(4,1)}), s8[4194304]{0:T(1024)(128)(4,1)S(1)}, s32[]{:S(2)}) async-start(s8[9961472]{0:T(1024)(128)(4,1)} %bitcast.20), calls=%async_computation.1 | async-start | bytes 8388608
  3.9 6.7 %collective-permute-start.2 = (f32[8,128]{1,0:T(8,128)S(1)}, f32[8,128]{1,0:T(8,128)S(1)}, u32[]{:S(2)}, u32[]{:S(2)}) collective-permute-start(f32[8,128]{1,0:T(8,128)S(1)} %get-tuple-element.137.refs_1_), channel_id=1, source_target_pairs={{2,4},{4,2},{3,5},{5,3},{10,12},{12,10},{11,13},{13,11},{18,20},{2... | collective-permute-start | bytes 12296 | tf_op jit(solution)/shard_map/ppermute | solution.py:934
  4.7 7.5 %collective-permute-start.1 = (f32[8,128]{1,0:T(8,128)S(1)}, f32[8,128]{1,0:T(8,128)S(1)}, u32[]{:S(2)}, u32[]{:S(2)}) collective-permute-start(f32[8,128]{1,0:T(8,128)S(1)} %get-tuple-element.137.refs_1_), channel_id=1, source_target_pairs={{0,2},{2,0},{4,6},{6,4},{1,3},{3,1},{5,7},{7,5},{8,10},{10,8},{12,... | collective-permute-start | bytes 12296 | tf_op jit(solution)/shard_map/ppermute | solution.py:933
  12.2 5.8 %slice-start.2 = ((s8[9961472]{0:T(1024)(128)(4,1)}), s8[1572864]{0:T(1024)(128)(4,1)S(1)}, s32[]{:S(2)}) async-start(s8[9961472]{0:T(1024)(128)(4,1)} %bitcast.20), calls=%async_computation.2 | async-start | bytes 3145728
  12.2 5.8 %copy-start.2 = (f32[2,1024,64]{1,2,0:T(8,128)S(1)}, f32[2,1024,64]{1,2,0:T(8,128)}, u32[]{:S(2)}) copy-start(f32[2,1024,64]{1,2,0:T(8,128)} %param.21) | copy-start | bytes 1572868
  12.2 5.8 %copy-start.3 = (f32[64,1024]{1,0:T(8,128)S(1)}, f32[64,1024]{1,0:T(8,128)}, u32[]{:S(2)}) copy-start(f32[64,1024]{1,0:T(8,128)} %refs_1_.1) | copy-start | bytes 786436
  12.2 5.8 %copy-start.4 = (f32[64,1024]{1,0:T(8,128)S(1)}, f32[64,1024]{1,0:T(8,128)}, u32[]{:S(2)}) copy-start(f32[64,1024]{1,0:T(8,128)} %refs_2_.1) | copy-start | bytes 786436
  12.2 5.8 %copy-start.5 = (f32[1024,64]{0,1:T(8,128)S(1)}, f32[1024,64]{0,1:T(8,128)}, u32[]{:S(2)}) copy-start(f32[1024,64]{0,1:T(8,128)} %param.20) | copy-start | bytes 786436
  12.2 5.8 %copy-start.6 = (f32[8,1024]{1,0:T(8,128)S(1)}, f32[8,1024]{1,0:T(8,128)}, u32[]{:S(2)}) copy-start(f32[8,1024]{1,0:T(8,128)} %refs_3_.1) | copy-start | bytes 98308
  12.2 5.8 %copy-start.7 = (s32[32,32]{1,0:T(8,128)S(1)}, s32[32,32]{1,0:T(8,128)}, u32[]{:S(2)}) copy-start(s32[32,32]{1,0:T(8,128)} %refs_6_.1) | copy-start | bytes 12292
  12.2 5.8 %copy-start.8 = (f32[9,64]{1,0:T(8,128)S(1)}, f32[9,64]{1,0:T(8,128)}, u32[]{:S(2)}) copy-start(f32[9,64]{1,0:T(8,128)} %refs_10_.1) | copy-start | bytes 6916
  12.3 5.8 %copy-start.9 = (f32[1024]{0:T(1024)S(1)}, f32[1024]{0:T(1024)}, u32[]{:S(2)}) copy-start(f32[1024]{0:T(1024)} %param.24) | copy-start | bytes 12292
  12.3 5.8 %copy-start.11 = (f32[3,32]{1,0:T(4,128)S(1)}, f32[3,32]{1,0:T(4,128)}, u32[]{:S(2)}) copy-start(f32[3,32]{1,0:T(4,128)} %refs_7_.1) | copy-start | bytes 1156
  12.3 5.8 %copy-start.13 = (s32[32]{0:T(128)S(1)}, s32[32]{0:T(128)}, u32[]{:S(2)}) copy-start(s32[32]{0:T(128)} %param.15) | copy-start | bytes 388
  12.3 5.8 %copy-start.14 = (f32[32]{0:T(128)S(1)}, f32[32]{0:T(128)}, u32[]{:S(2)}) copy-start(f32[32]{0:T(128)} %param.27) | copy-start | bytes 388
  12.3 5.8 %copy-start.15 = (f32[64]{0:T(128)S(1)}, f32[64]{0:T(128)}, u32[]{:S(2)}) copy-start(f32[64]{0:T(128)} %param.25) | copy-start | bytes 772
  12.3 5.8 %copy-start.16 = (f32[64]{0:T(128)S(1)}, f32[64]{0:T(128)}, u32[]{:S(2)}) copy-start(f32[64]{0:T(128)} %param.26) | copy-start | bytes 772
  12.9 7.9 %collective-permute-start.4 = (f32[8,384]{1,0:T(8,128)S(1)}, f32[8,384]{1,0:T(8,128)S(1)}, u32[]{:S(2)}, u32[]{:S(2)}) collective-permute-start(f32[8,384]{1,0:T(8,128)S(1)} %get-tuple-element.139.refs_1_), channel_id=1, source_target_pairs={{8,16},{16,8},{9,17},{17,9},{10,18},{18,10},{11,19},{19,11},{12,20... | collective-permute-start | bytes 36872 | tf_op jit(solution)/shard_map/ppermute | solution.py:934
  13.7 7.1 %collective-permute-start.3 = (f32[8,384]{1,0:T(8,128)S(1)}, f32[8,384]{1,0:T(8,128)S(1)}, u32[]{:S(2)}, u32[]{:S(2)}) collective-permute-start(f32[8,384]{1,0:T(8,128)S(1)} %get-tuple-element.139.refs_1_), channel_id=1, source_target_pairs={{0,8},{8,0},{16,24},{24,16},{1,9},{9,1},{17,25},{25,17},{2,10},{10... | collective-permute-start | bytes 36872 | tf_op jit(solution)/shard_map/ppermute | solution.py:933
  20.7 19.0 %copy-start.17 = (bf16[1216,1024]{1,0:T(8,128)(2,1)}, bf16[1216,1024]{1,0:T(8,128)(2,1)S(1)}, u32[]{:S(2)}) copy-start(bf16[1216,1024]{1,0:T(8,128)(2,1)S(1)} %get-tuple-element.144.refs_7_.refs_3_) | copy-start | bytes 7471108
  20.8 19.0 %copy-start.19 = (bf16[128,1024]{1,0:T(8,128)(2,1)}, bf16[128,1024]{1,0:T(8,128)(2,1)S(1)}, u32[]{:S(2)}) copy-start(bf16[128,1024]{1,0:T(8,128)(2,1)S(1)} %get-tuple-element.146.refs_9_.refs_4_) | copy-start | bytes 786436
  20.8 19.0 %copy-start.23 = (f32[576,128]{1,0:T(8,128)}, f32[576,128]{1,0:T(8,128)S(1)}, u32[]{:S(2)}) copy-start(f32[576,128]{1,0:T(8,128)S(1)} %get-tuple-element.150.refs_13_.refs_9_) | copy-start | bytes 884740
  20.8 19.0 %copy-start.27 = (f32[8,1024]{1,0:T(8,128)}, f32[8,1024]{1,0:T(8,128)S(1)}, u32[]{:S(2)}) copy-start(f32[8,1024]{1,0:T(8,128)S(1)} %get-tuple-element.142.refs_5_.refs_10_.refs_11_) | copy-start | bytes 98308
  20.8 19.0 %copy-start.33 = (s32[1,1024]{1,0:T(1,128)}, s32[1,1024]{1,0:T(1,128)S(1)}, u32[]{:S(2)}) copy-start(s32[1,1024]{1,0:T(1,128)S(1)} %get-tuple-element.141.refs_4_.refs_10_) | copy-start | bytes 12292
  20.8 45.0 %copy-start.25 = (f32[128,128]{1,0:T(8,128)}, f32[128,128]{1,0:T(8,128)S(1)}, u32[]{:S(2)}) copy-start(f32[128,128]{1,0:T(8,128)S(1)} %get-tuple-element.151.refs_14_.refs_4_.refs_8_.refs_16_) | copy-start | bytes 196612
  40.5 11.0 %copy-start.29 = (f32[128,1024]{1,0:T(8,128)}, f32[128,1024]{1,0:T(8,128)S(1)}, u32[]{:S(2)}) copy-start(f32[128,1024]{1,0:T(8,128)S(1)} %get-tuple-element.176.refs_4_) | copy-start | bytes 1572868
  40.5 15.9 %copy-start = (bf16[1216,1024]{1,0:T(8,128)(2,1)}, bf16[1216,1024]{1,0:T(8,128)(2,1)S(1)}, u32[]{:S(2)}) copy-start(bf16[1216,1024]{1,0:T(8,128)(2,1)S(1)} %get-tuple-element.154.refs_1_.refs_2_.refs_7_) | copy-start | bytes 7471108
  56.3 7.6 %collective-permute-start.5 = (f32[1216,512]{1,0:T(8,128)S(1)}, f32[1216,512]{1,0:T(8,128)S(1)}, u32[]{:S(2)}, u32[]{:S(2)}) collective-permute-start(f32[1216,512]{1,0:T(8,128)S(1)} %get-tuple-element.171), channel_id=1, source_target_pairs={{0,1},{1,0},{2,3},{3,2},{4,5},{5,4},{6,7},{7,6},{8,9},{9,8},{10,11... | collective-permute-start | bytes 7471112 | tf_op jit(solution)/shard_map/sum_a_down_0/ppermute | solution.py:973
  64.0 1.8 copy-start.21
  64.9 17.0 %collective-permute-start.6 = (f32[608,512]{1,0:T(8,128)S(1)}, f32[608,512]{1,0:T(8,128)S(1)}, u32[]{:S(2)}, u32[]{:S(2)}) collective-permute-start(f32[608,512]{1,0:T(8,128)S(1)} %get-tuple-element.181), channel_id=1, source_target_pairs={{0,8},{1,17},{2,10},{3,19},{4,12},{5,21},{6,14},{7,23},{8,0},{9,25... | collective-permute-start | bytes 3735560 | tf_op jit(solution)/shard_map/sum_a_down_1/ppermute | solution.py:973
  80.8 7.7 %collective-permute-start.8 = (f32[1216,512]{1,0:T(8,128)S(1)}, f32[1216,512]{1,0:T(8,128)S(1)}, u32[]{:S(2)}, u32[]{:S(2)}) collective-permute-start(f32[1216,512]{1,0:T(8,128)S(1)} %get-tuple-element.190), channel_id=1, source_target_pairs={{0,1},{1,0},{2,3},{3,2},{4,5},{5,4},{6,7},{7,6},{8,9},{9,8},{10,11... | collective-permute-start | bytes 7471112 | tf_op jit(solution)/shard_map/sum_c_down_0/ppermute | solution.py:973
  82.5 10.3 %collective-permute-start.7 = (f32[304,512]{1,0:T(8,128)S(1)}, f32[304,512]{1,0:T(8,128)S(1)}, u32[]{:S(2)}, u32[]{:S(2)}) collective-permute-start(f32[304,512]{1,0:T(8,128)S(1)} %get-tuple-element.187), channel_id=1, source_target_pairs={{0,16},{1,9},{2,18},{3,11},{4,20},{5,13},{6,22},{7,15},{8,24},{9,1... | collective-permute-start | bytes 1867784 | tf_op jit(solution)/shard_map/sum_a_down_2/ppermute | solution.py:973
  92.8 3.6 %copy-start.18 = (bf16[1216,1024]{1,0:T(8,128)(2,1)S(1)}, bf16[1216,1024]{1,0:T(8,128)(2,1)}, u32[]{:S(2)}) copy-start(bf16[1216,1024]{1,0:T(8,128)(2,1)} %copy-done.17) | copy-start | bytes 7471108
  92.8 3.6 %copy-start.24 = (f32[576,128]{1,0:T(8,128)S(1)}, f32[576,128]{1,0:T(8,128)}, u32[]{:S(2)}) copy-start(f32[576,128]{1,0:T(8,128)} %copy-done.23) | copy-start | bytes 884740
  92.8 3.6 %copy-start.30 = (f32[128,1024]{1,0:T(8,128)S(1)}, f32[128,1024]{1,0:T(8,128)}, u32[]{:S(2)}) copy-start(f32[128,1024]{1,0:T(8,128)} %copy-done.29) | copy-start | bytes 1572868
  92.8 3.6 %copy-start.32 = (f32[576,128]{1,0:T(8,128)S(1)}, f32[576,128]{1,0:T(8,128)}, u32[]{:S(2)}) copy-start(f32[576,128]{1,0:T(8,128)} %copy-done.31) | copy-start | bytes 884740
  93.5 9.3 %collective-permute-start.9 = (f32[152,512]{1,0:T(8,128)S(1)}, f32[152,512]{1,0:T(8,128)S(1)}, u32[]{:S(2)}, u32[]{:S(2)}) collective-permute-start(f32[152,512]{1,0:T(8,128)S(1)} %get-tuple-element.199), channel_id=1, source_target_pairs={{0,2},{1,3},{2,0},{3,1},{4,6},{5,7},{6,4},{7,5},{8,10},{9,11},{10,... | collective-permute-start | bytes 933896 | tf_op jit(solution)/shard_map/sum_a_down_3/ppermute | solution.py:973
  95.6 16.9 %collective-permute-start.11 = (f32[608,512]{1,0:T(8,128)S(1)}, f32[608,512]{1,0:T(8,128)S(1)}, u32[]{:S(2)}, u32[]{:S(2)}) collective-permute-start(f32[608,512]{1,0:T(8,128)S(1)} %get-tuple-element.207), channel_id=1, source_target_pairs={{0,8},{1,17},{2,10},{3,19},{4,12},{5,21},{6,14},{7,23},{8,0},{9,25... | collective-permute-start | bytes 3735560 | tf_op jit(solution)/shard_map/sum_c_down_1/ppermute | solution.py:973
  103.4 9.8 %collective-permute-start.10 = (f32[152,256]{1,0:T(8,128)S(1)}, f32[152,256]{1,0:T(8,128)S(1)}, u32[]{:S(2)}, u32[]{:S(2)}) collective-permute-start(f32[152,256]{1,0:T(8,128)S(1)} %get-tuple-element.205), channel_id=1, source_target_pairs={{0,4},{1,5},{2,6},{3,7},{4,0},{5,1},{6,2},{7,3},{8,12},{9,13},{10,... | collective-permute-start | bytes 466952 | tf_op jit(solution)/shard_map/sum_a_down_4/ppermute | solution.py:973
  113.2 1.7 copy-start.1
  113.2 1.7 copy-start.22
  113.8 7.7 %collective-permute-start.12 = (f32[152,256]{1,0:T(8,128)S(1)}, f32[152,256]{1,0:T(8,128)S(1)}, u32[]{:S(2)}, u32[]{:S(2)}) collective-permute-start(f32[152,256]{1,0:T(8,128)S(1)} %get-tuple-element.210.refs_1_), channel_id=1, source_target_pairs={{0,4},{1,5},{2,6},{3,7},{4,0},{5,1},{6,2},{7,3},{8,12},{9,13},{10,... | collective-permute-start | bytes 466952 | tf_op jit(solution)/shard_map/sum_a_up_4/ppermute | solution.py:973
  118.9 10.3 %collective-permute-start.14 = (f32[304,512]{1,0:T(8,128)S(1)}, f32[304,512]{1,0:T(8,128)S(1)}, u32[]{:S(2)}, u32[]{:S(2)}) collective-permute-start(f32[304,512]{1,0:T(8,128)S(1)} %get-tuple-element.228), channel_id=1, source_target_pairs={{0,16},{1,9},{2,18},{3,11},{4,20},{5,13},{6,22},{7,15},{8,24},{9,1... | collective-permute-start | bytes 1867784 | tf_op jit(solution)/shard_map/sum_c_down_2/ppermute | solution.py:973
  122.0 9.7 %collective-permute-start.13 = (f32[152,512]{1,0:T(8,128)S(1)}, f32[152,512]{1,0:T(8,128)S(1)}, u32[]{:S(2)}, u32[]{:S(2)}) collective-permute-start(f32[152,512]{1,0:T(8,128)S(1)} %get-tuple-element.226.refs_1_), channel_id=1, source_target_pairs={{0,2},{1,3},{2,0},{3,1},{4,6},{5,7},{6,4},{7,5},{8,10},{9,11},{10,... | collective-permute-start | bytes 933896 | tf_op jit(solution)/shard_map/sum_a_up_3/ppermute | solution.py:973
  129.9 7.7 %collective-permute-start.23 = (f32[152,512]{1,0:T(8,128)S(1)}, f32[152,512]{1,0:T(8,128)S(1)}, u32[]{:S(2)}, u32[]{:S(2)}) collective-permute-start(f32[152,512]{1,0:T(8,128)S(1)} %get-tuple-element.247), channel_id=1, source_target_pairs={{0,2},{1,3},{2,0},{3,1},{4,6},{5,7},{6,4},{7,5},{8,10},{9,11},{10,... | collective-permute-start | bytes 933896 | tf_op jit(solution)/shard_map/sum_c_down_3/ppermute | solution.py:973
  135.5 6.0 %collective-permute-start.15 = (f32[344,512]{1,0:T(8,128)S(1)}, f32[344,512]{1,0:T(8,128)S(1)}, u32[]{:S(2)}, u32[]{:S(2)}) collective-permute-start(f32[344,512]{1,0:T(8,128)S(1)} %get-tuple-element.233), channel_id=1, source_target_pairs={{0,1},{1,0},{2,3},{3,2},{4,5},{5,4},{6,7},{7,6},{8,9},{9,8},{10,11... | collective-permute-start | bytes 2113544 | tf_op jit(solution)/shard_map/sum_s_down_0/ppermute | solution.py:973
  135.6 15.3 %collective-permute-start.29 = (f32[304,512]{1,0:T(8,128)S(1)}, f32[304,512]{1,0:T(8,128)S(1)}, u32[]{:S(2)}, u32[]{:S(2)}) collective-permute-start(f32[304,512]{1,0:T(8,128)S(1)} %get-tuple-element.251.refs_1_), channel_id=1, source_target_pairs={{0,16},{1,9},{2,18},{3,11},{4,20},{5,13},{6,22},{7,15},{8,24},{9,1... | collective-permute-start | bytes 1867784 | tf_op jit(solution)/shard_map/sum_a_up_2/ppermute | solution.py:973
  138.7 9.0 %collective-permute-start.24 = (f32[152,256]{1,0:T(8,128)S(1)}, f32[152,256]{1,0:T(8,128)S(1)}, u32[]{:S(2)}, u32[]{:S(2)}) collective-permute-start(f32[152,256]{1,0:T(8,128)S(1)} %get-tuple-element.250), channel_id=1, source_target_pairs={{0,4},{1,5},{2,6},{3,7},{4,0},{5,1},{6,2},{7,3},{8,12},{9,13},{10,... | collective-permute-start | bytes 466952 | tf_op jit(solution)/shard_map/sum_c_down_4/ppermute | solution.py:973
  142.1 7.4 %collective-permute-start.16 = (f32[344,256]{1,0:T(8,128)S(1)}, f32[344,256]{1,0:T(8,128)S(1)}, u32[]{:S(2)}, u32[]{:S(2)}) collective-permute-start(f32[344,256]{1,0:T(8,128)S(1)} %get-tuple-element.235), channel_id=1, source_target_pairs={{0,8},{1,17},{2,10},{3,19},{4,12},{5,21},{6,14},{7,23},{8,0},{9,25... | collective-permute-start | bytes 1056776 | tf_op jit(solution)/shard_map/sum_s_down_1/ppermute | solution.py:973
  148.3 11.3 %collective-permute-start.25 = (f32[152,256]{1,0:T(8,128)S(1)}, f32[152,256]{1,0:T(8,128)S(1)}, u32[]{:S(2)}, u32[]{:S(2)}) collective-permute-start(f32[152,256]{1,0:T(8,128)S(1)} %land_c_down_5.1.refs_1_), channel_id=1, source_target_pairs={{0,4},{1,5},{2,6},{3,7},{4,0},{5,1},{6,2},{7,3},{8,12},{9,13},{10,... | collective-permute-start | bytes 466952 | tf_op jit(solution)/shard_map/sum_c_up_4/ppermute | solution.py:973
  150.1 7.0 %collective-permute-start.17 = (f32[344,128]{1,0:T(8,128)S(1)}, f32[344,128]{1,0:T(8,128)S(1)}, u32[]{:S(2)}, u32[]{:S(2)}) collective-permute-start(f32[344,128]{1,0:T(8,128)S(1)} %get-tuple-element.237), channel_id=1, source_target_pairs={{0,16},{1,9},{2,18},{3,11},{4,20},{5,13},{6,22},{7,15},{8,24},{9,1... | collective-permute-start | bytes 528392 | tf_op jit(solution)/shard_map/sum_s_down_2/ppermute | solution.py:973
  151.5 17.0 %collective-permute-start.30 = (f32[608,512]{1,0:T(8,128)S(1)}, f32[608,512]{1,0:T(8,128)S(1)}, u32[]{:S(2)}, u32[]{:S(2)}) collective-permute-start(f32[608,512]{1,0:T(8,128)S(1)} %land_a_up_2.1.refs_1_), channel_id=1, source_target_pairs={{0,8},{1,17},{2,10},{3,19},{4,12},{5,21},{6,14},{7,23},{8,0},{9,25... | collective-permute-start | bytes 3735560 | tf_op jit(solution)/shard_map/sum_a_up_1/ppermute | solution.py:973
  157.7 9.3 %collective-permute-start.18 = (f32[344,128]{1,0:T(8,128)S(1)}, f32[344,128]{1,0:T(8,128)S(1)}, u32[]{:S(2)}, u32[]{:S(2)}) collective-permute-start(f32[344,128]{1,0:T(8,128)S(1)} %land_s_down_3.1.refs_1_), channel_id=1, source_target_pairs={{0,2},{1,3},{2,0},{3,1},{4,6},{5,7},{6,4},{7,5},{8,10},{9,11},{10,... | collective-permute-start | bytes 528392 | tf_op jit(solution)/shard_map/sum_s_down_3/ppermute | solution.py:973
  160.1 10.7 %collective-permute-start.26 = (f32[152,512]{1,0:T(8,128)S(1)}, f32[152,512]{1,0:T(8,128)S(1)}, u32[]{:S(2)}, u32[]{:S(2)}) collective-permute-start(f32[152,512]{1,0:T(8,128)S(1)} %land_c_up_4.1.refs_1_), channel_id=1, source_target_pairs={{0,2},{1,3},{2,0},{3,1},{4,6},{5,7},{6,4},{7,5},{8,10},{9,11},{10,... | collective-permute-start | bytes 933896 | tf_op jit(solution)/shard_map/sum_c_up_3/ppermute | solution.py:973
  167.6 7.7 %collective-permute-start.19 = (f32[344,128]{1,0:T(8,128)S(1)}, f32[344,128]{1,0:T(8,128)S(1)}, u32[]{:S(2)}, u32[]{:S(2)}) collective-permute-start(f32[344,128]{1,0:T(8,128)S(1)} %land_s_down_4.1.refs_1_), channel_id=1, source_target_pairs={{0,4},{1,5},{2,6},{3,7},{4,0},{5,1},{6,2},{7,3},{8,12},{9,13},{10,... | collective-permute-start | bytes 528392 | tf_op jit(solution)/shard_map/sum_s_down_4/ppermute | solution.py:973
  169.2 17.2 %collective-permute-start.31 = (f32[1216,512]{1,0:T(8,128)S(1)}, f32[1216,512]{1,0:T(8,128)S(1)}, u32[]{:S(2)}, u32[]{:S(2)}) collective-permute-start(f32[1216,512]{1,0:T(8,128)S(1)} %land_a_up_1.1.refs_1_), channel_id=1, source_target_pairs={{0,1},{1,0},{2,3},{3,2},{4,5},{5,4},{6,7},{7,6},{8,9},{9,8},{10,11... | collective-permute-start | bytes 7471112 | tf_op jit(solution)/shard_map/sum_a_up_0/ppermute | solution.py:973
  171.4 10.3 %collective-permute-start.27 = (f32[304,512]{1,0:T(8,128)S(1)}, f32[304,512]{1,0:T(8,128)S(1)}, u32[]{:S(2)}, u32[]{:S(2)}) collective-permute-start(f32[304,512]{1,0:T(8,128)S(1)} %land_c_up_3.1.refs_1_), channel_id=1, source_target_pairs={{0,16},{1,9},{2,18},{3,11},{4,20},{5,13},{6,22},{7,15},{8,24},{9,1... | collective-permute-start | bytes 1867784 | tf_op jit(solution)/shard_map/sum_c_up_2/ppermute | solution.py:973
  175.8 8.3 %collective-permute-start.20 = (f32[344,128]{1,0:T(8,128)S(1)}, f32[344,128]{1,0:T(8,128)S(1)}, u32[]{:S(2)}, u32[]{:S(2)}) collective-permute-start(f32[344,128]{1,0:T(8,128)S(1)} %land_s_down_5.1.refs_1_), channel_id=1, source_target_pairs={{0,16},{1,9},{2,18},{3,11},{4,20},{5,13},{6,22},{7,15},{8,24},{9,1... | collective-permute-start | bytes 528392 | tf_op jit(solution)/shard_map/sum_s_up_2/ppermute | solution.py:973
  182.4 17.0 %collective-permute-start.28 = (f32[608,512]{1,0:T(8,128)S(1)}, f32[608,512]{1,0:T(8,128)S(1)}, u32[]{:S(2)}, u32[]{:S(2)}) collective-permute-start(f32[608,512]{1,0:T(8,128)S(1)} %land_c_up_2.1.refs_1_), channel_id=1, source_target_pairs={{0,8},{1,17},{2,10},{3,19},{4,12},{5,21},{6,14},{7,23},{8,0},{9,25... | collective-permute-start | bytes 3735560 | tf_op jit(solution)/shard_map/sum_c_up_1/ppermute | solution.py:973
  184.7 18.4 %collective-permute-start.21 = (f32[344,256]{1,0:T(8,128)S(1)}, f32[344,256]{1,0:T(8,128)S(1)}, u32[]{:S(2)}, u32[]{:S(2)}) collective-permute-start(f32[344,256]{1,0:T(8,128)S(1)} %land_s_up_2.1.refs_1_), channel_id=1, source_target_pairs={{0,8},{1,17},{2,10},{3,19},{4,12},{5,21},{6,14},{7,23},{8,0},{9,25... | collective-permute-start | bytes 1056776 | tf_op jit(solution)/shard_map/sum_s_up_1/ppermute | solution.py:973
  200.0 9.5 %collective-permute-start.32 = (f32[1216,512]{1,0:T(8,128)S(1)}, f32[1216,512]{1,0:T(8,128)S(1)}, u32[]{:S(2)}, u32[]{:S(2)}) collective-permute-start(f32[1216,512]{1,0:T(8,128)S(1)} %land_c_up_1.1.refs_1_), channel_id=1, source_target_pairs={{0,1},{1,0},{2,3},{3,2},{4,5},{5,4},{6,7},{7,6},{8,9},{9,8},{10,11... | collective-permute-start | bytes 7471112 | tf_op jit(solution)/shard_map/sum_c_up_0/ppermute | solution.py:973
  203.7 2.2 %collective-permute-start.22 = (f32[344,512]{1,0:T(8,128)S(1)}, f32[344,512]{1,0:T(8,128)S(1)}, u32[]{:S(2)}, u32[]{:S(2)}) collective-permute-start(f32[344,512]{1,0:T(8,128)S(1)} %land_s_up_1.1.refs_1_), channel_id=1, source_target_pairs={{0,1},{1,0},{2,3},{3,2},{4,5},{5,4},{6,7},{7,6},{8,9},{9,8},{10,11... | collective-permute-start | bytes 2113544 | tf_op jit(solution)/shard_map/sum_s_up_0/ppermute | solution.py:973
  (7 other events, 6.5 us)

commit v3 on v2

--- a/solution.py
+++ b/solution.py
@@ -853,8 +853,8 @@
     "late", "send_a", "keep_a", "mid", "a", "early", "send_c", "a", "keep_c", "c",
     "a", "couple", "a", "pre0", "c", "a", "weights", "a", "pre1", "c",
     "a", "last", "c", "free", "a", "a", "a", "a", "end_a", "c",
-    "s", "c", "s", "c", "s", "s", "c", "c", "s", "s",
-    "s", "end_s", "c",
+    "s", "c", "s", "c", "s", "s", "c", "c", "c", "end_c",
+    "s", "s", "s", "end_s",
 )
 
 
@@ -1266,6 +1266,8 @@
             return
         if name == "c" and chain.rising and chain.at == 1 and v.d_latent is not None:
             order.extra = (order.token,)
+        if name == "s" and chain.rising and chain.at == 1 and v.own_done:
+            order.extra = (order.token,)
         chain.land()
 
     def settle(name):
@@ -1280,13 +1282,18 @@
         settle("s")
         finish_small()
 
+    def finish_c():
+        settle("c")
+        finish(((0, 0, True),), (chains["c"].send,), mark=True)
+        v.own_done = True
+
     def set_free():
         order.free = True
 
     def set_bound():
         order.free = False
 
-    v = types.SimpleNamespace(d_latent=None, pres=[])
+    v = types.SimpleNamespace(d_latent=None, pres=[], own_done=False)
     steps = {
         "late": run_late,
         "mid": run_mid,
@@ -1307,13 +1314,11 @@
         "bind": set_bound,
         "end_a": finish_a,
         "end_s": finish_s,
+        "end_c": finish_c,
     }
     for step in PROGRAM:
         steps[step]()
-    settle("c")
-    c = chains["c"]
-    finish(((0, 0, True),), (c.send,))
-    finish(((0, 0, False),), (c.got,))
+    finish(((0, 0, False),), (chains["c"].got,))
     (center, neigh, radial, value, env, path_grad, out, scale, shift, position_grad,
      energies) = v.small
     d_latent = v.d_latent

time: 216 us -> 214 us (level)
  no operation moved by 1% of the time
where the time goes in v3:
time: 214 us; the launch traced here: 210 us
  Pallas kernels  118 us (55%)
  waiting for transfers between devices  50 us (23%)
  starting transfers between devices  37.5 us (18%)
  local copies, waits for them, and re-layouts  2.97 us (1%)
    pallas_call x46, Pallas kernels, __call__(): pl.pallas_call(kernel, name=name or getattr(body, 'func', body).__name__,...  118 us
    ppermute x28, waiting for transfers between devices, swap(): return lax.ppermute(x, self.names, self.pairs[at])  47.7 us
    ppermute x28, starting transfers between devices, swap(): return lax.ppermute(x, self.names, self.pairs[at])  25.2 us
    ppermute x3, starting transfers between devices, neighbours_of(): lax.ppermute(even, axis, even_pairs(axis))  10.7 us
  transfers between devices with their start and end apart: 33, of which 19 were waited for; matrix products, arithmetic and copies ran while one was open for 0% of the time, Pallas kernels for 37%

profile of v3, /device:TPU:0, one launch (start us, length us, event | category | flops | bytes accessed | tf_op | source)
XLA Modules:
  0.0 209.8 jit_solution(14946564022870672992)
XLA Ops:
  2.5 0.7 collective-permute-done.refs_2_
  3.9 0.8 collective-permute-start.2
  4.7 5.9 %collective-permute-start.1 = (f32[8,128]{1,0:T(8,128)S(1)}, f32[8,128]{1,0:T(8,128)S(1)}, u32[]{:S(2)}, u32[]{:S(2)}) collective-permute-start(f32[8,128]{1,0:T(8,128)S(1)} %get-tuple-element.139.refs_1_), channel_id=1, source_target_pairs={{0,2},{2,0},{4,6},{6,4},{1,3},{3,1},{5,7},{7,5},{8,10},{10,8},{12,... | collective-permute-start | bytes 12296 | tf_op jit(solution)/shard_map/ppermute | solution.py:933
  10.6 1.6 collective-permute-done.1.refs_2_
  12.9 0.8 collective-permute-start.4
  13.7 4.3 %collective-permute-start.3 = (f32[8,384]{1,0:T(8,128)S(1)}, f32[8,384]{1,0:T(8,128)S(1)}, u32[]{:S(2)}, u32[]{:S(2)}) collective-permute-start(f32[8,384]{1,0:T(8,128)S(1)} %get-tuple-element.141.refs_1_), channel_id=1, source_target_pairs={{0,8},{8,0},{16,24},{24,16},{1,9},{9,1},{17,25},{25,17},{2,10},{10... | collective-permute-start | bytes 36872 | tf_op jit(solution)/shard_map/ppermute | solution.py:933
  18.1 2.6 %prep_kernel.1 = (bf16[1216,1024]{1,0:T(8,128)(2,1)S(1)}, bf16[1216,1024]{1,0:T(8,128)(2,1)S(1)}, bf16[1216,1024]{1,0:T(8,128)(2,1)S(1)}, bf16[1216,1024]{1,0:T(...) custom-call(f32[2,1216,1024]{2,1,0:T(8,128)S(1)} %bitcast.21, ...), custom_call_target="tpu_custom_call" | custom-call | flops 12000000000 | bytes 1048576 | tf_op jit(solution)/shard_map/prep_kernel/pallas_call | solution.py:898
  20.8 18.9 %fwd_kernel.1 = (bf16[1216,1024]{1,0:T(8,128)(2,1)S(1)}, bf16[1216,1024]{1,0:T(8,128)(2,1)S(1)}, bf16[1216,1024]{1,0:T(8,128)(2,1)S(1)}, bf16[1216,1024]{1,0:T(8...) custom-call(s32[15]{0:T(128)S(1)} %stack.39.refs_0_, ...), custom_call_target="tpu_custom_call" | custom-call | flops 65999998976 | bytes 1048576 | tf_op jit(solution)/shard_map/fwd_kernel/pallas_call | solution.py:898
  39.8 0.7 copy-done.31
  40.5 10.9 %late_kernel.1 = (bf16[1024,1024]{1,0:T(8,128)(2,1)S(1)}, bf16[1024,1024]{1,0:T(8,128)(2,1)S(1)}, f32[8,1024]{1,0:T(8,128)S(1)}, f32[8,1024]{1,0:T(8,128)S(1)}, f32[8,128]{1,0:T(8,128)S(1)}) custom-call(bf16[1216,1024]{1,0:T(8,128)(2,1)S(1)} %get-tuple-element.155.refs_0_.refs_1_.refs_6_, bf16[1216,1024]{1,0:T(8,128)(2,1)S(1)} %get-tuple-element.156.refs_1_.refs_2_.refs_7_, ...), custom_call_target="tpu_custom_call" | custom-call | flops 19499999232 | bytes 1048576 | tf_op jit(solution)/shard_map/late_kernel/pallas_call | solution.py:898
  51.5 4.8 %grad_kernel.4 = (f32[1216,512]{1,0:T(8,128)S(1)}, f32[8,128]{1,0:T(8,128)S(1)}) custom-call(s32[15]{0:T(128)S(1)} %stack.39.refs_0_, bf16[1216,1024]{1,0:T(8,128)(2,1)S(1)} %get-tuple-element.155.refs_0_.refs_1_.refs_6_, bf16[1216,1024]{1,0:T(8,128)(2,1)S(1)} %get-tuple-element.156.refs_1_.refs_2_.refs_7_, ...), custom_call_target="tpu_custom_call" | custom-call | flops 13799999488 | bytes 1048576 | tf_op jit(solution)/shard_map/grad_kernel/pallas_call | solution.py:898
  56.4 4.7 %grad_kernel.5 = (f32[1216,512]{1,0:T(8,128)S(1)}, f32[8,128]{1,0:T(8,128)S(1)}) custom-call(s32[15]{0:T(128)S(1)} %stack.39.refs_0_, bf16[1216,1024]{1,0:T(8,128)(2,1)S(1)} %get-tuple-element.155.refs_0_.refs_1_.refs_6_, bf16[1216,1024]{1,0:T(8,128)(2,1)S(1)} %get-tuple-element.156.refs_1_.refs_2_.refs_7_, ...), custom_call_target="tpu_custom_call" | custom-call | flops 1710000000 | bytes 1048576 | tf_op jit(solution)/shard_map/grad_kernel/pallas_call | solution.py:898
  61.1 2.9 %mid_kernel.1 = (f32[192,1024]{1,0:T(8,128)S(1)}, bf16[64,1024]{1,0:T(8,128)(2,1)S(1)}, bf16[64,1024]{1,0:T(8,128)(2,1)S(1)}, f32[16,1024]{1,0:T(8,128)S(1)}, f32[8,128]{1,0:T(8,128)S(1)}) custom-call(bf16[1024,1024]{1,0:T(8,128)(2,1)S(1)} %get-tuple-element.161.refs_3_.refs_0_, bf16[1024,1024]{1,0:T(8,128)(2,1)S(1)} %get-tuple-element.162.refs_4_.refs_1_, ...), custom_call_target="tpu_custom_call" | custom-call | flops 8999999488 | bytes 1048576 | tf_op jit(solution)/shard_map/mid_kernel/pallas_call | solution.py:898
  64.0 0.9 land_a_down_1.1
  64.9 0.9 collective-permute-start.6
  65.8 10.4 %early_kernel.1 = (f32[1024,1024]{1,0:T(8,128)S(1)}, bf16[1024,1024]{1,0:T(8,128)(2,1)S(1)}, bf16[1024,1024]{1,0:T(8,128)(2,1)S(1)}, f32[8,1024]{1,0:T(8,128)S(1)}, f32[8,128]{1,0:T(8,128)S(1)}) custom-call(bf16[1024,1024]{1,0:T(8,128)(2,1)S(1)} %get-tuple-element.161.refs_3_.refs_0_, bf16[1024,1024]{1,0:T(8,128)(2,1)S(1)} %get-tuple-element.162.refs_4_.refs_1_, ...), custom_call_target="tpu_custom_call" | custom-call | flops 15000000512 | bytes 1048576 | tf_op jit(solution)/shard_map/early_kernel/pallas_call | solution.py:898
  76.2 4.7 %grad_kernel.6 = (f32[1216,512]{1,0:T(8,128)S(1)}, f32[8,128]{1,0:T(8,128)S(1)}) custom-call(s32[15]{0:T(128)S(1)} %stack.39.refs_0_, bf16[1216,1024]{1,0:T(8,128)(2,1)S(1)} %get-tuple-element.184.refs_1_.refs_2_, bf16[1216,1024]{1,0:T(8,128)(2,1)S(1)} %get-tuple-element.185.refs_2_.refs_3_, bf16[1024,1024]{1,0:T(8,128)(2,1)S(1)} %get-tuple-element.176.refs_3_.refs_0_, ...), custom_call_target="tpu_custom_call" | custom-call | flops 13799999488 | bytes 1048576 | tf_op jit(solution)/shard_map/grad_kernel/pallas_call | solution.py:898
  81.1 0.8 collective-permute-done.6.refs_2_
  81.8 0.7 land_a_down_2.1
  82.5 0.9 collective-permute-start.7
  83.4 5.1 %grad_kernel.7 = (f32[1216,512]{1,0:T(8,128)S(1)}, f32[8,128]{1,0:T(8,128)S(1)}) custom-call(s32[15]{0:T(128)S(1)} %stack.39.refs_0_, bf16[1216,1024]{1,0:T(8,128)(2,1)S(1)} %get-tuple-element.184.refs_1_.refs_2_, bf16[1216,1024]{1,0:T(8,128)(2,1)S(1)} %get-tuple-element.185.refs_2_.refs_3_, bf16[1024,1024]{1,0:T(8,128)(2,1)S(1)} %get-tuple-element.176.refs_3_.refs_0_, ...), custom_call_target="tpu_custom_call" | custom-call | flops 13799999488 | bytes 1048576 | tf_op jit(solution)/shard_map/grad_kernel/pallas_call | solution.py:898
  88.5 0.8 land_c_down_1.1
  89.3 3.5 %collective-permute-done.7.refs_2_ = f32[304,512]{1,0:T(8,128)S(1)} collective-permute-done((f32[304,512]{1,0:T(8,128)S(1)}, f32[304,512]{1,0:T(8,128)S(1)}, u32[]{:S(2)}, u32[]{:S(2)}) %collective-permute-start.7) | collective-permute-done | bytes 622624 | tf_op jit(solution)/shard_map/sum_a_down_2/ppermute | solution.py:973
  93.5 2.1 collective-permute-start.9
  95.6 0.8 collective-permute-start.11
  96.4 6.3 %couple_kernel.1 = (bf16[128,1024]{1,0:T(8,128)(2,1)S(1)}, bf16[128,1024]{1,0:T(8,128)(2,1)S(1)}, f32[16,1024]{1,0:T(8,128)S(1)}, f32[576,128]{1,0:T(8,128)S(1)}, f32[8,128]{1,0:T(8,128)S(1)}) custom-call(bf16[1024,1024]{1,0:T(8,128)(2,1)S(1)} %get-tuple-element.176.refs_3_.refs_0_, bf16[1024,1024]{1,0:T(8,128)(2,1)S(1)} %get-tuple-element.177.refs_4_.refs_1_, ...), custom_call_target="tpu_custom_call" | custom-call | flops 75600003072 | bytes 1048576 | tf_op jit(solution)/shard_map/couple_kernel/pallas_call | solution.py:898
  103.4 0.8 collective-permute-start.10
  104.2 6.7 %pre_kernel.2 = (bf16[512,1024]{1,0:T(8,128)(2,1)S(1)}, bf16[512,1024]{1,0:T(8,128)(2,1)S(1)}, f32[8,1024]{1,0:T(8,128)S(1)}, f32[8,1024]{1,0:T(8,128)S(1)}, f32[8,128]{1,0:T(8,128)S(1)}) custom-call(bf16[1024,1024]{1,0:T(8,128)(2,1)S(1)} %get-tuple-element.176.refs_3_.refs_0_, bf16[1024,1024]{1,0:T(8,128)(2,1)S(1)} %get-tuple-element.177.refs_4_.refs_1_, ...), custom_call_target="tpu_custom_call" | custom-call | flops 10499999744 | bytes 1048576 | tf_op jit(solution)/shard_map/pre_kernel/pallas_call | solution.py:898
  110.9 1.6 collective-permute-done.11.refs_2_
  113.8 0.7 collective-permute-start.12
  114.9 4.0 %weights_kernel.1 = (f32[192,1024]{1,0:T(8,128)S(1)}, f32[8,128]{1,0:T(8,128)S(1)}) custom-call(bf16[128,1024]{1,0:T(8,128)(2,1)S(1)} %get-tuple-element.196.refs_6_.refs_0_, bf16[128,1024]{1,0:T(8,128)(2,1)S(1)} %get-tuple-element.197.refs_7_.refs_1_, bf16[1216,1024]{1,0:T(8,128)(2,1)S(1)} %get-tuple-element.184.refs_1_.refs_2_, ...), custom_call_target="tpu_custom_call" | custom-call | flops 12000000000 | bytes 1048576 | tf_op jit(solution)/shard_map/weights_kernel/pallas_call | solution.py:898
  118.9 0.9 collective-permute-start.14
  119.8 1.6 collective-permute-done.12.refs_2_
  122.1 6.9 %pre_kernel.3 = (bf16[512,1024]{1,0:T(8,128)(2,1)S(1)}, bf16[512,1024]{1,0:T(8,128)(2,1)S(1)}, f32[8,1024]{1,0:T(8,128)S(1)}, f32[8,1024]{1,0:T(8,128)S(1)}, f32[8,128]{1,0:T(8,128)S(1)}) custom-call(bf16[1024,1024]{1,0:T(8,128)(2,1)S(1)} %get-tuple-element.176.refs_3_.refs_0_, bf16[1024,1024]{1,0:T(8,128)(2,1)S(1)} %get-tuple-element.177.refs_4_.refs_1_, ...), custom_call_target="tpu_custom_call" | custom-call | flops 10499999744 | bytes 1048576 | tf_op jit(solution)/shard_map/pre_kernel/pallas_call | solution.py:898
  129.9 1.9 collective-permute-start.22
  132.6 2.9 %last_kernel.1 = (f32[344,512]{1,0:T(8,128)S(1)}, f32[344,512]{1,0:T(8,128)S(1)}, f32[8,128]{1,0:T(8,128)S(1)}, f32[8,128]{1,0:T(8,128)S(1)}) custom-call(s32[15]{0:T(128)S(1)} %stack.39.refs_0_, bf16[512,1024]{1,0:T(8,128)(2,1)S(1)} %get-tuple-element.204.refs_1_, bf16[512,1024]{1,0:T(8,128)(2,1)S(1)} %get-tuple-element.205.refs_2_, ...), custom_call_target="tpu_custom_call" | custom-call | flops 15000000512 | bytes 1048576 | tf_op jit(solution)/shard_map/last_kernel/pallas_call | solution.py:898
  135.6 1.2 collective-permute-start.28
  136.8 0.8 collective-permute-done.22.refs_2_
  137.5 1.1 land_c_down_4.1
  138.7 2.8 %collective-permute-start.23 = (f32[152,256]{1,0:T(8,128)S(1)}, f32[152,256]{1,0:T(8,128)S(1)}, u32[]{:S(2)}, u32[]{:S(2)}) collective-permute-start(f32[152,256]{1,0:T(8,128)S(1)} %get-tuple-element.244), channel_id=1, source_target_pairs={{0,4},{1,5},{2,6},{3,7},{4,0},{5,1},{6,2},{7,3},{8,12},{9,13},{10,... | collective-permute-start | bytes 466952 | tf_op jit(solution)/shard_map/sum_c_down_4/ppermute | solution.py:973
  142.2 5.5 %collective-permute-done.23.refs_2_ = f32[152,256]{1,0:T(8,128)S(1)} collective-permute-done((f32[152,256]{1,0:T(8,128)S(1)}, f32[152,256]{1,0:T(8,128)S(1)}, u32[]{:S(2)}, u32[]{:S(2)}) %collective-permute-start.23) | collective-permute-done | bytes 155680 | tf_op jit(solution)/shard_map/sum_c_down_4/ppermute | solution.py:973
  148.3 1.2 collective-permute-done.16.refs_2_
  150.1 0.8 collective-permute-start.17
  151.5 1.5 collective-permute-start.29
  153.1 4.1 %collective-permute-done.17.refs_2_ = f32[344,128]{1,0:T(8,128)S(1)} collective-permute-done((f32[344,128]{1,0:T(8,128)S(1)}, f32[344,128]{1,0:T(8,128)S(1)}, u32[]{:S(2)}, u32[]{:S(2)}) %collective-permute-start.17) | collective-permute-done | bytes 176160 | tf_op jit(solution)/shard_map/sum_s_down_2/ppermute | solution.py:973
  157.7 1.8 collective-permute-start.18
  160.5 6.5 %collective-permute-done.18.refs_2_ = f32[344,128]{1,0:T(8,128)S(1)} collective-permute-done((f32[344,128]{1,0:T(8,128)S(1)}, f32[344,128]{1,0:T(8,128)S(1)}, u32[]{:S(2)}, u32[]{:S(2)}) %collective-permute-start.18) | collective-permute-done | bytes 176160 | tf_op jit(solution)/shard_map/sum_s_down_3/ppermute | solution.py:973
  167.8 0.7 collective-permute-done.29.refs_2_
  168.5 0.7 land_a_up_1.1.refs_1_
  169.9 1.0 collective-permute-done.25.refs_2_
  171.4 1.6 collective-permute-start.26
  173.1 2.2 %collective-permute-done.19.refs_2_ = f32[344,128]{1,0:T(8,128)S(1)} collective-permute-done((f32[344,128]{1,0:T(8,128)S(1)}, f32[344,128]{1,0:T(8,128)S(1)}, u32[]{:S(2)}, u32[]{:S(2)}) %collective-permute-start.19) | collective-permute-done | bytes 176160 | tf_op jit(solution)/shard_map/sum_s_down_4/ppermute | solution.py:973
  175.8 1.1 collective-permute-start.20
  177.0 4.8 %collective-permute-done.26.refs_2_ = f32[304,512]{1,0:T(8,128)S(1)} collective-permute-done((f32[304,512]{1,0:T(8,128)S(1)}, f32[304,512]{1,0:T(8,128)S(1)}, u32[]{:S(2)}, u32[]{:S(2)}) %collective-permute-start.26) | collective-permute-done | bytes 622624 | tf_op jit(solution)/shard_map/sum_c_up_2/ppermute | solution.py:973
  182.4 1.7 collective-permute-start.27
  184.6 1.8 collective-permute-start.21
  186.5 2.8 %end_kernel.3 = (f32[2,1216,1024]{2,1,0:T(8,128)}, f32[8,128]{1,0:T(8,128)S(1)}) custom-call(s32[15]{0:T(128)S(1)} %stack.39.refs_0_, f32[1216,512]{1,0:T(8,128)S(1)} %land_a_up_1.1.refs_1_, f32[1216,512]{1,0:T(8,128)S(1)} %collective-permute-done.30.refs_2_), custom_call_target="tpu_custom_call" | custom-call | flops 8999999488 | bytes 1048576 | tf_op jit(solution)/shard_map/end_kernel/pallas_call | solution.py:898
  189.3 10.0 %collective-permute-done.27.refs_2_ = f32[608,512]{1,0:T(8,128)S(1)} collective-permute-done((f32[608,512]{1,0:T(8,128)S(1)}, f32[608,512]{1,0:T(8,128)S(1)}, u32[]{:S(2)}, u32[]{:S(2)}) %collective-permute-start.27) | collective-permute-done | bytes 1245216 | tf_op jit(solution)/shard_map/sum_c_up_1/ppermute | solution.py:973
  199.3 0.7 land_c_up_1.1.refs_1_
  200.1 2.0 end_kernel.4
  202.2 1.0 collective-permute-done.21.refs_2_
  203.8 2.2 %collective-permute-done.31.refs_2_ = f32[344,512]{1,0:T(8,128)S(1)} collective-permute-done((f32[344,512]{1,0:T(8,128)S(1)}, f32[344,512]{1,0:T(8,128)S(1)}, u32[]{:S(2)}, u32[]{:S(2)}) %collective-permute-start.31) | collective-permute-done | bytes 704544 | tf_op jit(solution)/shard_map/sum_s_up_0/ppermute | solution.py:973
  206.0 1.6 small_end_kernel.1
  207.6 2.0 end_kernel.5
  (127 shorter events, 17.4 us)
Async XLA Ops:
  2.0 1.3 collective-permute-start
  3.3 14.7 %slice-start = ((s8[9961472]{0:T(1024)(128)(4,1)}), s8[4194304]{0:T(1024)(128)(4,1)S(1)}, s32[]{:S(2)}) async-start(s8[9961472]{0:T(1024)(128)(4,1)} %bitcast.20), calls=%async_computation | async-start | bytes 8388608
  3.3 14.7 %slice-start.1 = ((s8[9961472]{0:T(1024)(128)(4,1)}), s8[4194304]{0:T(1024)(128)(4,1)S(1)}, s32[]{:S(2)}) async-start(s8[9961472]{0:T(1024)(128)(4,1)} %bitcast.20), calls=%async_computation.1 | async-start | bytes 8388608
  3.9 6.7 %collective-permute-start.2 = (f32[8,128]{1,0:T(8,128)S(1)}, f32[8,128]{1,0:T(8,128)S(1)}, u32[]{:S(2)}, u32[]{:S(2)}) collective-permute-start(f32[8,128]{1,0:T(8,128)S(1)} %get-tuple-element.139.refs_1_), channel_id=1, source_target_pairs={{2,4},{4,2},{3,5},{5,3},{10,12},{12,10},{11,13},{13,11},{18,20},{2... | collective-permute-start | bytes 12296 | tf_op jit(solution)/shard_map/ppermute | solution.py:934
  4.7 7.5 %collective-permute-start.1 = (f32[8,128]{1,0:T(8,128)S(1)}, f32[8,128]{1,0:T(8,128)S(1)}, u32[]{:S(2)}, u32[]{:S(2)}) collective-permute-start(f32[8,128]{1,0:T(8,128)S(1)} %get-tuple-element.139.refs_1_), channel_id=1, source_target_pairs={{0,2},{2,0},{4,6},{6,4},{1,3},{3,1},{5,7},{7,5},{8,10},{10,8},{12,... | collective-permute-start | bytes 12296 | tf_op jit(solution)/shard_map/ppermute | solution.py:933
  12.2 5.8 %slice-start.2 = ((s8[9961472]{0:T(1024)(128)(4,1)}), s8[1572864]{0:T(1024)(128)(4,1)S(1)}, s32[]{:S(2)}) async-start(s8[9961472]{0:T(1024)(128)(4,1)} %bitcast.20), calls=%async_computation.2 | async-start | bytes 3145728
  12.2 5.8 %copy-start.2 = (f32[2,1024,64]{1,2,0:T(8,128)S(1)}, f32[2,1024,64]{1,2,0:T(8,128)}, u32[]{:S(2)}) copy-start(f32[2,1024,64]{1,2,0:T(8,128)} %param.21) | copy-start | bytes 1572868
  12.2 5.8 %copy-start.3 = (f32[64,1024]{1,0:T(8,128)S(1)}, f32[64,1024]{1,0:T(8,128)}, u32[]{:S(2)}) copy-start(f32[64,1024]{1,0:T(8,128)} %refs_1_.1) | copy-start | bytes 786436
  12.2 5.8 %copy-start.4 = (f32[64,1024]{1,0:T(8,128)S(1)}, f32[64,1024]{1,0:T(8,128)}, u32[]{:S(2)}) copy-start(f32[64,1024]{1,0:T(8,128)} %refs_2_.1) | copy-start | bytes 786436
  12.2 5.8 %copy-start.5 = (f32[1024,64]{0,1:T(8,128)S(1)}, f32[1024,64]{0,1:T(8,128)}, u32[]{:S(2)}) copy-start(f32[1024,64]{0,1:T(8,128)} %param.20) | copy-start | bytes 786436
  12.2 5.8 %copy-start.6 = (f32[8,1024]{1,0:T(8,128)S(1)}, f32[8,1024]{1,0:T(8,128)}, u32[]{:S(2)}) copy-start(f32[8,1024]{1,0:T(8,128)} %refs_3_.1) | copy-start | bytes 98308
  12.2 5.8 %copy-start.7 = (s32[32,32]{1,0:T(8,128)S(1)}, s32[32,32]{1,0:T(8,128)}, u32[]{:S(2)}) copy-start(s32[32,32]{1,0:T(8,128)} %refs_6_.1) | copy-start | bytes 12292
  12.2 5.8 %copy-start.8 = (f32[9,64]{1,0:T(8,128)S(1)}, f32[9,64]{1,0:T(8,128)}, u32[]{:S(2)}) copy-start(f32[9,64]{1,0:T(8,128)} %refs_10_.1) | copy-start | bytes 6916
  12.3 5.8 %copy-start.9 = (f32[1024]{0:T(1024)S(1)}, f32[1024]{0:T(1024)}, u32[]{:S(2)}) copy-start(f32[1024]{0:T(1024)} %param.24) | copy-start | bytes 12292
  12.3 5.8 %copy-start.11 = (f32[3,32]{1,0:T(4,128)S(1)}, f32[3,32]{1,0:T(4,128)}, u32[]{:S(2)}) copy-start(f32[3,32]{1,0:T(4,128)} %refs_7_.1) | copy-start | bytes 1156
  12.3 5.8 %copy-start.13 = (s32[32]{0:T(128)S(1)}, s32[32]{0:T(128)}, u32[]{:S(2)}) copy-start(s32[32]{0:T(128)} %param.15) | copy-start | bytes 388
  12.3 5.8 %copy-start.14 = (f32[32]{0:T(128)S(1)}, f32[32]{0:T(128)}, u32[]{:S(2)}) copy-start(f32[32]{0:T(128)} %param.27) | copy-start | bytes 388
  12.3 5.8 %copy-start.15 = (f32[64]{0:T(128)S(1)}, f32[64]{0:T(128)}, u32[]{:S(2)}) copy-start(f32[64]{0:T(128)} %param.25) | copy-start | bytes 772
  12.3 5.8 %copy-start.16 = (f32[64]{0:T(128)S(1)}, f32[64]{0:T(128)}, u32[]{:S(2)}) copy-start(f32[64]{0:T(128)} %param.26) | copy-start | bytes 772
  12.9 7.9 %collective-permute-start.4 = (f32[8,384]{1,0:T(8,128)S(1)}, f32[8,384]{1,0:T(8,128)S(1)}, u32[]{:S(2)}, u32[]{:S(2)}) collective-permute-start(f32[8,384]{1,0:T(8,128)S(1)} %get-tuple-element.141.refs_1_), channel_id=1, source_target_pairs={{8,16},{16,8},{9,17},{17,9},{10,18},{18,10},{11,19},{19,11},{12,20... | collective-permute-start | bytes 36872 | tf_op jit(solution)/shard_map/ppermute | solution.py:934
  13.7 7.1 %collective-permute-start.3 = (f32[8,384]{1,0:T(8,128)S(1)}, f32[8,384]{1,0:T(8,128)S(1)}, u32[]{:S(2)}, u32[]{:S(2)}) collective-permute-start(f32[8,384]{1,0:T(8,128)S(1)} %get-tuple-element.141.refs_1_), channel_id=1, source_target_pairs={{0,8},{8,0},{16,24},{24,16},{1,9},{9,1},{17,25},{25,17},{2,10},{10... | collective-permute-start | bytes 36872 | tf_op jit(solution)/shard_map/ppermute | solution.py:933
  20.7 19.0 %copy-start.17 = (bf16[1216,1024]{1,0:T(8,128)(2,1)}, bf16[1216,1024]{1,0:T(8,128)(2,1)S(1)}, u32[]{:S(2)}) copy-start(bf16[1216,1024]{1,0:T(8,128)(2,1)S(1)} %get-tuple-element.146.refs_7_.refs_3_) | copy-start | bytes 7471108
  20.8 19.0 %copy-start.19 = (bf16[128,1024]{1,0:T(8,128)(2,1)}, bf16[128,1024]{1,0:T(8,128)(2,1)S(1)}, u32[]{:S(2)}) copy-start(bf16[128,1024]{1,0:T(8,128)(2,1)S(1)} %get-tuple-element.148.refs_9_.refs_4_) | copy-start | bytes 786436
  20.8 19.0 %copy-start.23 = (f32[576,128]{1,0:T(8,128)}, f32[576,128]{1,0:T(8,128)S(1)}, u32[]{:S(2)}) copy-start(f32[576,128]{1,0:T(8,128)S(1)} %get-tuple-element.152.refs_13_.refs_9_) | copy-start | bytes 884740
  20.8 19.0 %copy-start.27 = (f32[8,1024]{1,0:T(8,128)}, f32[8,1024]{1,0:T(8,128)S(1)}, u32[]{:S(2)}) copy-start(f32[8,1024]{1,0:T(8,128)S(1)} %get-tuple-element.144.refs_5_.refs_10_.refs_11_) | copy-start | bytes 98308
  20.8 19.0 %copy-start.33 = (s32[1,1024]{1,0:T(1,128)}, s32[1,1024]{1,0:T(1,128)S(1)}, u32[]{:S(2)}) copy-start(s32[1,1024]{1,0:T(1,128)S(1)} %get-tuple-element.143.refs_4_.refs_10_) | copy-start | bytes 12292
  20.8 45.0 %copy-start.25 = (f32[128,128]{1,0:T(8,128)}, f32[128,128]{1,0:T(8,128)S(1)}, u32[]{:S(2)}) copy-start(f32[128,128]{1,0:T(8,128)S(1)} %get-tuple-element.153.refs_14_.refs_4_.refs_8_.refs_16_) | copy-start | bytes 196612
  40.5 11.0 %copy-start.29 = (f32[128,1024]{1,0:T(8,128)}, f32[128,1024]{1,0:T(8,128)S(1)}, u32[]{:S(2)}) copy-start(f32[128,1024]{1,0:T(8,128)S(1)} %get-tuple-element.178.refs_4_) | copy-start | bytes 1572868
  40.5 15.9 %copy-start = (bf16[1216,1024]{1,0:T(8,128)(2,1)}, bf16[1216,1024]{1,0:T(8,128)(2,1)S(1)}, u32[]{:S(2)}) copy-start(bf16[1216,1024]{1,0:T(8,128)(2,1)S(1)} %get-tuple-element.156.refs_1_.refs_2_.refs_7_) | copy-start | bytes 7471108
  56.4 7.6 %collective-permute-start.5 = (f32[1216,512]{1,0:T(8,128)S(1)}, f32[1216,512]{1,0:T(8,128)S(1)}, u32[]{:S(2)}, u32[]{:S(2)}) collective-permute-start(f32[1216,512]{1,0:T(8,128)S(1)} %get-tuple-element.173), channel_id=1, source_target_pairs={{0,1},{1,0},{2,3},{3,2},{4,5},{5,4},{6,7},{7,6},{8,9},{9,8},{10,11... | collective-permute-start | bytes 7471112 | tf_op jit(solution)/shard_map/sum_a_down_0/ppermute | solution.py:973
  64.0 1.8 copy-start.21
  64.9 17.0 %collective-permute-start.6 = (f32[608,512]{1,0:T(8,128)S(1)}, f32[608,512]{1,0:T(8,128)S(1)}, u32[]{:S(2)}, u32[]{:S(2)}) collective-permute-start(f32[608,512]{1,0:T(8,128)S(1)} %get-tuple-element.183), channel_id=1, source_target_pairs={{0,8},{1,17},{2,10},{3,19},{4,12},{5,21},{6,14},{7,23},{8,0},{9,25... | collective-permute-start | bytes 3735560 | tf_op jit(solution)/shard_map/sum_a_down_1/ppermute | solution.py:973
  80.8 7.7 %collective-permute-start.8 = (f32[1216,512]{1,0:T(8,128)S(1)}, f32[1216,512]{1,0:T(8,128)S(1)}, u32[]{:S(2)}, u32[]{:S(2)}) collective-permute-start(f32[1216,512]{1,0:T(8,128)S(1)} %get-tuple-element.192), channel_id=1, source_target_pairs={{0,1},{1,0},{2,3},{3,2},{4,5},{5,4},{6,7},{7,6},{8,9},{9,8},{10,11... | collective-permute-start | bytes 7471112 | tf_op jit(solution)/shard_map/sum_c_down_0/ppermute | solution.py:973
  82.5 10.3 %collective-permute-start.7 = (f32[304,512]{1,0:T(8,128)S(1)}, f32[304,512]{1,0:T(8,128)S(1)}, u32[]{:S(2)}, u32[]{:S(2)}) collective-permute-start(f32[304,512]{1,0:T(8,128)S(1)} %get-tuple-element.189), channel_id=1, source_target_pairs={{0,16},{1,9},{2,18},{3,11},{4,20},{5,13},{6,22},{7,15},{8,24},{9,1... | collective-permute-start | bytes 1867784 | tf_op jit(solution)/shard_map/sum_a_down_2/ppermute | solution.py:973
  92.8 3.6 %copy-start.18 = (bf16[1216,1024]{1,0:T(8,128)(2,1)S(1)}, bf16[1216,1024]{1,0:T(8,128)(2,1)}, u32[]{:S(2)}) copy-start(bf16[1216,1024]{1,0:T(8,128)(2,1)} %copy-done.17) | copy-start | bytes 7471108
  92.9 3.6 %copy-start.24 = (f32[576,128]{1,0:T(8,128)S(1)}, f32[576,128]{1,0:T(8,128)}, u32[]{:S(2)}) copy-start(f32[576,128]{1,0:T(8,128)} %copy-done.23) | copy-start | bytes 884740
  92.9 3.6 %copy-start.30 = (f32[128,1024]{1,0:T(8,128)S(1)}, f32[128,1024]{1,0:T(8,128)}, u32[]{:S(2)}) copy-start(f32[128,1024]{1,0:T(8,128)} %copy-done.29) | copy-start | bytes 1572868
  92.9 3.6 %copy-start.32 = (f32[576,128]{1,0:T(8,128)S(1)}, f32[576,128]{1,0:T(8,128)}, u32[]{:S(2)}) copy-start(f32[576,128]{1,0:T(8,128)} %copy-done.31) | copy-start | bytes 884740
  93.5 9.3 %collective-permute-start.9 = (f32[152,512]{1,0:T(8,128)S(1)}, f32[152,512]{1,0:T(8,128)S(1)}, u32[]{:S(2)}, u32[]{:S(2)}) collective-permute-start(f32[152,512]{1,0:T(8,128)S(1)} %get-tuple-element.201), channel_id=1, source_target_pairs={{0,2},{1,3},{2,0},{3,1},{4,6},{5,7},{6,4},{7,5},{8,10},{9,11},{10,... | collective-permute-start | bytes 933896 | tf_op jit(solution)/shard_map/sum_a_down_3/ppermute | solution.py:973
  95.6 16.9 %collective-permute-start.11 = (f32[608,512]{1,0:T(8,128)S(1)}, f32[608,512]{1,0:T(8,128)S(1)}, u32[]{:S(2)}, u32[]{:S(2)}) collective-permute-start(f32[608,512]{1,0:T(8,128)S(1)} %get-tuple-element.209), channel_id=1, source_target_pairs={{0,8},{1,17},{2,10},{3,19},{4,12},{5,21},{6,14},{7,23},{8,0},{9,25... | collective-permute-start | bytes 3735560 | tf_op jit(solution)/shard_map/sum_c_down_1/ppermute | solution.py:973
  103.4 9.8 %collective-permute-start.10 = (f32[152,256]{1,0:T(8,128)S(1)}, f32[152,256]{1,0:T(8,128)S(1)}, u32[]{:S(2)}, u32[]{:S(2)}) collective-permute-start(f32[152,256]{1,0:T(8,128)S(1)} %get-tuple-element.207), channel_id=1, source_target_pairs={{0,4},{1,5},{2,6},{3,7},{4,0},{5,1},{6,2},{7,3},{8,12},{9,13},{10,... | collective-permute-start | bytes 466952 | tf_op jit(solution)/shard_map/sum_a_down_4/ppermute | solution.py:973
  113.2 1.7 copy-start.1
  113.2 1.7 copy-start.22
  113.8 7.7 %collective-permute-start.12 = (f32[152,256]{1,0:T(8,128)S(1)}, f32[152,256]{1,0:T(8,128)S(1)}, u32[]{:S(2)}, u32[]{:S(2)}) collective-permute-start(f32[152,256]{1,0:T(8,128)S(1)} %get-tuple-element.212.refs_1_), channel_id=1, source_target_pairs={{0,4},{1,5},{2,6},{3,7},{4,0},{5,1},{6,2},{7,3},{8,12},{9,13},{10,... | collective-permute-start | bytes 466952 | tf_op jit(solution)/shard_map/sum_a_up_4/ppermute | solution.py:973
  118.9 10.3 %collective-permute-start.14 = (f32[304,512]{1,0:T(8,128)S(1)}, f32[304,512]{1,0:T(8,128)S(1)}, u32[]{:S(2)}, u32[]{:S(2)}) collective-permute-start(f32[304,512]{1,0:T(8,128)S(1)} %get-tuple-element.230), channel_id=1, source_target_pairs={{0,16},{1,9},{2,18},{3,11},{4,20},{5,13},{6,22},{7,15},{8,24},{9,1... | collective-permute-start | bytes 1867784 | tf_op jit(solution)/shard_map/sum_c_down_2/ppermute | solution.py:973
  122.0 9.7 %collective-permute-start.13 = (f32[152,512]{1,0:T(8,128)S(1)}, f32[152,512]{1,0:T(8,128)S(1)}, u32[]{:S(2)}, u32[]{:S(2)}) collective-permute-start(f32[152,512]{1,0:T(8,128)S(1)} %get-tuple-element.228.refs_1_), channel_id=1, source_target_pairs={{0,2},{1,3},{2,0},{3,1},{4,6},{5,7},{6,4},{7,5},{8,10},{9,11},{10,... | collective-permute-start | bytes 933896 | tf_op jit(solution)/shard_map/sum_a_up_3/ppermute | solution.py:973
  129.9 7.7 %collective-permute-start.22 = (f32[152,512]{1,0:T(8,128)S(1)}, f32[152,512]{1,0:T(8,128)S(1)}, u32[]{:S(2)}, u32[]{:S(2)}) collective-permute-start(f32[152,512]{1,0:T(8,128)S(1)} %get-tuple-element.241), channel_id=1, source_target_pairs={{0,2},{1,3},{2,0},{3,1},{4,6},{5,7},{6,4},{7,5},{8,10},{9,11},{10,... | collective-permute-start | bytes 933896 | tf_op jit(solution)/shard_map/sum_c_down_3/ppermute | solution.py:973
  135.5 6.0 %collective-permute-start.15 = (f32[344,512]{1,0:T(8,128)S(1)}, f32[344,512]{1,0:T(8,128)S(1)}, u32[]{:S(2)}, u32[]{:S(2)}) collective-permute-start(f32[344,512]{1,0:T(8,128)S(1)} %get-tuple-element.235), channel_id=1, source_target_pairs={{0,1},{1,0},{2,3},{3,2},{4,5},{5,4},{6,7},{7,6},{8,9},{9,8},{10,11... | collective-permute-start | bytes 2113544 | tf_op jit(solution)/shard_map/sum_s_down_0/ppermute | solution.py:973
  135.6 15.3 %collective-permute-start.28 = (f32[304,512]{1,0:T(8,128)S(1)}, f32[304,512]{1,0:T(8,128)S(1)}, u32[]{:S(2)}, u32[]{:S(2)}) collective-permute-start(f32[304,512]{1,0:T(8,128)S(1)} %get-tuple-element.245.refs_1_), channel_id=1, source_target_pairs={{0,16},{1,9},{2,18},{3,11},{4,20},{5,13},{6,22},{7,15},{8,24},{9,1... | collective-permute-start | bytes 1867784 | tf_op jit(solution)/shard_map/sum_a_up_2/ppermute | solution.py:973
  138.7 9.0 %collective-permute-start.23 = (f32[152,256]{1,0:T(8,128)S(1)}, f32[152,256]{1,0:T(8,128)S(1)}, u32[]{:S(2)}, u32[]{:S(2)}) collective-permute-start(f32[152,256]{1,0:T(8,128)S(1)} %get-tuple-element.244), channel_id=1, source_target_pairs={{0,4},{1,5},{2,6},{3,7},{4,0},{5,1},{6,2},{7,3},{8,12},{9,13},{10,... | collective-permute-start | bytes 466952 | tf_op jit(solution)/shard_map/sum_c_down_4/ppermute | solution.py:973
  142.1 7.4 %collective-permute-start.16 = (f32[344,256]{1,0:T(8,128)S(1)}, f32[344,256]{1,0:T(8,128)S(1)}, u32[]{:S(2)}, u32[]{:S(2)}) collective-permute-start(f32[344,256]{1,0:T(8,128)S(1)} %get-tuple-element.237), channel_id=1, source_target_pairs={{0,8},{1,17},{2,10},{3,19},{4,12},{5,21},{6,14},{7,23},{8,0},{9,25... | collective-permute-start | bytes 1056776 | tf_op jit(solution)/shard_map/sum_s_down_1/ppermute | solution.py:973
  148.3 11.3 %collective-permute-start.24 = (f32[152,256]{1,0:T(8,128)S(1)}, f32[152,256]{1,0:T(8,128)S(1)}, u32[]{:S(2)}, u32[]{:S(2)}) collective-permute-start(f32[152,256]{1,0:T(8,128)S(1)} %land_c_down_5.1.refs_1_), channel_id=1, source_target_pairs={{0,4},{1,5},{2,6},{3,7},{4,0},{5,1},{6,2},{7,3},{8,12},{9,13},{10,... | collective-permute-start | bytes 466952 | tf_op jit(solution)/shard_map/sum_c_up_4/ppermute | solution.py:973
  150.1 7.1 %collective-permute-start.17 = (f32[344,128]{1,0:T(8,128)S(1)}, f32[344,128]{1,0:T(8,128)S(1)}, u32[]{:S(2)}, u32[]{:S(2)}) collective-permute-start(f32[344,128]{1,0:T(8,128)S(1)} %get-tuple-element.239), channel_id=1, source_target_pairs={{0,16},{1,9},{2,18},{3,11},{4,20},{5,13},{6,22},{7,15},{8,24},{9,1... | collective-permute-start | bytes 528392 | tf_op jit(solution)/shard_map/sum_s_down_2/ppermute | solution.py:973
  151.5 17.0 %collective-permute-start.29 = (f32[608,512]{1,0:T(8,128)S(1)}, f32[608,512]{1,0:T(8,128)S(1)}, u32[]{:S(2)}, u32[]{:S(2)}) collective-permute-start(f32[608,512]{1,0:T(8,128)S(1)} %land_a_up_2.1.refs_1_), channel_id=1, source_target_pairs={{0,8},{1,17},{2,10},{3,19},{4,12},{5,21},{6,14},{7,23},{8,0},{9,25... | collective-permute-start | bytes 3735560 | tf_op jit(solution)/shard_map/sum_a_up_1/ppermute | solution.py:973
  157.7 9.3 %collective-permute-start.18 = (f32[344,128]{1,0:T(8,128)S(1)}, f32[344,128]{1,0:T(8,128)S(1)}, u32[]{:S(2)}, u32[]{:S(2)}) collective-permute-start(f32[344,128]{1,0:T(8,128)S(1)} %land_s_down_3.1.refs_1_), channel_id=1, source_target_pairs={{0,2},{1,3},{2,0},{3,1},{4,6},{5,7},{6,4},{7,5},{8,10},{9,11},{10,... | collective-permute-start | bytes 528392 | tf_op jit(solution)/shard_map/sum_s_down_3/ppermute | solution.py:973
  160.1 10.7 %collective-permute-start.25 = (f32[152,512]{1,0:T(8,128)S(1)}, f32[152,512]{1,0:T(8,128)S(1)}, u32[]{:S(2)}, u32[]{:S(2)}) collective-permute-start(f32[152,512]{1,0:T(8,128)S(1)} %land_c_up_4.1.refs_1_), channel_id=1, source_target_pairs={{0,2},{1,3},{2,0},{3,1},{4,6},{5,7},{6,4},{7,5},{8,10},{9,11},{10,... | collective-permute-start | bytes 933896 | tf_op jit(solution)/shard_map/sum_c_up_3/ppermute | solution.py:973
  167.6 7.7 %collective-permute-start.19 = (f32[344,128]{1,0:T(8,128)S(1)}, f32[344,128]{1,0:T(8,128)S(1)}, u32[]{:S(2)}, u32[]{:S(2)}) collective-permute-start(f32[344,128]{1,0:T(8,128)S(1)} %land_s_down_4.1.refs_1_), channel_id=1, source_target_pairs={{0,4},{1,5},{2,6},{3,7},{4,0},{5,1},{6,2},{7,3},{8,12},{9,13},{10,... | collective-permute-start | bytes 528392 | tf_op jit(solution)/shard_map/sum_s_down_4/ppermute | solution.py:973
  169.2 17.3 %collective-permute-start.30 = (f32[1216,512]{1,0:T(8,128)S(1)}, f32[1216,512]{1,0:T(8,128)S(1)}, u32[]{:S(2)}, u32[]{:S(2)}) collective-permute-start(f32[1216,512]{1,0:T(8,128)S(1)} %land_a_up_1.1.refs_1_), channel_id=1, source_target_pairs={{0,1},{1,0},{2,3},{3,2},{4,5},{5,4},{6,7},{7,6},{8,9},{9,8},{10,11... | collective-permute-start | bytes 7471112 | tf_op jit(solution)/shard_map/sum_a_up_0/ppermute | solution.py:973
  171.4 10.3 %collective-permute-start.26 = (f32[304,512]{1,0:T(8,128)S(1)}, f32[304,512]{1,0:T(8,128)S(1)}, u32[]{:S(2)}, u32[]{:S(2)}) collective-permute-start(f32[304,512]{1,0:T(8,128)S(1)} %land_c_up_3.1.refs_1_), channel_id=1, source_target_pairs={{0,16},{1,9},{2,18},{3,11},{4,20},{5,13},{6,22},{7,15},{8,24},{9,1... | collective-permute-start | bytes 1867784 | tf_op jit(solution)/shard_map/sum_c_up_2/ppermute | solution.py:973
  175.8 8.2 %collective-permute-start.20 = (f32[344,128]{1,0:T(8,128)S(1)}, f32[344,128]{1,0:T(8,128)S(1)}, u32[]{:S(2)}, u32[]{:S(2)}) collective-permute-start(f32[344,128]{1,0:T(8,128)S(1)} %land_s_down_5.1.refs_1_), channel_id=1, source_target_pairs={{0,16},{1,9},{2,18},{3,11},{4,20},{5,13},{6,22},{7,15},{8,24},{9,1... | collective-permute-start | bytes 528392 | tf_op jit(solution)/shard_map/sum_s_up_2/ppermute | solution.py:973
  182.4 17.0 %collective-permute-start.27 = (f32[608,512]{1,0:T(8,128)S(1)}, f32[608,512]{1,0:T(8,128)S(1)}, u32[]{:S(2)}, u32[]{:S(2)}) collective-permute-start(f32[608,512]{1,0:T(8,128)S(1)} %land_c_up_2.1.refs_1_), channel_id=1, source_target_pairs={{0,8},{1,17},{2,10},{3,19},{4,12},{5,21},{6,14},{7,23},{8,0},{9,25... | collective-permute-start | bytes 3735560 | tf_op jit(solution)/shard_map/sum_c_up_1/ppermute | solution.py:973
  184.6 18.5 %collective-permute-start.21 = (f32[344,256]{1,0:T(8,128)S(1)}, f32[344,256]{1,0:T(8,128)S(1)}, u32[]{:S(2)}, u32[]{:S(2)}) collective-permute-start(f32[344,256]{1,0:T(8,128)S(1)} %land_s_up_2.1.refs_1_), channel_id=1, source_target_pairs={{0,8},{1,17},{2,10},{3,19},{4,12},{5,21},{6,14},{7,23},{8,0},{9,25... | collective-permute-start | bytes 1056776 | tf_op jit(solution)/shard_map/sum_s_up_1/ppermute | solution.py:973
  200.1 7.5 %collective-permute-start.32 = (f32[1216,512]{1,0:T(8,128)S(1)}, f32[1216,512]{1,0:T(8,128)S(1)}, u32[]{:S(2)}, u32[]{:S(2)}) collective-permute-start(f32[1216,512]{1,0:T(8,128)S(1)} %land_c_up_1.1.refs_1_), channel_id=1, source_target_pairs={{0,1},{1,0},{2,3},{3,2},{4,5},{5,4},{6,7},{7,6},{8,9},{9,8},{10,11... | collective-permute-start | bytes 7471112 | tf_op jit(solution)/shard_map/sum_c_up_0/ppermute | solution.py:973
  203.7 2.2 %collective-permute-start.31 = (f32[344,512]{1,0:T(8,128)S(1)}, f32[344,512]{1,0:T(8,128)S(1)}, u32[]{:S(2)}, u32[]{:S(2)}) collective-permute-start(f32[344,512]{1,0:T(8,128)S(1)} %land_s_up_1.1.refs_1_), channel_id=1, source_target_pairs={{0,1},{1,0},{2,3},{3,2},{4,5},{5,4},{6,7},{7,6},{8,9},{9,8},{10,11... | collective-permute-start | bytes 2113544 | tf_op jit(solution)/shard_map/sum_s_up_0/ppermute | solution.py:973
  (7 other events, 6.5 us)
